TPU v7x, 512 devices: a whole 4x4x16 slice. The times are simulated.
512 devices in a mesh: fsdp: 32 (over z_lo, x), dp: 16 (over z_hi, y, core).
Axes of the slice: x: 4, y: 4, z: 16 (z_hi: 2, z_lo: 8; z = z_hi * 8 + z_lo), core: 2. Of those that a mesh axis runs over, the one named last changes fastest.
Arguments:
- tokens: bfloat16 [12288, 4096], P(('dp', 'fsdp')), parts along dimension 0, may hold values from -6 to 6
- frozen_slot_rows: bfloat16 [73728, 14336], P(('dp', 'fsdp')), parts along dimension 0
- adapter_down_factor: bfloat16 [73728, 64], P(('dp', 'fsdp')), parts along dimension 0, may hold values from -18 to 18
- adapter_up_factor: bfloat16 [1024, 14336], P('dp', 'fsdp'), parts along dimension 0, may hold values from -0.046875 to 0.046875
- magnitude: bfloat16 [229376], P(('dp', 'fsdp')), parts along dimension 0, may hold values from 0.5 to 2
- counts: int32 [512], P('dp'), parts along dimension 0, may hold values from 1 to 144, 4096 in all
Outputs:
- projected: bfloat16 [12288, 14336], P('dp', 'fsdp'), parts along dimension 0
There are 16 independent parts, one for each index of `dp`. A program takes and returns all parts, laid end to end along the dimension named above; each array names one. Nothing has to cross between parts.
Inputs may be any that keep to these rules, and one draw needn't show every extreme that they name: counts are at least 1, sum to 4096, and the largest equals 144; slots at or beyond a device's count hold arbitrary values.
All inputs are finite; a program needn't handle non-finite values.
Results may differ from a plain program's by a relative error of at most 0.0049.
Values may be sent and summed in bfloat16 or wider, within the bound.
No kernel may reach another device: no remote copies, remote signals or barrier semaphores. Data moves between devices by JAX's collectives and lax.ppermute only.
A program may use at most 64 MiB of HBM per device.

v0:
```python
import jax
import jax.numpy as jnp
from jax import lax
from jax.sharding import PartitionSpec as P


def locate(counts, slots_per, total_rows):
    offsets = jnp.cumsum(counts) - counts
    row_ids = jnp.arange(total_rows, dtype=jnp.int32)
    owner = jnp.sum((offsets[None, :] <= row_ids[:, None]).astype(jnp.int32), axis=1) - 1
    picked = jnp.arange(counts.shape[0], dtype=jnp.int32)[None, :] == owner[:, None]
    first = jnp.sum(jnp.where(picked, offsets[None, :], 0), axis=1)
    return owner * slots_per + row_ids - first


def body(tokens, frozen_slot_rows, adapter_down_factor, adapter_up_factor, magnitude, counts):
    slots_per = frozen_slot_rows.shape[0]
    groups = counts.shape[0]
    slot_positions = locate(counts, slots_per, tokens.shape[1])
    gathered_up_factor, scale_all = (
        lax.all_gather(adapter_up_factor, "fsdp", axis=1, tiled=True),
        lax.all_gather(magnitude, "fsdp", axis=0, tiled=True),
    )
    own_index = lax.axis_index("fsdp")
    own_count = jnp.sum(jnp.where(jnp.arange(groups, dtype=jnp.int32) == own_index, counts, 0))
    valid = (jnp.arange(slots_per, dtype=jnp.int32) < own_count)[:, None]
    merged_weight = frozen_slot_rows.astype(jnp.float32) + jnp.dot(
        adapter_down_factor, gathered_up_factor, preferred_element_type=jnp.float32
    )
    merged_weight = jnp.where(valid, merged_weight, 0.0)
    squares = lax.psum(jnp.sum(merged_weight * merged_weight, axis=0), "fsdp")
    length = jnp.sqrt(squares + 1e-06)
    scaled = (scale_all.astype(jnp.float32) * merged_weight / length).astype(jnp.bfloat16)
    received = lax.all_to_all(scaled, "fsdp", split_axis=1, concat_axis=0, tiled=True)
    weights = jnp.take(received, slot_positions, axis=0)
    result = jnp.dot(
        lax.all_gather(tokens, "fsdp", axis=0, tiled=True),
        weights,
        preferred_element_type=jnp.float32,
    )
    return result.astype(jnp.bfloat16)


def solution(mesh):
    in_specs = (
        P(("dp", "fsdp"), None),
        P(("dp", "fsdp"), None),
        P(("dp", "fsdp"), None),
        P("dp", "fsdp"),
        P(("dp", "fsdp")),
        P("dp"),
    )
    out_specs = P("dp", "fsdp")
    return jax.shard_map(body, mesh=mesh, in_specs=in_specs, out_specs=out_specs, check_vma=False)
```

profile of v0, /device:TPU:110, one launch (start us, length us, event | category | flops | bytes accessed | tf_op | source)
XLA Modules:
  0.0 783.5 jit_solution(8029859373965557383)
XLA Ops:
  6.5 0.0 copy-start
  6.5 0.0 all-gather.6.cloned.1.call-start
  6.5 0.7 all-gather.6.cloned.1.call-update
  7.3 0.7 copy.15
  8.0 0.1 reduce-window.9
  8.1 0.1 reduce
  8.2 1.3 dynamic-slice
  10.1 0.9 dynamic-update-slice
  11.0 165.9 %all-reduce = bf16[14336]{0:T(1024)(128)(2,1)S(1)} all-reduce(bf16[14336]{0:T(1024)(128)(2,1)S(1)} %dynamic-update-slice), channel_id=1, replica_groups=mesh['fsdp'=32,'dp'=16] {'fsdp'}, use_global_device_ids=true, to_apply=%add | all-reduce | flops 14336 | bytes 57344
  176.9 1.3 fusion.13
  178.2 0.6 iota_compare_fusion.2
  178.9 10.9 %all-gather.6.cloned.1.call-done = bf16[32,448,64]{1,2,0:T(8,128)(2,1)} async-done(((bf16[1,448,64]{1,2,0:T(8,128)(2,1)}), bf16[32,448,64]{1,2,0:T(8,128)(2,1)}) %all-gather.6.cloned.1.call-update) | async-done | bytes 1835024 | tf_op jit(solution)/shard_map/all_gather | solution.py:21
  189.8 2.8 copy.16
  192.5 3.3 reshape.96
  195.9 0.0 copy-done
  195.9 8.1 %multiply_reduce_fusion = (f32[14336]{0:T(1024)S(1)}, f32[144,14336]{1,0:T(8,128)}) fusion(bf16[144,64]{0,1:T(8,128)(2,1)S(1)} %copy-done, bf16[14336,64]{0,1:T(8,128)(2,1)} %reshape.96, bf16[144,14336]{1,0:T(8,128)(2,1)} %param.7, pred[144]{0:T(512)(128)(4,1)S(1)} %iota_compare_fusion.2), kind=kOutput, calls=%fused_computation.4 | convolution fusion | flops 274548736 | bytes 14297232 | tf_op jit(solution)/shard_map/dot_general | solution.py:27
  204.0 217.5 %psum.7 = f32[14336]{0:T(1024)S(1)} all-reduce(f32[14336]{0:T(1024)S(1)} %get-tuple-element.9), channel_id=1, replica_groups=mesh['fsdp'=32,'dp'=16] {'fsdp'}, use_global_device_ids=true, to_apply=%region_5.6 | all-reduce | flops 14336 | bytes 114688 | tf_op jit(solution)/shard_map/psum | solution.py:31
  421.4 6.3 divide_convert_fusion
  427.7 8.6 %all_to_all.14 = bf16[144,32,448]{2,1,0:T(8,128)(2,1)} reshape(bf16[144,14336]{1,0:T(8,128)(2,1)} %divide_convert_fusion) | data formatting | bytes 8257536 | tf_op jit(solution)/shard_map/all_to_all | solution.py:34
  436.3 7.2 copy.17
  443.5 72.3 %all-to-all-start = ((bf16[144,32,448]{2,0,1:T(8,128)(2,1)}), bf16[144,32,448]{2,0,1:T(8,128)(2,1)}, u32[]{:S(2)}, u32[]{:S(2)}) async-start(bf16[144,32,448]{2,0,1:T(8,128)(2,1)} %copy.17), calls=%async_computation | async-start | bytes 9437184 | tf_op jit(solution)/shard_map/all_to_all | solution.py:34
  515.7 0.2 all-gather.4.cloned.1.call-start
  516.0 0.5 all-gather.4.cloned.1.call-update
  516.5 0.1 convert_reduce_fusion
  516.7 0.2 select_reduce_fusion
  516.9 195.7 %all-to-all-done = bf16[144,32,448]{2,0,1:T(8,128)(2,1)} async-done(((bf16[144,32,448]{2,0,1:T(8,128)(2,1)}), bf16[144,32,448]{2,0,1:T(8,128)(2,1)}, u32[]{:S(2)}, u32[]{:S(2)}) %all-to-all-start) | async-done | bytes 4128800 | tf_op jit(solution)/shard_map/all_to_all | solution.py:34
  712.6 20.3 %gather_fusion = bf16[4096,448]{1,0:T(8,128)(2,1)} fusion(bf16[4608,448]{1,0:T(8,128)(2,1)} %bitcast.5, s32[4096]{0:T(1024)S(1)} %broadcast_clamp_fusion), kind=kCustom, calls=%fused_computation | custom fusion | bytes 7356416 | tf_op jit(solution)/shard_map/jit(_take)/gather | solution.py:35
  733.0 34.7 %all-gather.4.cloned.1.call-done = bf16[768,4096]{1,0:T(8,128)(2,1)} async-done(((bf16[24,4096]{1,0:T(8,128)(2,1)}), bf16[768,4096]{1,0:T(8,128)(2,1)}) %all-gather.4.cloned.1.call-update) | async-done | bytes 6291472 | tf_op jit(solution)/shard_map/all_gather | solution.py:37
  767.6 9.0 %fusion.8 = bf16[768,448]{0,1:T(8,128)(2,1)} fusion(bf16[768,4096]{1,0:T(8,128)(2,1)} %all-gather.4.cloned.1.call-done, bf16[4096,448]{1,0:T(8,128)(2,1)} %gather_fusion, pred[4096]{0:T(1024)(128)(4,1)S(1)} %compare_and_fusion), kind=kOutput, calls=%fused_computation.10 | convolution fusion | flops 2820751360 | bytes 10653696 | tf_op jit(solution)/shard_map/dot_general | solution.py:36
  (7 shorter events, 0.1 us)
Async XLA Ops:
  6.5 189.3 %copy-start = (bf16[144,64]{0,1:T(8,128)(2,1)S(1)}, bf16[144,64]{0,1:T(8,128)(2,1)}, u32[]{:S(2)}) copy-start(bf16[144,64]{0,1:T(8,128)(2,1)} %param.8) | copy-start | bytes 55300
  6.5 183.2 %all-gather.6.cloned.1.call-start = ((), (), s32[]{:S(2)}) async-start(), calls=%async_computation.2 | async-start | bytes 2162688 | tf_op jit(solution)/shard_map/all_gather | solution.py:21
  443.5 269.2 %all-to-all-start = ((bf16[144,32,448]{2,0,1:T(8,128)(2,1)}), bf16[144,32,448]{2,0,1:T(8,128)(2,1)}, u32[]{:S(2)}, u32[]{:S(2)}) async-start(bf16[144,32,448]{2,0,1:T(8,128)(2,1)} %copy.17), calls=%async_computation | async-start | bytes 9437184 | tf_op jit(solution)/shard_map/all_to_all | solution.py:34
  515.7 251.9 %all-gather.4.cloned.1.call-start = ((), (), s32[]{:S(2)}) async-start(), calls=%async_computation.1 | async-start | bytes 6488064 | tf_op jit(solution)/shard_map/all_gather | solution.py:37
Sparse Core Ops, SparseCore 0:
  9.4 180.2 all-gather.5
  518.7 248.9 all-gather.3
where the time goes:
time: 784 us; the launch traced here: 783 us
  blocking collectives  383 us (49%)
  waiting for transfers between devices  243 us (31%)
  starting transfers between devices  72.5 us (9%)
  local copies, waits for them, and re-layouts  45.1 us (6%)
  matrix products  17.1 us (2%)
  between operations  14.1 us (2%)
  other arithmetic  8.76 us (1%)
    psum x1, blocking collectives, body(): squares = lax.psum(jnp.sum(merged_weight * merged_weight, axis=0), 'fsdp')  217 us
    all_to_all x1, waiting for transfers between devices, body(): lax.all_to_all(scaled, 'fsdp', split_axis=1, concat_axis=0, tiled=True)  196 us
    unnamed x1, blocking collectives  166 us
    all_to_all x1, starting transfers between devices, body(): lax.all_to_all(scaled, 'fsdp', split_axis=1, concat_axis=0, tiled=True)  72.3 us
    all_gather x1, waiting for transfers between devices, body(): lax.all_gather(tokens, 'fsdp', axis=0, tiled=True)  34.7 us
    gather x1, local copies, waits for them, and re-layouts, body(): weights = jnp.take(received, slot_positions, axis=0)  20.3 us
    all_to_all x2, local copies, waits for them, and re-layouts, body(): lax.all_to_all(scaled, 'fsdp', split_axis=1, concat_axis=0, tiled=True)  15.8 us
  transfers between devices with their start and end apart: 3, of which 3 were waited for; matrix products, arithmetic and copies ran while one was open for 3% of the time, Pallas kernels for 0%

commit v1 on v0

v1 whole, which is shorter than its diff:
```python
import functools

import jax
import jax.numpy as jnp
from jax import lax
from jax.experimental import pallas as pl
from jax.experimental.pallas import tpu as pltpu
from jax.sharding import PartitionSpec as P

AXIS = "fsdp"
GROUP = 8
PAIRS = 4
SLOTS = 144
RANK = 64
UNITS = 448
KEYS = GROUP * SLOTS
TOKENS = 768
OWN_TOKENS = 24
FEATURES = 4096
WINDOW = 384
CHUNKS = ((0, 256), (256, 192))
VMEM_LIMIT = 48 * 1024 * 1024

NEAR = [[GROUP * p + i for i in range(GROUP)] for p in range(PAIRS)]
FAR = [[GROUP * p + i for p in range(PAIRS)] for i in range(GROUP)]
ALONG_X = [[4 * z + x for x in range(4)] for z in range(8)]


def whole(memory_space=pltpu.VMEM):
    return pl.BlockSpec(memory_space=memory_space)


def params():
    return pltpu.CompilerParams(vmem_limit_bytes=VMEM_LIMIT)


def window_kernel(place_ref, counts_ref, tokens_ref, out_ref, padded, lined):
    padded[:, FEATURES:] = jnp.zeros((OWN_TOKENS, WINDOW), jnp.float32)
    padded[:, :FEATURES] = tokens_ref[...].astype(jnp.float32)
    starts = [jnp.int32(0)]
    for f in range(GROUP * PAIRS - 1):
        starts.append(starts[-1] + counts_ref[f])
    pair = place_ref[0] // GROUP
    lane = lax.broadcasted_iota(jnp.int32, (OWN_TOKENS, WINDOW), 1)
    for target in range(PAIRS):
        for i in range(GROUP):
            start = starts[GROUP * target + i]
            base = pl.multiple_of((start // 128) * 128, 128)
            place = SLOTS * i
            low = (place // 128) * 128
            rest = place - low
            shift = lax.rem(rest - (start - base) + WINDOW, WINDOW)
            moved = pltpu.roll(padded[:, pl.ds(base, WINDOW)], shift, 1)
            keep = (lane >= rest) & (lane < rest + SLOTS)
            lined[:, low : low + WINDOW] = jnp.where(keep, moved, lined[:, low : low + WINDOW])
        out_ref[lax.rem(target - pair + PAIRS, PAIRS)] = lined[:, :KEYS].astype(jnp.bfloat16)


def own_windows(place, counts, tokens):
    return pl.pallas_call(
        window_kernel,
        out_shape=jax.ShapeDtypeStruct((PAIRS, OWN_TOKENS, KEYS), jnp.bfloat16),
        in_specs=[whole(pltpu.SMEM), whole(pltpu.SMEM), whole()],
        out_specs=whole(),
        scratch_shapes=[
            pltpu.VMEM((OWN_TOKENS, FEATURES + WINDOW), jnp.float32),
            pltpu.VMEM((OWN_TOKENS, KEYS + 128), jnp.float32),
        ],
        compiler_params=params(),
    )(place, counts, tokens)


def collect_kernel(place_ref, own_ref, one_ref, two_ref, three_ref, down_ref, out_ref, rows):
    pair = place_ref[0] // GROUP
    blocks = (own_ref[0], one_ref[...], two_ref[...], three_ref[...])
    for step, block in enumerate(blocks):
        origin = lax.rem(pair - step + PAIRS, PAIRS)
        rows[pl.ds(pl.multiple_of(origin * OWN_TOKENS, 8), OWN_TOKENS), :] = block.astype(jnp.float32)
    down = down_ref[...].astype(jnp.float32)
    rows[PAIRS * OWN_TOKENS :, :] = jnp.concatenate(
        [down[8 * g : 8 * g + 8, :] for g in range(SLOTS // 8)], axis=1
    )
    out_ref[...] = rows[...].astype(jnp.bfloat16)


def collect(place, own, one, two, three, down):
    height = PAIRS * OWN_TOKENS + 8
    return pl.pallas_call(
        collect_kernel,
        out_shape=jax.ShapeDtypeStruct((height, KEYS), jnp.bfloat16),
        in_specs=[whole(pltpu.SMEM)] + [whole()] * 5,
        out_specs=whole(),
        scratch_shapes=[pltpu.VMEM((height, KEYS), jnp.float32)],
        compiler_params=params(),
    )(place, own, one, two, three, down)


def pack_kernel(rows_ref, *out_refs):
    step = pl.program_id(0)
    for q in range(PAIRS):

        @pl.when(step == q)
        def _():
            for out_ref, (first, width) in zip(out_refs, CHUNKS):
                for i in range(GROUP):
                    begin = UNITS * i + first
                    out_ref[i, :, q * width : (q + 1) * width] = rows_ref[:, begin : begin + width]


def pack(rows):
    return pl.pallas_call(
        pack_kernel,
        grid=(PAIRS,),
        out_shape=[
            jax.ShapeDtypeStruct((GROUP, SLOTS, PAIRS * width), jnp.bfloat16) for _, width in CHUNKS
        ],
        in_specs=[pl.BlockSpec((SLOTS, GROUP * UNITS), lambda q: (0, q))],
        out_specs=[
            pl.BlockSpec((GROUP, SLOTS, PAIRS * width), lambda q: (0, 0, 0)) for _, width in CHUNKS
        ],
        compiler_params=params(),
    )(rows)


def partial_kernel(first, width, place_ref, counts_ref, rows_ref, blocks_ref, up0_ref, up1_ref, up2_ref, up3_ref, out_ref, squares_ref, tokens, merged, ups):
    place = place_ref[0]
    pair, side = place // GROUP, (place // 4) % 2
    row = lax.broadcasted_iota(jnp.int32, (SLOTS, width), 0)
    downs, valid = [], []
    for i in range(GROUP):
        origin = lax.rem(side + i // 4, 2)
        tokens[96 * i : 96 * i + 96, :] = blocks_ref[i % 4, origin, 0:96, :]
        folded = blocks_ref[i % 4, origin, 96:104, :].astype(jnp.float32)
        downs.append(
            jnp.concatenate([folded[:, RANK * g : RANK * g + RANK] for g in range(SLOTS // 8)], axis=0).astype(jnp.bfloat16)
        )
        valid.append(row < counts_ref[GROUP * pair + i])
    for step, up_ref in enumerate((up0_ref, up1_ref, up2_ref, up3_ref)):
        ups[lax.rem(pair - step + PAIRS, PAIRS)] = up_ref[...]
    all_tokens = tokens[...]
    for q in range(PAIRS):
        up = ups[q, :, first : first + width]
        total = jnp.zeros((1, width), jnp.float32)
        for i in range(GROUP):
            low = jnp.dot(downs[i], up, preferred_element_type=jnp.float32)
            base = rows_ref[i, :, q * width : (q + 1) * width].astype(jnp.float32)
            value = jnp.where(valid[i], base + low, 0.0)
            total = total + jnp.sum(value * value, axis=0, keepdims=True)
            merged[SLOTS * i : SLOTS * i + SLOTS, :] = value.astype(jnp.bfloat16)
        squares_ref[q] = total
        out_ref[q] = lax.dot_general(
            merged[...], all_tokens, (((0,), (1,)), ((), ())), preferred_element_type=jnp.float32
        ).astype(jnp.bfloat16)


def partial_products(chunk, place, counts, rows, blocks, ups):
    first, width = chunk
    return pl.pallas_call(
        functools.partial(partial_kernel, first, width),
        out_shape=[
            jax.ShapeDtypeStruct((PAIRS, width, TOKENS), jnp.bfloat16),
            jax.ShapeDtypeStruct((PAIRS, 1, width), jnp.float32),
        ],
        in_specs=[whole(pltpu.SMEM), whole(pltpu.SMEM)] + [whole()] * 6,
        out_specs=[whole(), whole()],
        scratch_shapes=[
            pltpu.VMEM((TOKENS, KEYS), jnp.bfloat16),
            pltpu.VMEM((KEYS, width), jnp.bfloat16),
            pltpu.VMEM((PAIRS, RANK, UNITS), jnp.bfloat16),
        ],
        compiler_params=params(),
    )(place, counts, rows, blocks, *ups)


def finish_kernel(squares_ref, scale_ref, *refs):
    sum_refs, out_ref = refs[:-1], refs[-1]
    total = jnp.sum(squares_ref[...], axis=0)
    factor = scale_ref[...].astype(jnp.float32) / jnp.sqrt(total + 1e-06)
    sums = jnp.concatenate([s[...].astype(jnp.float32) for s in sum_refs], axis=0).T
    result = jnp.where(factor == 0.0, 0.0, sums * factor)
    out_ref[...] = jnp.concatenate(
        [
            result[OWN_TOKENS * (PAIRS * i + q) : OWN_TOKENS * (PAIRS * i + q + 1), :]
            for q in range(PAIRS)
            for i in range(GROUP)
        ],
        axis=0,
    ).astype(jnp.bfloat16)


def finish(squares, scale, sums):
    return pl.pallas_call(
        finish_kernel,
        out_shape=jax.ShapeDtypeStruct((TOKENS, UNITS), jnp.bfloat16),
        in_specs=[whole()] * (2 + len(sums)),
        out_specs=whole(),
        compiler_params=params(),
    )(squares, scale, *sums)


def to_pair(array, step):
    return lax.ppermute(
        array,
        AXIS,
        [(GROUP * p + i, GROUP * ((p + step) % PAIRS) + i) for p in range(PAIRS) for i in range(GROUP)],
    )


def body(tokens, frozen_slot_rows, adapter_down_factor, adapter_up_factor, magnitude, counts):
    place = lax.axis_index(AXIS).astype(jnp.int32).reshape(1)
    own = own_windows(place, counts, tokens)
    moved = [to_pair(own[step], step) for step in range(1, PAIRS)]
    ups = [adapter_up_factor] + [to_pair(adapter_up_factor, step) for step in range(1, PAIRS)]
    column = collect(place, own, *moved, adapter_down_factor)
    other = lax.ppermute(column, AXIS, [(f, f ^ 4) for f in range(GROUP * PAIRS)])
    pair_blocks = jnp.stack([column, other])
    packed = list(pack(frozen_slot_rows))
    packed[0], pair_blocks = lax.optimization_barrier((packed[0], pair_blocks))
    blocks = lax.all_gather(pair_blocks, AXIS, axis_index_groups=ALONG_X, axis=0)
    sums, squares = [], []
    product = None
    for chunk, send in zip(CHUNKS, packed):
        if product is not None:
            send, product = lax.optimization_barrier((send, product))
            sums.append(lax.psum_scatter(product, AXIS, axis_index_groups=FAR, scatter_dimension=0, tiled=False))
        rows = lax.all_to_all(send, AXIS, 0, 0, axis_index_groups=NEAR, tiled=True)
        product, square = partial_products(chunk, place, counts, rows, blocks, ups)
        squares.append(square)
    sums.append(lax.psum_scatter(product, AXIS, axis_index_groups=FAR, scatter_dimension=0, tiled=False))
    squares = lax.all_to_all(jnp.concatenate(squares, axis=2), AXIS, 0, 0, axis_index_groups=FAR, tiled=True)
    return finish(squares, magnitude.reshape(1, UNITS), sums)


def solution(mesh):
    in_specs = (
        P(("dp", "fsdp"), None),
        P(("dp", "fsdp"), None),
        P(("dp", "fsdp"), None),
        P("dp", "fsdp"),
        P(("dp", "fsdp")),
        P("dp"),
    )
    out_specs = P("dp", "fsdp")
    return jax.shard_map(body, mesh=mesh, in_specs=in_specs, out_specs=out_specs, check_vma=False)
```

time: 784 us -> 254 us (0.32)
  the two profiles are of different devices: /device:TPU:110 before, /device:TPU:1 now
where the time goes in v1:
time: 254 us; the launch traced here: 253 us
  waiting for transfers between devices  160 us (63%)
  starting transfers between devices  52 us (20%)
  Pallas kernels  16.7 us (7%)
  between operations  13.3 us (5%)
  local copies, waits for them, and re-layouts  9.75 us (4%)
    reduce_scatter x2, waiting for transfers between devices, body(): lax.psum_scatter(product, AXIS, axis_index_groups=FAR, scatter_dimension=...  104 us
    ppermute x6, starting transfers between devices, to_pair(): lax.ppermute(array, AXIS, [(GROUP * p + i, GROUP * ((p + step) % PAIRS) +...  31.7 us
    all_to_all x2, waiting for transfers between devices, body(): rows = lax.all_to_all(send, AXIS, 0, 0, axis_index_groups=NEAR, tiled=True)  21.9 us
    all_gather x1, waiting for transfers between devices, body(): lax.all_gather(pair_blocks, AXIS, axis_index_groups=ALONG_X, axis=0)  17 us
    ppermute x6, waiting for transfers between devices, to_pair(): lax.ppermute(array, AXIS, [(GROUP * p + i, GROUP * ((p + step) % PAIRS) +...  15.8 us
    pallas_call x2, Pallas kernels, partial_products(): pl.pallas_call(functools.partial(partial_kernel, first, width), out_shape...  11.9 us
    all_to_all x2, starting transfers between devices, body(): rows = lax.all_to_all(send, AXIS, 0, 0, axis_index_groups=NEAR, tiled=True)  9.21 us
    unnamed x23, local copies, waits for them, and re-layouts  8.62 us
  transfers between devices with their start and end apart: 13, of which 8 were waited for; matrix products, arithmetic and copies ran while one was open for 1% of the time, Pallas kernels for 4%

profile of v1, /device:TPU:1, one launch (start us, length us, event | category | flops | bytes accessed | tf_op | source)
XLA Modules:
  0.0 252.9 jit_solution(6607194754737408842)
XLA Ops:
  6.5 0.9 copy-done.7
  8.1 1.0 shard_map.65.own_ref
  9.1 5.7 %collective-permute-start = (bf16[24,1152]{1,0:T(8,128)(2,1)S(1)}, bf16[24,1152]{1,0:T(8,128)(2,1)S(1)}, u32[]{:S(2)}, u32[]{:S(2)}) collective-permute-start(bf16[24,1152]{1,0:T(8,128)(2,1)S(1)} %get-tuple-element.27), channel_id=1, source_target_pairs={{0,128},{16,144},{32,160},{48,176},{64,192},{80,208},{96,224},{112... | collective-permute-start | bytes 165896 | tf_op jit(solution)/shard_map/ppermute | solution.py:202
  14.9 8.8 %collective-permute-start.1 = (bf16[24,1152]{1,0:T(8,128)(2,1)S(1)}, bf16[24,1152]{1,0:T(8,128)(2,1)S(1)}, u32[]{:S(2)}, u32[]{:S(2)}) collective-permute-start(bf16[24,1152]{1,0:T(8,128)(2,1)S(1)} %get-tuple-element.26), channel_id=1, source_target_pairs={{0,256},{16,272},{32,288},{48,304},{64,320},{80,336},{96,352},{112... | collective-permute-start | bytes 165896 | tf_op jit(solution)/shard_map/ppermute | solution.py:202
  23.7 4.3 %collective-permute-start.2 = (bf16[24,1152]{1,0:T(8,128)(2,1)S(1)}, bf16[24,1152]{1,0:T(8,128)(2,1)S(1)}, u32[]{:S(2)}, u32[]{:S(2)}) collective-permute-start(bf16[24,1152]{1,0:T(8,128)(2,1)S(1)} %get-tuple-element.25), channel_id=1, source_target_pairs={{0,384},{16,400},{32,416},{48,432},{64,448},{80,464},{96,480},{112... | collective-permute-start | bytes 165896 | tf_op jit(solution)/shard_map/ppermute | solution.py:202
  28.0 0.9 copy.9.down_ref
  28.9 1.3 collective-permute-done.2.three_ref
  30.3 3.8 %collective-permute-start.3 = (bf16[104,1152]{1,0:T(8,128)(2,1)S(1)}, bf16[104,1152]{1,0:T(8,128)(2,1)S(1)}, u32[]{:S(2)}, u32[]{:S(2)}) collective-permute-start(bf16[104,1152]{1,0:T(8,128)(2,1)S(1)} %shard_map.66), channel_id=1, source_target_pairs={{0,64},{16,80},{32,96},{48,112},{64,0},{80,16},{96,32},{112,48},{1... | collective-permute-start | bytes 718856 | tf_op jit(solution)/shard_map/ppermute | solution.py:215
  34.1 3.5 %shard_map.64 = (bf16[8,144,1024]{2,1,0:T(8,128)(2,1)S(1)}, bf16[8,144,768]{2,1,0:T(8,128)(2,1)S(1)}) custom-call(bf16[144,14336]{1,0:T(8,128)(2,1)} %rows_ref.1), custom_call_target="tpu_custom_call" | custom-call | tf_op jit(solution)/shard_map/pallas_call | solution.py:111
  37.6 1.4 copy-done.2
  39.0 1.3 copy-done.3
  40.3 0.8 pad_maximum_fusion
  41.1 4.8 %all-to-all-start = ((bf16[8,144,1024]{2,1,0:T(8,128)(2,1)}), bf16[8,144,1024]{2,1,0:T(8,128)(2,1)S(1)}, u32[]{:S(2)}, u32[]{:S(2)}) async-start(bf16[8,144,1024]{2,1,0:T(8,128)(2,1)} %copy-done.2), calls=%async_computation | async-start | bytes 4718592 | tf_op jit(solution)/shard_map/all_to_all | solution.py:226
  46.6 2.2 collective-permute-start.4
  48.8 7.7 %collective-permute-start.5 = (bf16[64,448]{1,0:T(8,128)(2,1)S(1)}, bf16[64,448]{1,0:T(8,128)(2,1)S(1)}, u32[]{:S(2)}, u32[]{:S(2)}) collective-permute-start(bf16[64,448]{1,0:T(8,128)(2,1)S(1)} %copy-done.6), channel_id=1, source_target_pairs={{0,256},{16,272},{32,288},{48,304},{64,320},{80,336},{96,352},{112... | collective-permute-start | bytes 172040 | tf_op jit(solution)/shard_map/ppermute | solution.py:202
  56.5 3.0 %collective-permute-start.6 = (bf16[64,448]{1,0:T(8,128)(2,1)S(1)}, bf16[64,448]{1,0:T(8,128)(2,1)S(1)}, u32[]{:S(2)}, u32[]{:S(2)}) collective-permute-start(bf16[64,448]{1,0:T(8,128)(2,1)S(1)} %copy-done.6), channel_id=1, source_target_pairs={{0,384},{16,400},{32,416},{48,432},{64,448},{80,464},{96,480},{112... | collective-permute-start | bytes 172040 | tf_op jit(solution)/shard_map/ppermute | solution.py:202
  59.6 11.6 %collective-permute-done.4.up1_ref = bf16[64,448]{1,0:T(8,128)(2,1)S(1)} collective-permute-done((bf16[64,448]{1,0:T(8,128)(2,1)S(1)}, bf16[64,448]{1,0:T(8,128)(2,1)S(1)}, u32[]{:S(2)}, u32[]{:S(2)}) %collective-permute-start.4) | collective-permute-done | bytes 57376 | tf_op jit(solution)/shard_map/ppermute | solution.py:202
  71.2 1.4 collective-permute-done.5.up2_ref
  72.6 1.4 collective-permute-done.6.up3_ref
  74.0 17.0 %all-gather.3.cloned.1.call-done = bf16[8,104,1152]{2,1,0:T(8,128)(2,1)} async-done(((bf16[2,104,1152]{2,1,0:T(8,128)(2,1)}), bf16[8,104,1152]{2,1,0:T(8,128)(2,1)}) %all-gather.3.cloned.1.call-update) | async-done | bytes 1916944 | tf_op jit(solution)/shard_map/all_gather | solution.py:219
  91.0 1.5 copy-done
  92.6 5.0 %shard_map.67 = (bf16[4,256,768]{2,1,0:T(8,128)(2,1)}, f32[4,1,256]{2,1,0:T(1,128)S(1)}) custom-call(s32[1]{0:T(128)} %bitcast.place_ref, s32[32]{0:T(128)S(1)} %copy-done.9, bf16[8,144,1024]{2,1,0:T(8,128)(2,1)S(1)} %all-to-all-done.rows_ref, bf16[4,2,104,1152]{3,2,1,0:T(8,128)(2,1)S(1)} %bitcast.12, bf16[64,448]{1,0:T(8,128)(2,1)S(1)} %copy-done.6, ...), custom_call_target="tpu_custom_call" | custom-call | tf_op jit(solution)/shard_map/pallas_call | solution.py:158
  97.6 4.4 %all-to-all-start.1 = ((bf16[8,144,768]{2,1,0:T(8,128)(2,1)}), bf16[8,144,768]{2,1,0:T(8,128)(2,1)}, u32[]{:S(2)}, u32[]{:S(2)}) async-start(bf16[8,144,768]{2,1,0:T(8,128)(2,1)} %copy-done.3), calls=%async_computation.1 | async-start | bytes 3538944 | tf_op jit(solution)/shard_map/all_to_all | solution.py:226
  102.1 0.7 reduce-scatter.3.cloned.1.call-update
  102.8 21.9 %all-to-all-done.1.rows_ref = bf16[8,144,768]{2,1,0:T(8,128)(2,1)} async-done(((bf16[8,144,768]{2,1,0:T(8,128)(2,1)}), bf16[8,144,768]{2,1,0:T(8,128)(2,1)}, u32[]{:S(2)}, u32[]{:S(2)}) %all-to-all-start.1) | async-done | bytes 1769504 | tf_op jit(solution)/shard_map/all_to_all | solution.py:226
  124.7 6.8 %shard_map.68 = (bf16[4,192,768]{2,1,0:T(8,128)(2,1)}, f32[4,1,192]{2,1,0:T(1,128)S(1)}) custom-call(s32[1]{0:T(128)} %bitcast.place_ref, s32[32]{0:T(128)S(1)} %copy-done.9, bf16[8,144,768]{2,1,0:T(8,128)(2,1)} %all-to-all-done.1.rows_ref, bf16[4,2,104,1152]{3,2,1,0:T(8,128)(2,1)S(1)} %bitcast.13, bf16[64,448]{1,0:T(8,128)(2,1)S(1)} %copy-done.6, ...), custom_call_target="tpu_custom_call" | custom-call | tf_op jit(solution)/shard_map/pallas_call | solution.py:158
  132.2 7.1 %all-to-all-start.2 = ((f32[4,1,448]{2,1,0:T(1,128)}), f32[4,1,448]{2,1,0:T(1,128)S(1)}, u32[]{:S(2)}, u32[]{:S(2)}) async-start(f32[4,1,448]{2,1,0:T(1,128)} %pad_maximum_fusion.1), calls=%async_computation.2 | async-start | bytes 16384 | tf_op jit(solution)/shard_map/all_to_all | solution.py:230
  139.4 42.6 %reduce-scatter.3.cloned.1.call-done = bf16[1,256,768]{2,1,0:T(8,128)(2,1)} async-done(((bf16[4,256,768]{2,1,0:T(8,128)(2,1)}), bf16[1,256,768]{2,1,0:T(8,128)(2,1)}) %reduce-scatter.3.cloned.1.call-update) | async-done | bytes 393232 | tf_op jit(solution)/shard_map/reduce_scatter | solution.py:225
  182.0 61.1 %reduce-scatter.5.cloned.1.call-done = bf16[1,192,768]{2,1,0:T(8,128)(2,1)} async-done(((bf16[4,192,768]{2,1,0:T(8,128)(2,1)}), bf16[1,192,768]{2,1,0:T(8,128)(2,1)}) %reduce-scatter.5.cloned.1.call-update) | async-done | bytes 294928 | tf_op jit(solution)/shard_map/reduce_scatter | solution.py:229
  243.1 1.0 copy-done.4
  244.0 1.0 copy-done.5
  245.3 1.1 copy.10
  (31 shorter events, 2.5 us)
Async XLA Ops:
  6.5 0.9 copy-start.7
  7.5 0.7 copy-start.8
  9.1 19.7 %collective-permute-start = (bf16[24,1152]{1,0:T(8,128)(2,1)S(1)}, bf16[24,1152]{1,0:T(8,128)(2,1)S(1)}, u32[]{:S(2)}, u32[]{:S(2)}) collective-permute-start(bf16[24,1152]{1,0:T(8,128)(2,1)S(1)} %get-tuple-element.27), channel_id=1, source_target_pairs={{0,128},{16,144},{32,160},{48,176},{64,192},{80,208},{96,224},{112... | collective-permute-start | bytes 165896 | tf_op jit(solution)/shard_map/ppermute | solution.py:202
  14.9 14.0 %collective-permute-start.1 = (bf16[24,1152]{1,0:T(8,128)(2,1)S(1)}, bf16[24,1152]{1,0:T(8,128)(2,1)S(1)}, u32[]{:S(2)}, u32[]{:S(2)}) collective-permute-start(bf16[24,1152]{1,0:T(8,128)(2,1)S(1)} %get-tuple-element.26), channel_id=1, source_target_pairs={{0,256},{16,272},{32,288},{48,304},{64,320},{80,336},{96,352},{112... | collective-permute-start | bytes 165896 | tf_op jit(solution)/shard_map/ppermute | solution.py:202
  23.7 6.5 %collective-permute-start.2 = (bf16[24,1152]{1,0:T(8,128)(2,1)S(1)}, bf16[24,1152]{1,0:T(8,128)(2,1)S(1)}, u32[]{:S(2)}, u32[]{:S(2)}) collective-permute-start(bf16[24,1152]{1,0:T(8,128)(2,1)S(1)} %get-tuple-element.25), channel_id=1, source_target_pairs={{0,384},{16,400},{32,416},{48,432},{64,448},{80,464},{96,480},{112... | collective-permute-start | bytes 165896 | tf_op jit(solution)/shard_map/ppermute | solution.py:202
  30.3 10.0 %collective-permute-start.3 = (bf16[104,1152]{1,0:T(8,128)(2,1)S(1)}, bf16[104,1152]{1,0:T(8,128)(2,1)S(1)}, u32[]{:S(2)}, u32[]{:S(2)}) collective-permute-start(bf16[104,1152]{1,0:T(8,128)(2,1)S(1)} %shard_map.66), channel_id=1, source_target_pairs={{0,64},{16,80},{32,96},{48,112},{64,0},{80,16},{96,32},{112,48},{1... | collective-permute-start | bytes 718856 | tf_op jit(solution)/shard_map/ppermute | solution.py:215
  37.6 1.4 copy-start.2
  39.0 1.3 copy-start.3
  41.1 5.5 %copy-start.6 = (bf16[64,448]{1,0:T(8,128)(2,1)S(1)}, bf16[64,448]{1,0:T(8,128)(2,1)}, u32[]{:S(2)}) copy-start(bf16[64,448]{1,0:T(8,128)(2,1)} %up0_ref.3) | copy-start | bytes 172036
  41.1 49.9 %copy-start.9 = (s32[32]{0:T(128)S(1)}, s32[32]{0:T(128)}, u32[]{:S(2)}) copy-start(s32[32]{0:T(128)} %counts_ref.5) | copy-start | bytes 388
  41.1 49.9 %all-to-all-start = ((bf16[8,144,1024]{2,1,0:T(8,128)(2,1)}), bf16[8,144,1024]{2,1,0:T(8,128)(2,1)S(1)}, u32[]{:S(2)}, u32[]{:S(2)}) async-start(bf16[8,144,1024]{2,1,0:T(8,128)(2,1)} %copy-done.2), calls=%async_computation | async-start | bytes 4718592 | tf_op jit(solution)/shard_map/all_to_all | solution.py:226
  45.9 45.1 %all-gather.3.cloned.1.call-start = ((), (), s32[]{:S(2)}) async-start(), calls=%async_computation.7 | async-start | bytes 2396160 | tf_op jit(solution)/shard_map/all_gather | solution.py:219
  46.6 24.5 %collective-permute-start.4 = (bf16[64,448]{1,0:T(8,128)(2,1)S(1)}, bf16[64,448]{1,0:T(8,128)(2,1)S(1)}, u32[]{:S(2)}, u32[]{:S(2)}) collective-permute-start(bf16[64,448]{1,0:T(8,128)(2,1)S(1)} %copy-done.6), channel_id=1, source_target_pairs={{0,128},{16,144},{32,160},{48,176},{64,192},{80,208},{96,224},{112... | collective-permute-start | bytes 172040 | tf_op jit(solution)/shard_map/ppermute | solution.py:202
  48.8 23.8 %collective-permute-start.5 = (bf16[64,448]{1,0:T(8,128)(2,1)S(1)}, bf16[64,448]{1,0:T(8,128)(2,1)S(1)}, u32[]{:S(2)}, u32[]{:S(2)}) collective-permute-start(bf16[64,448]{1,0:T(8,128)(2,1)S(1)} %copy-done.6), channel_id=1, source_target_pairs={{0,256},{16,272},{32,288},{48,304},{64,320},{80,336},{96,352},{112... | collective-permute-start | bytes 172040 | tf_op jit(solution)/shard_map/ppermute | solution.py:202
  56.5 17.5 %collective-permute-start.6 = (bf16[64,448]{1,0:T(8,128)(2,1)S(1)}, bf16[64,448]{1,0:T(8,128)(2,1)S(1)}, u32[]{:S(2)}, u32[]{:S(2)}) collective-permute-start(bf16[64,448]{1,0:T(8,128)(2,1)S(1)} %copy-done.6), channel_id=1, source_target_pairs={{0,384},{16,400},{32,416},{48,432},{64,448},{80,464},{96,480},{112... | collective-permute-start | bytes 172040 | tf_op jit(solution)/shard_map/ppermute | solution.py:202
  91.0 1.5 copy-start
  97.6 27.2 %copy-start.1 = (bf16[8,104,1152]{2,1,0:T(8,128)(2,1)S(1)}, bf16[8,104,1152]{2,1,0:T(8,128)(2,1)}, u32[]{:S(2)}) copy-start(bf16[8,104,1152]{2,1,0:T(8,128)(2,1)} %all-gather.3.cloned.1.call-done) | copy-start | bytes 5750788
  97.6 27.2 %all-to-all-start.1 = ((bf16[8,144,768]{2,1,0:T(8,128)(2,1)}), bf16[8,144,768]{2,1,0:T(8,128)(2,1)}, u32[]{:S(2)}, u32[]{:S(2)}) async-start(bf16[8,144,768]{2,1,0:T(8,128)(2,1)} %copy-done.3), calls=%async_computation.1 | async-start | bytes 3538944 | tf_op jit(solution)/shard_map/all_to_all | solution.py:226
  102.0 79.9 %reduce-scatter.3.cloned.1.call-start = ((), (), s32[]{:S(2)}) async-start(), calls=%async_computation.5 | async-start | bytes 1966080 | tf_op jit(solution)/shard_map/reduce_scatter | solution.py:225
  102.8 36.6 %copy-start.10 = (bf16[448]{0:T(512)(128)(2,1)S(1)}, bf16[448]{0:T(512)(128)(2,1)}, u32[]{:S(2)}) copy-start(bf16[448]{0:T(512)(128)(2,1)} %param.10) | copy-start | bytes 2692
  102.8 140.2 %reduce-scatter.5.cloned.1.call-start = ((), (), s32[]{:S(2)}) async-start(), calls=%async_computation.6 | async-start | bytes 1474560 | tf_op jit(solution)/shard_map/reduce_scatter | solution.py:229
  132.2 49.8 %all-to-all-start.2 = ((f32[4,1,448]{2,1,0:T(1,128)}), f32[4,1,448]{2,1,0:T(1,128)S(1)}, u32[]{:S(2)}, u32[]{:S(2)}) async-start(f32[4,1,448]{2,1,0:T(1,128)} %pad_maximum_fusion.1), calls=%async_computation.2 | async-start | bytes 16384 | tf_op jit(solution)/shard_map/all_to_all | solution.py:230
  243.0 1.0 copy-start.4
  244.0 1.0 copy-start.5
Sparse Core Ops, SparseCore 0:
  48.8 42.1 all-gather.2
  105.7 76.2 reduce-scatter.2
  184.9 58.1 reduce-scatter.4

commit v2 on v1

v2 whole, which is shorter than its diff:
```python
import functools

import jax
import jax.numpy as jnp
from jax import lax
from jax.experimental import pallas as pl
from jax.experimental.pallas import tpu as pltpu
from jax.sharding import PartitionSpec as P

AXIS = "fsdp"
GROUP = 8
PAIRS = 4
SLOTS = 144
RANK = 64
UNITS = 448
KEYS = GROUP * SLOTS
TOKENS = 768
OWN_TOKENS = 24
FEATURES = 4096
WINDOW = 384
CHUNKS = ((0, 256), (256, 192))
HALF = TOKENS // 2
TAIL = 16
LANES = 384
VMEM_LIMIT = 48 * 1024 * 1024

NEAR = [[GROUP * p + i for i in range(GROUP)] for p in range(PAIRS)]
FAR = [[GROUP * p + i for p in range(PAIRS)] for i in range(GROUP)]


def whole(memory_space=pltpu.VMEM):
    return pl.BlockSpec(memory_space=memory_space)


def params():
    return pltpu.CompilerParams(vmem_limit_bytes=VMEM_LIMIT)


def window_kernel(place_ref, counts_ref, tokens_ref, out_ref, padded, lined):
    padded[:, FEATURES:] = jnp.zeros((OWN_TOKENS, WINDOW), jnp.float32)
    padded[:, :FEATURES] = tokens_ref[...].astype(jnp.float32)
    starts = [jnp.int32(0)]
    for f in range(GROUP * PAIRS - 1):
        starts.append(starts[-1] + counts_ref[f])
    pair = place_ref[0] // GROUP
    lane = lax.broadcasted_iota(jnp.int32, (OWN_TOKENS, WINDOW), 1)
    for target in range(PAIRS):
        for i in range(GROUP):
            start = starts[GROUP * target + i]
            base = pl.multiple_of((start // 128) * 128, 128)
            place = SLOTS * i
            low = (place // 128) * 128
            rest = place - low
            shift = lax.rem(rest - (start - base) + WINDOW, WINDOW)
            moved = pltpu.roll(padded[:, pl.ds(base, WINDOW)], shift, 1)
            keep = (lane >= rest) & (lane < rest + SLOTS)
            lined[:, low : low + WINDOW] = jnp.where(keep, moved, lined[:, low : low + WINDOW])
        out_ref[lax.rem(target - pair + PAIRS, PAIRS)] = lined[:, :KEYS].astype(jnp.bfloat16)


def own_windows(place, counts, tokens):
    return pl.pallas_call(
        window_kernel,
        out_shape=jax.ShapeDtypeStruct((PAIRS, OWN_TOKENS, KEYS), jnp.bfloat16),
        in_specs=[whole(pltpu.SMEM), whole(pltpu.SMEM), whole()],
        out_specs=whole(),
        scratch_shapes=[
            pltpu.VMEM((OWN_TOKENS, FEATURES + WINDOW), jnp.float32),
            pltpu.VMEM((OWN_TOKENS, KEYS + 128), jnp.float32),
        ],
        compiler_params=params(),
    )(place, counts, tokens)


def collect_kernel(place_ref, own_ref, one_ref, two_ref, three_ref, down_ref, out_ref, rows):
    pair = place_ref[0] // GROUP
    blocks = (own_ref[0], one_ref[...], two_ref[...], three_ref[...])
    for step, block in enumerate(blocks):
        origin = lax.rem(pair - step + PAIRS, PAIRS)
        rows[pl.ds(pl.multiple_of(origin * OWN_TOKENS, 8), OWN_TOKENS), :] = block.astype(jnp.float32)
    down = down_ref[...].astype(jnp.float32)
    rows[PAIRS * OWN_TOKENS :, :] = jnp.concatenate(
        [down[8 * g : 8 * g + 8, :] for g in range(SLOTS // 8)], axis=1
    )
    out_ref[...] = rows[...].astype(jnp.bfloat16)


def collect(place, own, one, two, three, down):
    height = PAIRS * OWN_TOKENS + 8
    return pl.pallas_call(
        collect_kernel,
        out_shape=jax.ShapeDtypeStruct((height, KEYS), jnp.bfloat16),
        in_specs=[whole(pltpu.SMEM)] + [whole()] * 5,
        out_specs=whole(),
        scratch_shapes=[pltpu.VMEM((height, KEYS), jnp.float32)],
        compiler_params=params(),
    )(place, own, one, two, three, down)


def pack_kernel(rows_ref, out_ref):
    step = pl.program_id(0)
    for q in range(PAIRS):

        @pl.when(step == q)
        def _():
            for i in range(GROUP):
                out_ref[i, :, UNITS * q : UNITS * (q + 1)] = rows_ref[:, UNITS * i : UNITS * (i + 1)]


def pack(rows):
    return pl.pallas_call(
        pack_kernel,
        grid=(PAIRS,),
        out_shape=jax.ShapeDtypeStruct((GROUP, SLOTS, PAIRS * UNITS), jnp.bfloat16),
        in_specs=[pl.BlockSpec((SLOTS, GROUP * UNITS), lambda q: (0, q))],
        out_specs=pl.BlockSpec((GROUP, SLOTS, PAIRS * UNITS), lambda q: (0, 0, 0)),
        compiler_params=params(),
    )(rows)


def assemble_kernel(place_ref, *refs):
    block_refs, up_refs = refs[:4], refs[4:8]
    tokens_ref, down_ref, up_ref = refs[8:]
    place = place_ref[0]
    pair, side, x = place // GROUP, (place // 4) % 2, place % 4
    for step, block_ref in enumerate(block_refs):
        for far in range(2):
            origin = 4 * lax.rem(side + far, 2) + lax.rem(x - step + 4, 4)
            tokens_ref[pl.ds(pl.multiple_of(origin * 96, 96), 96), :] = block_ref[far, 0:96, :]
            folded = block_ref[far, 96:104, :].astype(jnp.float32)
            down_ref[origin] = jnp.concatenate(
                [folded[:, RANK * g : RANK * g + RANK] for g in range(SLOTS // 8)], axis=0
            ).astype(jnp.bfloat16)
    for step, ref in enumerate(up_refs):
        up_ref[lax.rem(pair - step + PAIRS, PAIRS)] = ref[...]


def assemble(place, blocks, ups):
    return pl.pallas_call(
        assemble_kernel,
        out_shape=[
            jax.ShapeDtypeStruct((TOKENS, KEYS), jnp.bfloat16),
            jax.ShapeDtypeStruct((GROUP, SLOTS, RANK), jnp.bfloat16),
            jax.ShapeDtypeStruct((PAIRS, RANK, UNITS), jnp.bfloat16),
        ],
        in_specs=[whole(pltpu.SMEM)] + [whole()] * 8,
        out_specs=[whole()] * 3,
        compiler_params=params(),
    )(place, *blocks, *ups)


def split(total):
    pieces = [total[:, : UNITS // 2], total[:, UNITS // 2 :]]
    rows = []
    for piece in pieces:
        high = piece.astype(jnp.bfloat16).astype(jnp.float32)
        rows += [high, piece - high]
    rows.append(jnp.zeros((TAIL - 4, UNITS // 2), jnp.float32))
    rows = jnp.concatenate(rows, axis=0)
    return jnp.concatenate([rows, jnp.zeros((TAIL, LANES - UNITS // 2), jnp.float32)], axis=1).astype(jnp.bfloat16)


def joined(tail):
    rows = tail.astype(jnp.float32)[:, : UNITS // 2]
    return jnp.concatenate([rows[0:1] + rows[1:2], rows[2:3] + rows[3:4]], axis=1)


def partial_kernel(chunk, place_ref, counts_ref, rows_ref, tokens_ref, down_ref, up_ref, *refs):
    first, width = chunk
    last = first > 0
    earlier_ref = refs[0] if last else None
    squares_ref, out_ref, above_ref, below_ref, merged = refs[-5:]
    pair = place_ref[0] // GROUP
    row = lax.broadcasted_iota(jnp.int32, (SLOTS, width), 0)
    valid = [row < counts_ref[GROUP * pair + i] for i in range(GROUP)]
    for q in range(PAIRS):
        up = up_ref[q, :, first : first + width]
        total = jnp.zeros((1, width), jnp.float32)
        begin = UNITS * q + first
        for i in range(GROUP):
            low = jnp.dot(down_ref[i], up, preferred_element_type=jnp.float32)
            base = rows_ref[i, :, begin : begin + width].astype(jnp.float32)
            value = jnp.where(valid[i], base + low, 0.0)
            total = total + jnp.sum(value * value, axis=0, keepdims=True)
            merged[SLOTS * i : SLOTS * i + SLOTS, :] = value.astype(jnp.bfloat16)
        product = jnp.dot(tokens_ref[...], merged[...], preferred_element_type=jnp.float32)
        offset = lax.rem(q - pair + PAIRS, PAIRS)
        if last:
            product = jnp.concatenate([product[:HALF], product[HALF:]], axis=1)
            total = jnp.concatenate([earlier_ref[offset], total], axis=1)
        out_ref[offset] = product
        squares_ref[offset] = total

        @pl.when(offset == 3)
        def _():
            above_ref[: product.shape[0]] = product.astype(jnp.bfloat16)
            if last:
                above_ref[HALF:] = split(total)

        @pl.when(offset == 1)
        def _():
            below_ref[: product.shape[0]] = product.astype(jnp.bfloat16)
            if last:
                below_ref[HALF:] = split(total)


def partial_products(chunk, place, counts, rows, tokens, down, up, *earlier):
    width = chunk[1]
    shape = (HALF, 2 * width) if earlier else (TOKENS, width)
    sent = (HALF + TAIL, 2 * width) if earlier else shape
    out_shape = [
        jax.ShapeDtypeStruct((PAIRS, 1, UNITS if earlier else width), jnp.float32),
        jax.ShapeDtypeStruct((PAIRS,) + shape, jnp.float32),
        jax.ShapeDtypeStruct(sent, jnp.bfloat16),
        jax.ShapeDtypeStruct(sent, jnp.bfloat16),
    ]
    return pl.pallas_call(
        functools.partial(partial_kernel, chunk),
        out_shape=out_shape,
        in_specs=[whole(pltpu.SMEM), whole(pltpu.SMEM)] + [whole()] * (4 + len(earlier)),
        out_specs=[whole()] * len(out_shape),
        scratch_shapes=[pltpu.VMEM((KEYS, width), jnp.bfloat16)],
        compiler_params=params(),
    )(place, counts, rows, tokens, down, up, *earlier)


def forward_kernel(up_got_ref, down_got_ref, up_own_ref, down_own_ref, up_squares_ref, down_squares_ref, up_ref, down_ref):
    height = up_own_ref.shape[1]
    for got, own, squares, out in (
        (up_got_ref, up_own_ref, up_squares_ref, up_ref),
        (down_got_ref, down_own_ref, down_squares_ref, down_ref),
    ):
        out[:height] = (got[:height].astype(jnp.float32) + own[0]).astype(jnp.bfloat16)
        if out.shape[0] > height:
            out[height:] = split(joined(got[height:]) + squares[0])


def forward(up_got, down_got, products, squares, step):
    def own(array, offset):
        return pl.BlockSpec((1,) + array.shape[1:], lambda _: (offset, 0, 0))

    got = pl.BlockSpec(up_got.shape, lambda _: (0, 0))
    return pl.pallas_call(
        forward_kernel,
        grid=(1,),
        out_shape=[jax.ShapeDtypeStruct(up_got.shape, jnp.bfloat16)] * 2,
        in_specs=[got, got]
        + [own(products, PAIRS - step), own(products, step), own(squares, PAIRS - step), own(squares, step)],
        out_specs=[got, got],
        compiler_params=params(),
    )(up_got, down_got, products, products, squares, squares)


def finish_kernel(squares_ref, scale_ref, *refs):
    out_ref = refs[-1]
    own, above, below = refs[0:3]
    front = own[0] + above[...].astype(jnp.float32) + below[...].astype(jnp.float32)
    own, above, below = refs[3:6]
    back = own[0] + above[:HALF].astype(jnp.float32) + below[:HALF].astype(jnp.float32)
    width = back.shape[1] // 2
    back = jnp.concatenate([back[:, :width], back[:, width:]], axis=0)
    total = squares_ref[0] + joined(above[HALF:]) + joined(below[HALF:])
    factor = scale_ref[...].astype(jnp.float32) / jnp.sqrt(total + 1e-06)
    result = jnp.concatenate([front, back], axis=1)
    result = jnp.where(factor == 0.0, 0.0, result * factor)
    out_ref[...] = jnp.concatenate(
        [
            result[OWN_TOKENS * (PAIRS * i + q) : OWN_TOKENS * (PAIRS * i + q + 1), :]
            for q in range(PAIRS)
            for i in range(GROUP)
        ],
        axis=0,
    ).astype(jnp.bfloat16)


def finish(squares, scale, sums):
    def same(*shape):
        return pl.BlockSpec(shape, lambda _: (0,) * len(shape))

    return pl.pallas_call(
        finish_kernel,
        grid=(1,),
        out_shape=jax.ShapeDtypeStruct((TOKENS, UNITS), jnp.bfloat16),
        in_specs=[same(1, 1, UNITS), same(1, UNITS)]
        + [same(1, *array.shape[1:]) if array.ndim == 3 else same(*array.shape) for array in sums],
        out_specs=same(TOKENS, UNITS),
        compiler_params=params(),
    )(squares, scale, *sums)


def to_pair(array, step):
    return lax.ppermute(
        array,
        AXIS,
        [(GROUP * p + i, GROUP * ((p + step) % PAIRS) + i) for p in range(PAIRS) for i in range(GROUP)],
    )


def along_x(array, step):
    return lax.ppermute(array, AXIS, [(4 * z + x, 4 * z + (x + step) % 4) for z in range(8) for x in range(4)])


def hop(array, froms, way):
    return lax.ppermute(
        array, AXIS, [(GROUP * p + i, GROUP * (p + way) + i) for p in froms for i in range(GROUP)]
    )


def exchange(send):
    return lax.all_to_all(send, AXIS, 0, 0, axis_index_groups=NEAR, tiled=True)


def hops(sends, step):
    return hop(sends[0], range(step), 1), hop(sends[1], range(PAIRS - step, PAIRS), -1)


def body(tokens, frozen_slot_rows, adapter_down_factor, adapter_up_factor, magnitude, counts):
    place = lax.axis_index(AXIS).astype(jnp.int32).reshape(1)
    send = pack(frozen_slot_rows)
    rows = exchange(send)
    own = own_windows(place, counts, tokens)
    moved = [to_pair(own[step], step) for step in range(1, PAIRS)]
    ups = [adapter_up_factor] + [to_pair(adapter_up_factor, step) for step in range(1, PAIRS)]
    column = collect(place, own, *moved, adapter_down_factor)
    other = lax.ppermute(column, AXIS, [(f, f ^ 4) for f in range(GROUP * PAIRS)])
    blocks = jnp.stack([column, other])
    blocks = [blocks] + [along_x(blocks, step) for step in (1, 3, 2)]
    blocks = [blocks[0], blocks[1], blocks[3], blocks[2]]
    all_tokens, down, up = assemble(place, blocks, ups)
    a_squares, a, *ready = partial_products(CHUNKS[0], place, counts, rows, all_tokens, down, up)
    a_got = hops(ready, 1)
    squares, b, *ready = partial_products(CHUNKS[1], place, counts, rows, all_tokens, down, up, a_squares)
    b_got = hops(ready, 1)
    for step in range(2, PAIRS):
        a_got = hops(forward(*a_got, a, a_squares, step), step)
        b_got = hops(forward(*b_got, b, squares, step), step)
    return finish(squares, magnitude.reshape(1, UNITS), [a, *a_got, b, *b_got])


def solution(mesh):
    in_specs = (
        P(("dp", "fsdp"), None),
        P(("dp", "fsdp"), None),
        P(("dp", "fsdp"), None),
        P("dp", "fsdp"),
        P(("dp", "fsdp")),
        P("dp"),
    )
    out_specs = P("dp", "fsdp")
    return jax.shard_map(body, mesh=mesh, in_specs=in_specs, out_specs=out_specs, check_vma=False)
```

time: 254 us -> 226 us (0.89)
  waiting for transfers between devices: 160 us -> 58.7 us
  starting transfers between devices: 52 us -> 136 us
  between operations: 13.3 us -> 0.37 us
  Pallas kernels: 16.7 us -> 25.6 us
  local copies, waits for them, and re-layouts: 9.75 us -> 3.25 us
    reduce_scatter x2 -> x0, waiting for transfers between devices: 104 us -> none  [body(): lax.psum_scatter(product, AXIS, axis_index_groups=FAR, scatter_dimension=...]
    ppermute x0 -> x15, starting transfers between devices: none -> 83.1 us  [the longest x12 72.6 us: hop(): lax.ppermute(array, AXIS, [(GROUP * p + i, GROUP * (p + way) + i) for p i...]
    ppermute x0 -> x15, waiting for transfers between devices: none -> 24.6 us  [the longest x12 24.6 us: hop(): lax.ppermute(array, AXIS, [(GROUP * p + i, GROUP * (p + way) + i) for p i...]
    all_to_all x3 -> x1, waiting for transfers between devices: 21.9 us -> 0.01 us  [exchange(): return lax.all_to_all(send, AXIS, 0, 0, axis_index_groups=NEAR, tiled=True)]
    all_gather x1 -> x0, waiting for transfers between devices: 17 us -> none  [body(): lax.all_gather(pair_blocks, AXIS, axis_index_groups=ALONG_X, axis=0)]
    ppermute x6, waiting for transfers between devices: 15.8 us -> 30.6 us  [to_pair(): lax.ppermute(array, AXIS, [(GROUP * p + i, GROUP * ((p + step) % PAIRS) +...]
    ppermute x1, starting transfers between devices: 3.76 us -> 17.7 us  [body(): lax.ppermute(column, AXIS, [(f, f ^ 4) for f in range(GROUP * PAIRS)])]
    all_to_all x3 -> x1, starting transfers between devices: 16.3 us -> 6.35 us  [exchange(): return lax.all_to_all(send, AXIS, 0, 0, axis_index_groups=NEAR, tiled=True)]
  transfers between devices with their start and end apart: 13 -> 23, of which waited for: 8 -> 10; matrix products, arithmetic and copies ran while one was open for 1% -> 0% of each run, Pallas kernels for 4% -> 5%
where the time goes in v2:
time: 226 us; the launch traced here: 224 us
  starting transfers between devices  136 us (60%)
  waiting for transfers between devices  58.7 us (26%)
  Pallas kernels  25.6 us (11%)
  local copies, waits for them, and re-layouts  3.25 us (1%)
    ppermute x12, starting transfers between devices, hop(): lax.ppermute(array, AXIS, [(GROUP * p + i, GROUP * (p + way) + i) for p i...  72.6 us
    ppermute x6, waiting for transfers between devices, to_pair(): lax.ppermute(array, AXIS, [(GROUP * p + i, GROUP * ((p + step) % PAIRS) +...  30.6 us
    ppermute x6, starting transfers between devices, to_pair(): lax.ppermute(array, AXIS, [(GROUP * p + i, GROUP * ((p + step) % PAIRS) +...  28.5 us
    ppermute x12, waiting for transfers between devices, hop(): lax.ppermute(array, AXIS, [(GROUP * p + i, GROUP * (p + way) + i) for p i...  24.6 us
    pallas_call x2, Pallas kernels, partial_products(): pl.pallas_call(functools.partial(partial_kernel, chunk), out_shape=out_sh...  18.3 us
    ppermute x1, starting transfers between devices, body(): lax.ppermute(column, AXIS, [(f, f ^ 4) for f in range(GROUP * PAIRS)])  17.7 us
    ppermute x3, starting transfers between devices, along_x(): lax.ppermute(array, AXIS, [(4 * z + x, 4 * z + (x + step) % 4) for z in r...  10.6 us
    all_to_all x1, starting transfers between devices, exchange(): return lax.all_to_all(send, AXIS, 0, 0, axis_index_groups=NEAR, tiled=True)  6.35 us
  transfers between devices with their start and end apart: 23, of which 10 were waited for; matrix products, arithmetic and copies ran while one was open for 0% of the time, Pallas kernels for 5%

profile of v2, /device:TPU:1, one launch (start us, length us, event | category | flops | bytes accessed | tf_op | source)
XLA Modules:
  0.0 223.7 jit_solution(15443762580043333498)
XLA Ops:
  0.0 3.3 %shard_map.64 = bf16[8,144,1792]{2,1,0:T(8,128)(2,1)S(1)} custom-call(bf16[144,14336]{1,0:T(8,128)(2,1)} %rows_ref.1), custom_call_target="tpu_custom_call" | custom-call | tf_op jit(solution)/shard_map/pallas_call | solution.py:111
  3.3 2.0 copy-done.1
  5.3 6.3 %all-to-all-start = ((bf16[8,144,1792]{2,1,0:T(8,128)(2,1)}), bf16[8,144,1792]{2,1,0:T(8,128)(2,1)}, u32[]{:S(2)}, u32[]{:S(2)}) async-start(bf16[8,144,1792]{2,1,0:T(8,128)(2,1)} %copy-done.1), calls=%async_computation | async-start | bytes 8257536 | tf_op jit(solution)/shard_map/all_to_all | solution.py:310
  12.7 4.9 %collective-permute-start = (bf16[24,1152]{1,0:T(8,128)(2,1)S(1)}, bf16[24,1152]{1,0:T(8,128)(2,1)S(1)}, u32[]{:S(2)}, u32[]{:S(2)}) collective-permute-start(bf16[24,1152]{1,0:T(8,128)(2,1)S(1)} %get-tuple-element.45), channel_id=1, source_target_pairs={{0,128},{16,144},{32,160},{48,176},{64,192},{80,208},{96,224},{112... | collective-permute-start | bytes 165896 | tf_op jit(solution)/shard_map/ppermute | solution.py:292
  17.6 8.8 %collective-permute-start.1 = (bf16[24,1152]{1,0:T(8,128)(2,1)S(1)}, bf16[24,1152]{1,0:T(8,128)(2,1)S(1)}, u32[]{:S(2)}, u32[]{:S(2)}) collective-permute-start(bf16[24,1152]{1,0:T(8,128)(2,1)S(1)} %get-tuple-element.44), channel_id=1, source_target_pairs={{0,256},{16,272},{32,288},{48,304},{64,320},{80,336},{96,352},{112... | collective-permute-start | bytes 165896 | tf_op jit(solution)/shard_map/ppermute | solution.py:292
  26.4 4.3 %collective-permute-start.2 = (bf16[24,1152]{1,0:T(8,128)(2,1)S(1)}, bf16[24,1152]{1,0:T(8,128)(2,1)S(1)}, u32[]{:S(2)}, u32[]{:S(2)}) collective-permute-start(bf16[24,1152]{1,0:T(8,128)(2,1)S(1)} %get-tuple-element.43), channel_id=1, source_target_pairs={{0,384},{16,400},{32,416},{48,432},{64,448},{80,464},{96,480},{112... | collective-permute-start | bytes 165896 | tf_op jit(solution)/shard_map/ppermute | solution.py:292
  30.8 21.7 %collective-permute-done.one_ref = bf16[24,1152]{1,0:T(8,128)(2,1)S(1)} collective-permute-done((bf16[24,1152]{1,0:T(8,128)(2,1)S(1)}, bf16[24,1152]{1,0:T(8,128)(2,1)S(1)}, u32[]{:S(2)}, u32[]{:S(2)}) %collective-permute-start) | collective-permute-done | bytes 55328 | tf_op jit(solution)/shard_map/ppermute | solution.py:292
  52.5 1.2 collective-permute-done.1.two_ref
  55.0 17.7 %collective-permute-start.3 = (bf16[104,1152]{1,0:T(8,128)(2,1)S(1)}, bf16[104,1152]{1,0:T(8,128)(2,1)S(1)}, u32[]{:S(2)}, u32[]{:S(2)}) collective-permute-start(bf16[104,1152]{1,0:T(8,128)(2,1)S(1)} %shard_map.66), channel_id=1, source_target_pairs={{0,64},{16,80},{32,96},{48,112},{64,0},{80,16},{96,32},{112,48},{1... | collective-permute-start | bytes 718856 | tf_op jit(solution)/shard_map/ppermute | solution.py:325
  72.7 3.5 %collective-permute-done.3 = bf16[104,1152]{1,0:T(8,128)(2,1)S(1)} collective-permute-done((bf16[104,1152]{1,0:T(8,128)(2,1)S(1)}, bf16[104,1152]{1,0:T(8,128)(2,1)S(1)}, u32[]{:S(2)}, u32[]{:S(2)}) %collective-permute-start.3) | collective-permute-done | bytes 239648 | tf_op jit(solution)/shard_map/ppermute | solution.py:325
  76.2 3.2 %collective-permute-start.4 = (bf16[2,104,1152]{2,1,0:T(8,128)(2,1)S(1)}, bf16[2,104,1152]{2,1,0:T(8,128)(2,1)S(1)}, u32[]{:S(2)}, u32[]{:S(2)}) collective-permute-start(bf16[2,104,1152]{2,1,0:T(8,128)(2,1)S(1)} %pad_maximum_fusion.refs_0_), channel_id=1, source_target_pairs={{0,16},{16,32},{32,48},{48,0},{64,80},{80,96},{96,112},{112,64},{1... | collective-permute-start | bytes 1437704 | tf_op jit(solution)/shard_map/ppermute | solution.py:300
  79.4 4.7 %collective-permute-start.5 = (bf16[2,104,1152]{2,1,0:T(8,128)(2,1)S(1)}, bf16[2,104,1152]{2,1,0:T(8,128)(2,1)S(1)}, u32[]{:S(2)}, u32[]{:S(2)}) collective-permute-start(bf16[2,104,1152]{2,1,0:T(8,128)(2,1)S(1)} %pad_maximum_fusion.refs_0_), channel_id=1, source_target_pairs={{0,32},{16,48},{32,0},{48,16},{64,96},{80,112},{96,64},{112,80},{1... | collective-permute-start | bytes 1437704 | tf_op jit(solution)/shard_map/ppermute | solution.py:300
  84.1 2.7 %collective-permute-start.6 = (bf16[2,104,1152]{2,1,0:T(8,128)(2,1)S(1)}, bf16[2,104,1152]{2,1,0:T(8,128)(2,1)S(1)}, u32[]{:S(2)}, u32[]{:S(2)}) collective-permute-start(bf16[2,104,1152]{2,1,0:T(8,128)(2,1)S(1)} %pad_maximum_fusion.refs_0_), channel_id=1, source_target_pairs={{0,48},{16,0},{32,16},{48,32},{64,112},{80,64},{96,80},{112,96},{1... | collective-permute-start | bytes 1437704 | tf_op jit(solution)/shard_map/ppermute | solution.py:300
  86.8 4.4 %collective-permute-start.7 = (bf16[64,448]{1,0:T(8,128)(2,1)S(1)}, bf16[64,448]{1,0:T(8,128)(2,1)S(1)}, u32[]{:S(2)}, u32[]{:S(2)}) collective-permute-start(bf16[64,448]{1,0:T(8,128)(2,1)S(1)} %copy-done.3), channel_id=1, source_target_pairs={{0,128},{16,144},{32,160},{48,176},{64,192},{80,208},{96,224},{112... | collective-permute-start | bytes 172040 | tf_op jit(solution)/shard_map/ppermute | solution.py:292
  91.3 3.5 %collective-permute-start.8 = (bf16[64,448]{1,0:T(8,128)(2,1)S(1)}, bf16[64,448]{1,0:T(8,128)(2,1)S(1)}, u32[]{:S(2)}, u32[]{:S(2)}) collective-permute-start(bf16[64,448]{1,0:T(8,128)(2,1)S(1)} %copy-done.3), channel_id=1, source_target_pairs={{0,256},{16,272},{32,288},{48,304},{64,320},{80,336},{96,352},{112... | collective-permute-start | bytes 172040 | tf_op jit(solution)/shard_map/ppermute | solution.py:292
  94.7 2.8 %collective-permute-done.7.refs_5_ = bf16[64,448]{1,0:T(8,128)(2,1)S(1)} collective-permute-done((bf16[64,448]{1,0:T(8,128)(2,1)S(1)}, bf16[64,448]{1,0:T(8,128)(2,1)S(1)}, u32[]{:S(2)}, u32[]{:S(2)}) %collective-permute-start.7) | collective-permute-done | bytes 57376 | tf_op jit(solution)/shard_map/ppermute | solution.py:292
  97.6 2.6 %collective-permute-start.9 = (bf16[64,448]{1,0:T(8,128)(2,1)S(1)}, bf16[64,448]{1,0:T(8,128)(2,1)S(1)}, u32[]{:S(2)}, u32[]{:S(2)}) collective-permute-start(bf16[64,448]{1,0:T(8,128)(2,1)S(1)} %copy-done.3), channel_id=1, source_target_pairs={{0,384},{16,400},{32,416},{48,432},{64,448},{80,464},{96,480},{112... | collective-permute-start | bytes 172040 | tf_op jit(solution)/shard_map/ppermute | solution.py:292
  100.2 1.8 collective-permute-done.8.refs_6_
  102.0 1.9 collective-permute-done.9.refs_7_
  104.2 9.7 %shard_map.68 = (f32[4,1,256]{2,1,0:T(1,128)S(1)}, f32[4,768,256]{2,1,0:T(8,128)}, bf16[768,256]{1,0:T(8,128)(2,1)S(1)}, bf16[768,256]{1,0:T(8,128)(2,1)S(1)}) custom-call(s32[1]{0:T(128)} %bitcast.place_ref, s32[32]{0:T(128)S(1)} %copy-done.4, bf16[8,144,1792]{2,1,0:T(8,128)(2,1)} %all-to-all-done.rows_ref, ...), custom_call_target="tpu_custom_call" | custom-call | tf_op jit(solution)/shard_map/pallas_call | solution.py:217
  114.0 7.3 %collective-permute-start.10 = (bf16[768,256]{1,0:T(8,128)(2,1)S(1)}, bf16[768,256]{1,0:T(8,128)(2,1)S(1)}, u32[]{:S(2)}, u32[]{:S(2)}) collective-permute-start(bf16[768,256]{1,0:T(8,128)(2,1)S(1)} %get-tuple-element.30), channel_id=1, source_target_pairs={{0,128},{16,144},{32,160},{48,176},{64,192},{80,208},{96,224},{112... | collective-permute-start | bytes 1179656 | tf_op jit(solution)/shard_map/ppermute | solution.py:304
  122.0 8.6 %shard_map.69 = (f32[4,1,448]{2,1,0:T(1,128)S(1)}, f32[4,384,384]{2,1,0:T(8,128)S(1)}, bf16[400,384]{1,0:T(8,128)(2,1)S(1)}, bf16[400,384]{1,0:T(8,128)(2,1)S(1)}) custom-call(s32[1]{0:T(128)} %bitcast.place_ref, s32[32]{0:T(128)S(1)} %copy-done.4, bf16[8,144,1792]{2,1,0:T(8,128)(2,1)} %all-to-all-done.rows_ref, ...), custom_call_target="tpu_custom_call" | custom-call | tf_op jit(solution)/shard_map/pallas_call | solution.py:217
  130.5 1.3 collective-permute-start.16
  132.7 1.3 collective-permute-start.12
  136.0 26.4 %collective-permute-start.18 = (bf16[400,384]{1,0:T(8,128)(2,1)S(1)}, bf16[400,384]{1,0:T(8,128)(2,1)S(1)}, u32[]{:S(2)}, u32[]{:S(2)}) collective-permute-start(bf16[400,384]{1,0:T(8,128)(2,1)S(1)} %get-tuple-element.39), channel_id=1, source_target_pairs={{0,128},{16,144},{32,160},{48,176},{64,192},{80,208},{96,224},{112... | collective-permute-start | bytes 921608 | tf_op jit(solution)/shard_map/ppermute | solution.py:304
  163.3 23.0 %collective-permute-start.14 = (bf16[768,256]{1,0:T(8,128)(2,1)S(1)}, bf16[768,256]{1,0:T(8,128)(2,1)S(1)}, u32[]{:S(2)}, u32[]{:S(2)}) collective-permute-start(bf16[768,256]{1,0:T(8,128)(2,1)S(1)} %get-tuple-element.34), channel_id=1, source_target_pairs={{0,128},{16,144},{32,160},{48,176},{64,192},{80,208},{96,224},{112... | collective-permute-start | bytes 1179656 | tf_op jit(solution)/shard_map/ppermute | solution.py:304
  186.3 1.3 collective-permute-start.15
  188.0 8.0 %collective-permute-start.20 = (bf16[400,384]{1,0:T(8,128)(2,1)S(1)}, bf16[400,384]{1,0:T(8,128)(2,1)S(1)}, u32[]{:S(2)}, u32[]{:S(2)}) collective-permute-start(bf16[400,384]{1,0:T(8,128)(2,1)S(1)} %get-tuple-element.41), channel_id=1, source_target_pairs={{0,128},{16,144},{32,160},{48,176},{64,192},{80,208},{96,224},{112... | collective-permute-start | bytes 921608 | tf_op jit(solution)/shard_map/ppermute | solution.py:304
  195.9 1.3 collective-permute-start.21
  197.3 3.1 %collective-permute-done.20.refs_4_ = bf16[400,384]{1,0:T(8,128)(2,1)S(1)} collective-permute-done((bf16[400,384]{1,0:T(8,128)(2,1)S(1)}, bf16[400,384]{1,0:T(8,128)(2,1)S(1)}, u32[]{:S(2)}, u32[]{:S(2)}) %collective-permute-start.20) | collective-permute-done | bytes 307232 | tf_op jit(solution)/shard_map/ppermute | solution.py:304
  200.4 20.5 %collective-permute-done.21.refs_5_ = bf16[400,384]{1,0:T(8,128)(2,1)S(1)} collective-permute-done((bf16[400,384]{1,0:T(8,128)(2,1)S(1)}, bf16[400,384]{1,0:T(8,128)(2,1)S(1)}, u32[]{:S(2)}, u32[]{:S(2)}) %collective-permute-start.21) | collective-permute-done | bytes 307232 | tf_op jit(solution)/shard_map/ppermute | solution.py:304
  220.9 1.7 shard_map.74
  (44 shorter events, 8.5 us)
Async XLA Ops:
  3.3 2.0 copy-start.1
  5.3 6.4 %copy-start.2 = (bf16[24,4096]{1,0:T(8,128)(2,1)S(1)}, bf16[24,4096]{1,0:T(8,128)(2,1)}, u32[]{:S(2)}) copy-start(bf16[24,4096]{1,0:T(8,128)(2,1)} %tokens_ref.1) | copy-start | bytes 589828
  5.3 6.4 %copy-start.4 = (s32[32]{0:T(128)S(1)}, s32[32]{0:T(128)}, u32[]{:S(2)}) copy-start(s32[32]{0:T(128)} %counts_ref.5) | copy-start | bytes 388
  5.3 25.4 %copy-start.5 = (bf16[144,64]{0,1:T(8,128)(2,1)S(1)}, bf16[144,64]{0,1:T(8,128)(2,1)}, u32[]{:S(2)}) copy-start(bf16[144,64]{0,1:T(8,128)(2,1)} %param.8) | copy-start | bytes 55300
  5.3 81.5 %copy-start.3 = (bf16[64,448]{1,0:T(8,128)(2,1)S(1)}, bf16[64,448]{1,0:T(8,128)(2,1)}, u32[]{:S(2)}) copy-start(bf16[64,448]{1,0:T(8,128)(2,1)} %refs_4_.1) | copy-start | bytes 172036
  5.3 98.9 %all-to-all-start = ((bf16[8,144,1792]{2,1,0:T(8,128)(2,1)}), bf16[8,144,1792]{2,1,0:T(8,128)(2,1)}, u32[]{:S(2)}, u32[]{:S(2)}) async-start(bf16[8,144,1792]{2,1,0:T(8,128)(2,1)} %copy-done.1), calls=%async_computation | async-start | bytes 8257536 | tf_op jit(solution)/shard_map/all_to_all | solution.py:310
  12.7 39.8 %collective-permute-start = (bf16[24,1152]{1,0:T(8,128)(2,1)S(1)}, bf16[24,1152]{1,0:T(8,128)(2,1)S(1)}, u32[]{:S(2)}, u32[]{:S(2)}) collective-permute-start(bf16[24,1152]{1,0:T(8,128)(2,1)S(1)} %get-tuple-element.45), channel_id=1, source_target_pairs={{0,128},{16,144},{32,160},{48,176},{64,192},{80,208},{96,224},{112... | collective-permute-start | bytes 165896 | tf_op jit(solution)/shard_map/ppermute | solution.py:292
  17.6 36.1 %collective-permute-start.1 = (bf16[24,1152]{1,0:T(8,128)(2,1)S(1)}, bf16[24,1152]{1,0:T(8,128)(2,1)S(1)}, u32[]{:S(2)}, u32[]{:S(2)}) collective-permute-start(bf16[24,1152]{1,0:T(8,128)(2,1)S(1)} %get-tuple-element.44), channel_id=1, source_target_pairs={{0,256},{16,272},{32,288},{48,304},{64,320},{80,336},{96,352},{112... | collective-permute-start | bytes 165896 | tf_op jit(solution)/shard_map/ppermute | solution.py:292
  26.4 28.5 %collective-permute-start.2 = (bf16[24,1152]{1,0:T(8,128)(2,1)S(1)}, bf16[24,1152]{1,0:T(8,128)(2,1)S(1)}, u32[]{:S(2)}, u32[]{:S(2)}) collective-permute-start(bf16[24,1152]{1,0:T(8,128)(2,1)S(1)} %get-tuple-element.43), channel_id=1, source_target_pairs={{0,384},{16,400},{32,416},{48,432},{64,448},{80,464},{96,480},{112... | collective-permute-start | bytes 165896 | tf_op jit(solution)/shard_map/ppermute | solution.py:292
  55.0 21.2 %collective-permute-start.3 = (bf16[104,1152]{1,0:T(8,128)(2,1)S(1)}, bf16[104,1152]{1,0:T(8,128)(2,1)S(1)}, u32[]{:S(2)}, u32[]{:S(2)}) collective-permute-start(bf16[104,1152]{1,0:T(8,128)(2,1)S(1)} %shard_map.66), channel_id=1, source_target_pairs={{0,64},{16,80},{32,96},{48,112},{64,0},{80,16},{96,32},{112,48},{1... | collective-permute-start | bytes 718856 | tf_op jit(solution)/shard_map/ppermute | solution.py:325
  76.2 27.7 %collective-permute-start.4 = (bf16[2,104,1152]{2,1,0:T(8,128)(2,1)S(1)}, bf16[2,104,1152]{2,1,0:T(8,128)(2,1)S(1)}, u32[]{:S(2)}, u32[]{:S(2)}) collective-permute-start(bf16[2,104,1152]{2,1,0:T(8,128)(2,1)S(1)} %pad_maximum_fusion.refs_0_), channel_id=1, source_target_pairs={{0,16},{16,32},{32,48},{48,0},{64,80},{80,96},{96,112},{112,64},{1... | collective-permute-start | bytes 1437704 | tf_op jit(solution)/shard_map/ppermute | solution.py:300
  79.4 24.5 %collective-permute-start.5 = (bf16[2,104,1152]{2,1,0:T(8,128)(2,1)S(1)}, bf16[2,104,1152]{2,1,0:T(8,128)(2,1)S(1)}, u32[]{:S(2)}, u32[]{:S(2)}) collective-permute-start(bf16[2,104,1152]{2,1,0:T(8,128)(2,1)S(1)} %pad_maximum_fusion.refs_0_), channel_id=1, source_target_pairs={{0,32},{16,48},{32,0},{48,16},{64,96},{80,112},{96,64},{112,80},{1... | collective-permute-start | bytes 1437704 | tf_op jit(solution)/shard_map/ppermute | solution.py:300
  84.1 19.9 %collective-permute-start.6 = (bf16[2,104,1152]{2,1,0:T(8,128)(2,1)S(1)}, bf16[2,104,1152]{2,1,0:T(8,128)(2,1)S(1)}, u32[]{:S(2)}, u32[]{:S(2)}) collective-permute-start(bf16[2,104,1152]{2,1,0:T(8,128)(2,1)S(1)} %pad_maximum_fusion.refs_0_), channel_id=1, source_target_pairs={{0,48},{16,0},{32,16},{48,32},{64,112},{80,64},{96,80},{112,96},{1... | collective-permute-start | bytes 1437704 | tf_op jit(solution)/shard_map/ppermute | solution.py:300
  86.8 10.7 %collective-permute-start.7 = (bf16[64,448]{1,0:T(8,128)(2,1)S(1)}, bf16[64,448]{1,0:T(8,128)(2,1)S(1)}, u32[]{:S(2)}, u32[]{:S(2)}) collective-permute-start(bf16[64,448]{1,0:T(8,128)(2,1)S(1)} %copy-done.3), channel_id=1, source_target_pairs={{0,128},{16,144},{32,160},{48,176},{64,192},{80,208},{96,224},{112... | collective-permute-start | bytes 172040 | tf_op jit(solution)/shard_map/ppermute | solution.py:292
  91.3 10.8 %collective-permute-start.8 = (bf16[64,448]{1,0:T(8,128)(2,1)S(1)}, bf16[64,448]{1,0:T(8,128)(2,1)S(1)}, u32[]{:S(2)}, u32[]{:S(2)}) collective-permute-start(bf16[64,448]{1,0:T(8,128)(2,1)S(1)} %copy-done.3), channel_id=1, source_target_pairs={{0,256},{16,272},{32,288},{48,304},{64,320},{80,336},{96,352},{112... | collective-permute-start | bytes 172040 | tf_op jit(solution)/shard_map/ppermute | solution.py:292
  97.6 6.4 %collective-permute-start.9 = (bf16[64,448]{1,0:T(8,128)(2,1)S(1)}, bf16[64,448]{1,0:T(8,128)(2,1)S(1)}, u32[]{:S(2)}, u32[]{:S(2)}) collective-permute-start(bf16[64,448]{1,0:T(8,128)(2,1)S(1)} %copy-done.3), channel_id=1, source_target_pairs={{0,384},{16,400},{32,416},{48,432},{64,448},{80,464},{96,480},{112... | collective-permute-start | bytes 172040 | tf_op jit(solution)/shard_map/ppermute | solution.py:292
  114.0 18.6 %copy-start = (f32[4,768,256]{2,1,0:T(8,128)S(1)}, f32[4,768,256]{2,1,0:T(8,128)}, u32[]{:S(2)}) copy-start(f32[4,768,256]{2,1,0:T(8,128)} %get-tuple-element.29.up_own_ref.down_own_ref.refs_0_) | copy-start | bytes 9437188
  114.0 18.5 %collective-permute-start.10 = (bf16[768,256]{1,0:T(8,128)(2,1)S(1)}, bf16[768,256]{1,0:T(8,128)(2,1)S(1)}, u32[]{:S(2)}, u32[]{:S(2)}) collective-permute-start(bf16[768,256]{1,0:T(8,128)(2,1)S(1)} %get-tuple-element.30), channel_id=1, source_target_pairs={{0,128},{16,144},{32,160},{48,176},{64,192},{80,208},{96,224},{112... | collective-permute-start | bytes 1179656 | tf_op jit(solution)/shard_map/ppermute | solution.py:304
  121.3 11.3 %collective-permute-start.11 = (bf16[768,256]{1,0:T(8,128)(2,1)S(1)}, bf16[768,256]{1,0:T(8,128)(2,1)S(1)}, u32[]{:S(2)}, u32[]{:S(2)}) collective-permute-start(bf16[768,256]{1,0:T(8,128)(2,1)S(1)} %get-tuple-element.31), channel_id=1, source_target_pairs={{384,256},{400,272},{416,288},{432,304},{448,320},{464,336},{480,3... | collective-permute-start | bytes 1179656 | tf_op jit(solution)/shard_map/ppermute | solution.py:304
  130.5 5.1 %collective-permute-start.16 = (bf16[400,384]{1,0:T(8,128)(2,1)S(1)}, bf16[400,384]{1,0:T(8,128)(2,1)S(1)}, u32[]{:S(2)}, u32[]{:S(2)}) collective-permute-start(bf16[400,384]{1,0:T(8,128)(2,1)S(1)} %get-tuple-element.37), channel_id=1, source_target_pairs={{0,128},{16,144},{32,160},{48,176},{64,192},{80,208},{96,224},{112... | collective-permute-start | bytes 921608 | tf_op jit(solution)/shard_map/ppermute | solution.py:304
  131.8 3.8 %collective-permute-start.17 = (bf16[400,384]{1,0:T(8,128)(2,1)S(1)}, bf16[400,384]{1,0:T(8,128)(2,1)S(1)}, u32[]{:S(2)}, u32[]{:S(2)}) collective-permute-start(bf16[400,384]{1,0:T(8,128)(2,1)S(1)} %get-tuple-element.38), channel_id=1, source_target_pairs={{384,256},{400,272},{416,288},{432,304},{448,320},{464,336},{480,3... | collective-permute-start | bytes 921608 | tf_op jit(solution)/shard_map/ppermute | solution.py:304
  132.7 30.4 %collective-permute-start.12 = (bf16[768,256]{1,0:T(8,128)(2,1)S(1)}, bf16[768,256]{1,0:T(8,128)(2,1)S(1)}, u32[]{:S(2)}, u32[]{:S(2)}) collective-permute-start(bf16[768,256]{1,0:T(8,128)(2,1)S(1)} %get-tuple-element.32), channel_id=1, source_target_pairs={{0,128},{16,144},{32,160},{48,176},{64,192},{80,208},{96,224},{112... | collective-permute-start | bytes 1179656 | tf_op jit(solution)/shard_map/ppermute | solution.py:304
  134.0 29.0 %collective-permute-start.13 = (bf16[768,256]{1,0:T(8,128)(2,1)S(1)}, bf16[768,256]{1,0:T(8,128)(2,1)S(1)}, u32[]{:S(2)}, u32[]{:S(2)}) collective-permute-start(bf16[768,256]{1,0:T(8,128)(2,1)S(1)} %get-tuple-element.33), channel_id=1, source_target_pairs={{256,128},{272,144},{288,160},{304,176},{320,192},{336,208},{352,2... | collective-permute-start | bytes 1179656 | tf_op jit(solution)/shard_map/ppermute | solution.py:304
  136.0 51.6 %collective-permute-start.18 = (bf16[400,384]{1,0:T(8,128)(2,1)S(1)}, bf16[400,384]{1,0:T(8,128)(2,1)S(1)}, u32[]{:S(2)}, u32[]{:S(2)}) collective-permute-start(bf16[400,384]{1,0:T(8,128)(2,1)S(1)} %get-tuple-element.39), channel_id=1, source_target_pairs={{0,128},{16,144},{32,160},{48,176},{64,192},{80,208},{96,224},{112... | collective-permute-start | bytes 921608 | tf_op jit(solution)/shard_map/ppermute | solution.py:304
  162.4 25.2 %collective-permute-start.19 = (bf16[400,384]{1,0:T(8,128)(2,1)S(1)}, bf16[400,384]{1,0:T(8,128)(2,1)S(1)}, u32[]{:S(2)}, u32[]{:S(2)}) collective-permute-start(bf16[400,384]{1,0:T(8,128)(2,1)S(1)} %get-tuple-element.40), channel_id=1, source_target_pairs={{256,128},{272,144},{288,160},{304,176},{320,192},{336,208},{352,2... | collective-permute-start | bytes 921608 | tf_op jit(solution)/shard_map/ppermute | solution.py:304
  163.3 34.0 %copy-start.6 = (bf16[448]{0:T(512)(128)(2,1)S(1)}, bf16[448]{0:T(512)(128)(2,1)}, u32[]{:S(2)}) copy-start(bf16[448]{0:T(512)(128)(2,1)} %param.10) | copy-start | bytes 2692
  163.3 57.6 %collective-permute-start.14 = (bf16[768,256]{1,0:T(8,128)(2,1)S(1)}, bf16[768,256]{1,0:T(8,128)(2,1)S(1)}, u32[]{:S(2)}, u32[]{:S(2)}) collective-permute-start(bf16[768,256]{1,0:T(8,128)(2,1)S(1)} %get-tuple-element.34), channel_id=1, source_target_pairs={{0,128},{16,144},{32,160},{48,176},{64,192},{80,208},{96,224},{112... | collective-permute-start | bytes 1179656 | tf_op jit(solution)/shard_map/ppermute | solution.py:304
  186.3 34.6 %collective-permute-start.15 = (bf16[768,256]{1,0:T(8,128)(2,1)S(1)}, bf16[768,256]{1,0:T(8,128)(2,1)S(1)}, u32[]{:S(2)}, u32[]{:S(2)}) collective-permute-start(bf16[768,256]{1,0:T(8,128)(2,1)S(1)} %get-tuple-element.35), channel_id=1, source_target_pairs={{128,0},{144,16},{160,32},{176,48},{192,64},{208,80},{224,96},{240... | collective-permute-start | bytes 1179656 | tf_op jit(solution)/shard_map/ppermute | solution.py:304
  188.0 12.4 %collective-permute-start.20 = (bf16[400,384]{1,0:T(8,128)(2,1)S(1)}, bf16[400,384]{1,0:T(8,128)(2,1)S(1)}, u32[]{:S(2)}, u32[]{:S(2)}) collective-permute-start(bf16[400,384]{1,0:T(8,128)(2,1)S(1)} %get-tuple-element.41), channel_id=1, source_target_pairs={{0,128},{16,144},{32,160},{48,176},{64,192},{80,208},{96,224},{112... | collective-permute-start | bytes 921608 | tf_op jit(solution)/shard_map/ppermute | solution.py:304
  195.9 24.9 %collective-permute-start.21 = (bf16[400,384]{1,0:T(8,128)(2,1)S(1)}, bf16[400,384]{1,0:T(8,128)(2,1)S(1)}, u32[]{:S(2)}, u32[]{:S(2)}) collective-permute-start(bf16[400,384]{1,0:T(8,128)(2,1)S(1)} %get-tuple-element.42), channel_id=1, source_target_pairs={{128,0},{144,16},{160,32},{176,48},{192,64},{208,80},{224,96},{240... | collective-permute-start | bytes 921608 | tf_op jit(solution)/shard_map/ppermute | solution.py:304

commit v3 on v2

v3 whole, which is shorter than its diff:
```python
import functools

import jax
import jax.numpy as jnp
from jax import lax
from jax.experimental import pallas as pl
from jax.experimental.pallas import tpu as pltpu
from jax.sharding import PartitionSpec as P

AXIS = "fsdp"
GROUP = 8
PAIRS = 4
SLOTS = 144
RANK = 64
UNITS = 448
KEYS = GROUP * SLOTS
TOKENS = 768
OWN_TOKENS = 24
FEATURES = 4096
WINDOW = 384
FRONT = 256
HALF = TOKENS // 2
LANES = 2 * (UNITS - FRONT)
TAIL = 16
VMEM_LIMIT = 48 * 1024 * 1024

NEAR = [[GROUP * p + i for i in range(GROUP)] for p in range(PAIRS)]
FAR = [[GROUP * p + i for p in range(PAIRS)] for i in range(GROUP)]


def whole(memory_space=pltpu.VMEM):
    return pl.BlockSpec(memory_space=memory_space)


def params():
    return pltpu.CompilerParams(vmem_limit_bytes=VMEM_LIMIT)


def window_kernel(place_ref, counts_ref, tokens_ref, out_ref, padded, lined):
    padded[:, FEATURES:] = jnp.zeros((OWN_TOKENS, WINDOW), jnp.float32)
    padded[:, :FEATURES] = tokens_ref[...].astype(jnp.float32)
    starts = [jnp.int32(0)]
    for f in range(GROUP * PAIRS - 1):
        starts.append(starts[-1] + counts_ref[f])
    pair = place_ref[0] // GROUP
    lane = lax.broadcasted_iota(jnp.int32, (OWN_TOKENS, WINDOW), 1)
    for target in range(PAIRS):
        for i in range(GROUP):
            start = starts[GROUP * target + i]
            base = pl.multiple_of((start // 128) * 128, 128)
            place = SLOTS * i
            low = (place // 128) * 128
            rest = place - low
            shift = lax.rem(rest - (start - base) + WINDOW, WINDOW)
            moved = pltpu.roll(padded[:, pl.ds(base, WINDOW)], shift, 1)
            keep = (lane >= rest) & (lane < rest + SLOTS)
            lined[:, low : low + WINDOW] = jnp.where(keep, moved, lined[:, low : low + WINDOW])
        out_ref[lax.rem(target - pair + PAIRS, PAIRS)] = lined[:, :KEYS].astype(jnp.bfloat16)


def own_windows(place, counts, tokens):
    return pl.pallas_call(
        window_kernel,
        out_shape=jax.ShapeDtypeStruct((PAIRS, OWN_TOKENS, KEYS), jnp.bfloat16),
        in_specs=[whole(pltpu.SMEM), whole(pltpu.SMEM), whole()],
        out_specs=whole(),
        scratch_shapes=[
            pltpu.VMEM((OWN_TOKENS, FEATURES + WINDOW), jnp.float32),
            pltpu.VMEM((OWN_TOKENS, KEYS + 128), jnp.float32),
        ],
        compiler_params=params(),
    )(place, counts, tokens)


def collect_kernel(place_ref, own_ref, one_ref, two_ref, three_ref, down_ref, out_ref, rows):
    pair = place_ref[0] // GROUP
    blocks = (own_ref[0], one_ref[...], two_ref[...], three_ref[...])
    for step, block in enumerate(blocks):
        origin = lax.rem(pair - step + PAIRS, PAIRS)
        rows[pl.ds(pl.multiple_of(origin * OWN_TOKENS, 8), OWN_TOKENS), :] = block.astype(jnp.float32)
    down = down_ref[...].astype(jnp.float32)
    rows[PAIRS * OWN_TOKENS :, :] = jnp.concatenate(
        [down[8 * g : 8 * g + 8, :] for g in range(SLOTS // 8)], axis=1
    )
    out_ref[...] = rows[...].astype(jnp.bfloat16)


def collect(place, own, one, two, three, down):
    height = PAIRS * OWN_TOKENS + 8
    return pl.pallas_call(
        collect_kernel,
        out_shape=jax.ShapeDtypeStruct((height, KEYS), jnp.bfloat16),
        in_specs=[whole(pltpu.SMEM)] + [whole()] * 5,
        out_specs=whole(),
        scratch_shapes=[pltpu.VMEM((height, KEYS), jnp.float32)],
        compiler_params=params(),
    )(place, own, one, two, three, down)


def offset_of(k, pair):
    last = pair == PAIRS - 1
    return jnp.where(k == 0, jnp.where(last, 1, 3), jnp.where(k == 1, 2, jnp.where(k == 2, jnp.where(last, 3, 1), 0)))


def pack_kernel(place_ref, rows_ref, *out_refs):
    step = pl.program_id(0)
    for k in range(PAIRS):

        @pl.when(step == k)
        def _():
            at = UNITS * (k % 2)
            for i in range(GROUP):
                out_refs[k // 2][i, :, at : at + UNITS] = rows_ref[:, UNITS * i : UNITS * (i + 1)]


def pack(place, rows):
    def block(k, place_ref):
        pair = place_ref[0] // GROUP
        return 0, lax.rem(pair + offset_of(k, pair), PAIRS)

    return pl.pallas_call(
        pack_kernel,
        grid_spec=pltpu.PrefetchScalarGridSpec(
            num_scalar_prefetch=1,
            grid=(PAIRS,),
            in_specs=[pl.BlockSpec((SLOTS, GROUP * UNITS), block)],
            out_specs=[pl.BlockSpec((GROUP, SLOTS, 2 * UNITS), lambda k, _: (0, 0, 0))] * 2,
        ),
        out_shape=[jax.ShapeDtypeStruct((GROUP, SLOTS, 2 * UNITS), jnp.bfloat16)] * 2,
        compiler_params=params(),
    )(place, rows)


def assemble_kernel(place_ref, *refs):
    block_refs, up_refs = refs[:8], refs[8:12]
    tokens_ref, down_ref, up_ref = refs[12:]
    place = place_ref[0]
    pair, side, x = place // GROUP, (place // 4) % 2, place % 4
    for far in range(2):
        for step in range(4):
            block_ref = block_refs[4 * far + step]
            origin = 4 * lax.rem(side + far, 2) + lax.rem(x - step + 4, 4)
            tokens_ref[pl.ds(pl.multiple_of(origin * 96, 96), 96), :] = block_ref[0:96, :]
            folded = block_ref[96:104, :].astype(jnp.float32)
            down_ref[origin] = jnp.concatenate(
                [folded[:, RANK * g : RANK * g + RANK] for g in range(SLOTS // 8)], axis=0
            ).astype(jnp.bfloat16)
    for step, ref in enumerate(up_refs):
        up_ref[lax.rem(pair - step + PAIRS, PAIRS)] = ref[...]


def assemble(place, blocks, ups):
    return pl.pallas_call(
        assemble_kernel,
        out_shape=[
            jax.ShapeDtypeStruct((TOKENS, KEYS), jnp.bfloat16),
            jax.ShapeDtypeStruct((GROUP, SLOTS, RANK), jnp.bfloat16),
            jax.ShapeDtypeStruct((PAIRS, RANK, UNITS), jnp.bfloat16),
        ],
        in_specs=[whole(pltpu.SMEM)] + [whole()] * 12,
        out_specs=[whole()] * 3,
        compiler_params=params(),
    )(place, *blocks, *ups)


def split(total):
    pieces = [total[:, : UNITS // 2], total[:, UNITS // 2 :]]
    rows = []
    for piece in pieces:
        high = piece.astype(jnp.bfloat16).astype(jnp.float32)
        rows += [high, piece - high]
    rows.append(jnp.zeros((TAIL - 4, UNITS // 2), jnp.float32))
    rows = jnp.concatenate(rows, axis=0)
    return jnp.concatenate([rows, jnp.zeros((TAIL, LANES - UNITS // 2), jnp.float32)], axis=1).astype(jnp.bfloat16)


def joined(tail):
    rows = tail.astype(jnp.float32)[:, : UNITS // 2]
    return jnp.concatenate([rows[0:1] + rows[1:2], rows[2:3] + rows[3:4]], axis=1)


def pieces(product):
    back = product[:, FRONT:]
    return product[:, :FRONT], jnp.concatenate([back[:HALF], back[HALF:]], axis=1)


def partial_kernel(stage, place_ref, counts_ref, rows_ref, tokens_ref, down_ref, up_ref, *refs):
    squares_ref, front_ref, back_ref, merged = refs[0], refs[1], refs[2], refs[-1]
    pair = place_ref[0] // GROUP
    row = lax.broadcasted_iota(jnp.int32, (SLOTS, UNITS), 0)
    for k in range(2):
        up = up_ref[lax.rem(pair + offset_of(2 * stage + k, pair), PAIRS)]
        total = jnp.zeros((1, UNITS), jnp.float32)
        for i in range(GROUP):
            low = jnp.dot(down_ref[i], up, preferred_element_type=jnp.float32)
            base = rows_ref[i, :, UNITS * k : UNITS * (k + 1)].astype(jnp.float32)
            value = jnp.where(row < counts_ref[GROUP * pair + i], base + low, 0.0)
            total = total + jnp.sum(value * value, axis=0, keepdims=True)
            merged[SLOTS * i : SLOTS * i + SLOTS, :] = value.astype(jnp.bfloat16)
        product = jnp.dot(tokens_ref[...], merged[...], preferred_element_type=jnp.float32)
        squares_ref[k] = total
        front, back = pieces(product)
        front_ref[k] = front
        back_ref[k] = back
        if stage == 0 and k == 0:
            refs[3][...] = front.astype(jnp.bfloat16)
            refs[4][:HALF] = back.astype(jnp.bfloat16)
            refs[4][HALF:] = split(total)


def partial_products(stage, place, counts, rows, tokens, down, up):
    out_shape = [
        jax.ShapeDtypeStruct((2, 1, UNITS), jnp.float32),
        jax.ShapeDtypeStruct((2, TOKENS, FRONT), jnp.float32),
        jax.ShapeDtypeStruct((2, HALF, LANES), jnp.float32),
    ]
    if stage == 0:
        out_shape += [
            jax.ShapeDtypeStruct((TOKENS, FRONT), jnp.bfloat16),
            jax.ShapeDtypeStruct((HALF + TAIL, LANES), jnp.bfloat16),
        ]
    return pl.pallas_call(
        functools.partial(partial_kernel, stage),
        out_shape=out_shape,
        in_specs=[whole(pltpu.SMEM), whole(pltpu.SMEM)] + [whole()] * 4,
        out_specs=[whole()] * len(out_shape),
        scratch_shapes=[pltpu.VMEM((KEYS, UNITS), jnp.bfloat16)],
        compiler_params=params(),
    )(place, counts, rows, tokens, down, up)


def forward_kernel(step, place_ref, up_got_ref, down_got_ref, early_ref, late_ref, early_squares_ref, late_squares_ref, up_ref, down_ref):
    height = early_ref.shape[1]

    def send(got, own, squares, out):
        out[:height] = (got[:height].astype(jnp.float32) + own).astype(jnp.bfloat16)
        if out.shape[0] > height:
            out[height:] = split(joined(got[height:]) + squares)

    if step == 2:
        send(up_got_ref, early_ref[0], early_squares_ref[0], up_ref)
        send(down_got_ref, early_ref[0], early_squares_ref[0], down_ref)
    else:
        last = place_ref[0] // GROUP == PAIRS - 1
        send(up_got_ref, late_ref[0], late_squares_ref[0], up_ref)
        send(
            down_got_ref,
            jnp.where(last, late_ref[0], early_ref[0]),
            jnp.where(last, late_squares_ref[0], early_squares_ref[0]),
            down_ref,
        )


def forward(step, place, got, early, late, early_squares, late_squares):
    def own(array):
        return pl.BlockSpec((1,) + array.shape[1:], lambda _: (1 if step == 2 else 0, 0, 0))

    moved = pl.BlockSpec(got[0].shape, lambda _: (0, 0))
    return pl.pallas_call(
        functools.partial(forward_kernel, step),
        grid=(1,),
        out_shape=[jax.ShapeDtypeStruct(got[0].shape, jnp.bfloat16)] * 2,
        in_specs=[whole(pltpu.SMEM), moved, moved, own(early), own(late), own(early_squares), own(late_squares)],
        out_specs=[moved, moved],
        compiler_params=params(),
    )(place, *got, early, late, early_squares, late_squares)


def finish_kernel(squares_ref, scale_ref, *refs):
    out_ref = refs[-1]
    own, above, below = refs[0:3]
    front = own[0] + above[...].astype(jnp.float32) + below[...].astype(jnp.float32)
    own, above, below = refs[3:6]
    back = own[0] + above[:HALF].astype(jnp.float32) + below[:HALF].astype(jnp.float32)
    width = back.shape[1] // 2
    back = jnp.concatenate([back[:, :width], back[:, width:]], axis=0)
    total = squares_ref[0] + joined(above[HALF:]) + joined(below[HALF:])
    factor = scale_ref[...].astype(jnp.float32) / jnp.sqrt(total + 1e-06)
    result = jnp.concatenate([front, back], axis=1)
    result = jnp.where(factor == 0.0, 0.0, result * factor)
    out_ref[...] = jnp.concatenate(
        [
            result[OWN_TOKENS * (PAIRS * i + q) : OWN_TOKENS * (PAIRS * i + q + 1), :]
            for q in range(PAIRS)
            for i in range(GROUP)
        ],
        axis=0,
    ).astype(jnp.bfloat16)


def finish(squares, scale, front, back, sums):
    def at(index, *shape):
        return pl.BlockSpec(shape, lambda _: (index,) + (0,) * (len(shape) - 1))

    def same(array):
        return pl.BlockSpec(array.shape, lambda _: (0, 0))

    return pl.pallas_call(
        finish_kernel,
        grid=(1,),
        out_shape=jax.ShapeDtypeStruct((TOKENS, UNITS), jnp.bfloat16),
        in_specs=[at(1, 1, 1, UNITS), same(scale)]
        + [at(1, 1, TOKENS, FRONT), same(sums[0]), same(sums[1])]
        + [at(1, 1, HALF, LANES), same(sums[2]), same(sums[3])],
        out_specs=pl.BlockSpec((TOKENS, UNITS), lambda _: (0, 0)),
        compiler_params=params(),
    )(squares, scale, front, sums[0], sums[1], back, sums[2], sums[3])


def to_pair(array, step):
    return lax.ppermute(
        array,
        AXIS,
        [(GROUP * p + i, GROUP * ((p + step) % PAIRS) + i) for p in range(PAIRS) for i in range(GROUP)],
    )


def along_x(array, step):
    return lax.ppermute(array, AXIS, [(4 * z + x, 4 * z + (x + step) % 4) for z in range(8) for x in range(4)])


def hop(array, froms, way):
    return lax.ppermute(
        array, AXIS, [(GROUP * p + i, GROUP * (p + way) + i) for p in froms for i in range(GROUP)]
    )


def hops(sends, step):
    return hop(sends[0], range(step), 1), hop(sends[1], range(PAIRS - step, PAIRS), -1)


def exchange(send):
    return lax.all_to_all(send, AXIS, 0, 0, axis_index_groups=NEAR, tiled=True)


def body(tokens, frozen_slot_rows, adapter_down_factor, adapter_up_factor, magnitude, counts):
    place = lax.axis_index(AXIS).astype(jnp.int32).reshape(1)
    own = own_windows(place, counts, tokens)
    moved = [to_pair(own[step], step) for step in range(1, PAIRS)]
    ups = [adapter_up_factor] + [to_pair(adapter_up_factor, step) for step in range(1, PAIRS)]
    frozen_slot_rows, moved[0] = lax.optimization_barrier((frozen_slot_rows, moved[0]))
    sends = list(pack(place, frozen_slot_rows))
    column = collect(place, own, *moved, adapter_down_factor)
    other = lax.ppermute(column, AXIS, [(f, f ^ 4) for f in range(GROUP * PAIRS)])
    blocks = [column] + [along_x(column, step) for step in range(1, 4)]
    blocks += [other] + [along_x(other, step) for step in range(1, 4)]
    sends[0], blocks[5] = lax.optimization_barrier((sends[0], blocks[5]))
    rows = exchange(sends[0])
    all_tokens, down, up = assemble(place, blocks, ups)
    early_squares, early_front, early_back, first_front, first_back = partial_products(
        0, place, counts, rows, all_tokens, down, up
    )
    sends[1], early_front = lax.optimization_barrier((sends[1], early_front))
    a, b = hops((first_front, first_front), 1), hops((first_back, first_back), 1)
    rows = exchange(sends[1])
    a = hops(forward(2, place, a, early_front, early_front, early_squares, early_squares), 2)
    b = hops(forward(2, place, b, early_back, early_back, early_squares, early_squares), 2)
    rows, *a = lax.optimization_barrier((rows, *a))
    squares, front, back = partial_products(1, place, counts, rows, all_tokens, down, up)
    a = hops(forward(3, place, a, early_front, front, early_squares, squares), 3)
    b = hops(forward(3, place, b, early_back, back, early_squares, squares), 3)
    return finish(squares, magnitude.reshape(1, UNITS), front, back, [*a, *b])


def solution(mesh):
    in_specs = (
        P(("dp", "fsdp"), None),
        P(("dp", "fsdp"), None),
        P(("dp", "fsdp"), None),
        P("dp", "fsdp"),
        P(("dp", "fsdp")),
        P("dp"),
    )
    out_specs = P("dp", "fsdp")
    return jax.shard_map(body, mesh=mesh, in_specs=in_specs, out_specs=out_specs, check_vma=False)
```

time: 226 us -> 210 us (0.929)
  the two profiles are of different devices: /device:TPU:1 before, /device:TPU:46 now
where the time goes in v3:
time: 210 us; the launch traced here: 209 us
  starting transfers between devices  117 us (56%)
  waiting for transfers between devices  60.2 us (29%)
  Pallas kernels  19.4 us (9%)
  local copies, waits for them, and re-layouts  12.1 us (6%)
    ppermute x12, starting transfers between devices, hop(): lax.ppermute(array, AXIS, [(GROUP * p + i, GROUP * (p + way) + i) for p i...  51.8 us
    ppermute x12, waiting for transfers between devices, hop(): lax.ppermute(array, AXIS, [(GROUP * p + i, GROUP * (p + way) + i) for p i...  36.2 us
    ppermute x6, starting transfers between devices, to_pair(): lax.ppermute(array, AXIS, [(GROUP * p + i, GROUP * ((p + step) % PAIRS) +...  32.4 us
    ppermute x6, starting transfers between devices, along_x(): lax.ppermute(array, AXIS, [(4 * z + x, 4 * z + (x + step) % 4) for z in r...  18.9 us
    all_to_all x2, starting transfers between devices, exchange(): return lax.all_to_all(send, AXIS, 0, 0, axis_index_groups=NEAR, tiled=True)  11.9 us
    unnamed x31, local copies, waits for them, and re-layouts  11 us
    ppermute x6, waiting for transfers between devices, to_pair(): lax.ppermute(array, AXIS, [(GROUP * p + i, GROUP * ((p + step) % PAIRS) +...  9.99 us
    pallas_call x2, Pallas kernels, partial_products(): pl.pallas_call(functools.partial(partial_kernel, stage), out_shape=out_sh...  9.95 us
  transfers between devices with their start and end apart: 27, of which 10 were waited for; matrix products, arithmetic and copies ran while one was open for 0% of the time, Pallas kernels for 6%

profile of v3, /device:TPU:46, one launch (start us, length us, event | category | flops | bytes accessed | tf_op | source)
XLA Modules:
  0.0 209.3 jit_solution(628939808272623182)
XLA Ops:
  2.6 5.2 %collective-permute-start = (bf16[24,1152]{1,0:T(8,128)(2,1)S(1)}, bf16[24,1152]{1,0:T(8,128)(2,1)S(1)}, u32[]{:S(2)}, u32[]{:S(2)}) collective-permute-start(bf16[24,1152]{1,0:T(8,128)(2,1)S(1)} %get-tuple-element.67), channel_id=1, source_target_pairs={{0,128},{16,144},{32,160},{48,176},{64,192},{80,208},{96,224},{112... | collective-permute-start | bytes 165896 | tf_op jit(solution)/shard_map/ppermute | solution.py:311
  7.8 9.1 %collective-permute-start.1 = (bf16[24,1152]{1,0:T(8,128)(2,1)S(1)}, bf16[24,1152]{1,0:T(8,128)(2,1)S(1)}, u32[]{:S(2)}, u32[]{:S(2)}) collective-permute-start(bf16[24,1152]{1,0:T(8,128)(2,1)S(1)} %get-tuple-element.66), channel_id=1, source_target_pairs={{0,256},{16,272},{32,288},{48,304},{64,320},{80,336},{96,352},{112... | collective-permute-start | bytes 165896 | tf_op jit(solution)/shard_map/ppermute | solution.py:311
  16.9 4.6 %collective-permute-start.2 = (bf16[24,1152]{1,0:T(8,128)(2,1)S(1)}, bf16[24,1152]{1,0:T(8,128)(2,1)S(1)}, u32[]{:S(2)}, u32[]{:S(2)}) collective-permute-start(bf16[24,1152]{1,0:T(8,128)(2,1)S(1)} %get-tuple-element.65), channel_id=1, source_target_pairs={{0,384},{16,400},{32,416},{48,432},{64,448},{80,464},{96,480},{112... | collective-permute-start | bytes 165896 | tf_op jit(solution)/shard_map/ppermute | solution.py:311
  22.3 1.6 collective-permute-done.2.three_ref
  24.1 2.0 collective-permute-start.3
  26.0 7.2 %collective-permute-done.3.refs_4_ = bf16[104,1152]{1,0:T(8,128)(2,1)S(1)} collective-permute-done((bf16[104,1152]{1,0:T(8,128)(2,1)S(1)}, bf16[104,1152]{1,0:T(8,128)(2,1)S(1)}, u32[]{:S(2)}, u32[]{:S(2)}) %collective-permute-start.3) | collective-permute-done | bytes 239648 | tf_op jit(solution)/shard_map/ppermute | solution.py:344
  33.2 2.4 %collective-permute-start.4 = (bf16[104,1152]{1,0:T(8,128)(2,1)S(1)}, bf16[104,1152]{1,0:T(8,128)(2,1)S(1)}, u32[]{:S(2)}, u32[]{:S(2)}) collective-permute-start(bf16[104,1152]{1,0:T(8,128)(2,1)S(1)} %collective-permute-done.3.refs_4_), channel_id=1, source_target_pairs={{0,16},{16,32},{32,48},{48,0},{64,80},{80,96},{96,112},{112,64},{1... | collective-permute-start | bytes 718856 | tf_op jit(solution)/shard_map/ppermute | solution.py:319
  35.6 4.7 %shard_map.65 = (bf16[8,144,896]{2,1,0:T(8,128)(2,1)}, bf16[8,144,896]{2,1,0:T(8,128)(2,1)S(1)}) custom-call(s32[1]{0:T(128)} %bitcast.place_ref, bf16[144,14336]{1,0:T(8,128)(2,1)} %rows_ref), custom_call_target="tpu_custom_call" | custom-call | tf_op jit(solution)/shard_map/pallas_call | solution.py:121
  41.6 6.5 %all-to-all-start = ((bf16[8,144,896]{2,1,0:T(8,128)(2,1)}), bf16[8,144,896]{2,1,0:T(8,128)(2,1)}, u32[]{:S(2)}, u32[]{:S(2)}) async-start(bf16[8,144,896]{2,1,0:T(8,128)(2,1)} %get-tuple-element.39), calls=%async_computation | async-start | bytes 4128768 | tf_op jit(solution)/shard_map/all_to_all | solution.py:333
  48.1 2.6 %collective-permute-start.10 = (bf16[64,448]{1,0:T(8,128)(2,1)S(1)}, bf16[64,448]{1,0:T(8,128)(2,1)S(1)}, u32[]{:S(2)}, u32[]{:S(2)}) collective-permute-start(bf16[64,448]{1,0:T(8,128)(2,1)S(1)} %copy-done.9), channel_id=1, source_target_pairs={{0,128},{16,144},{32,160},{48,176},{64,192},{80,208},{96,224},{112... | collective-permute-start | bytes 172040 | tf_op jit(solution)/shard_map/ppermute | solution.py:311
  50.7 8.4 %collective-permute-start.11 = (bf16[64,448]{1,0:T(8,128)(2,1)S(1)}, bf16[64,448]{1,0:T(8,128)(2,1)S(1)}, u32[]{:S(2)}, u32[]{:S(2)}) collective-permute-start(bf16[64,448]{1,0:T(8,128)(2,1)S(1)} %copy-done.9), channel_id=1, source_target_pairs={{0,256},{16,272},{32,288},{48,304},{64,320},{80,336},{96,352},{112... | collective-permute-start | bytes 172040 | tf_op jit(solution)/shard_map/ppermute | solution.py:311
  59.1 2.6 %collective-permute-start.12 = (bf16[64,448]{1,0:T(8,128)(2,1)S(1)}, bf16[64,448]{1,0:T(8,128)(2,1)S(1)}, u32[]{:S(2)}, u32[]{:S(2)}) collective-permute-start(bf16[64,448]{1,0:T(8,128)(2,1)S(1)} %copy-done.9), channel_id=1, source_target_pairs={{0,384},{16,400},{32,416},{48,432},{64,448},{80,464},{96,480},{112... | collective-permute-start | bytes 172040 | tf_op jit(solution)/shard_map/ppermute | solution.py:311
  61.7 2.5 %collective-permute-start.5 = (bf16[104,1152]{1,0:T(8,128)(2,1)S(1)}, bf16[104,1152]{1,0:T(8,128)(2,1)S(1)}, u32[]{:S(2)}, u32[]{:S(2)}) collective-permute-start(bf16[104,1152]{1,0:T(8,128)(2,1)S(1)} %shard_map.66.refs_0_), channel_id=1, source_target_pairs={{0,16},{16,32},{32,48},{48,0},{64,80},{80,96},{96,112},{112,64},{1... | collective-permute-start | bytes 718856 | tf_op jit(solution)/shard_map/ppermute | solution.py:319
  64.2 4.3 %collective-permute-start.6 = (bf16[104,1152]{1,0:T(8,128)(2,1)S(1)}, bf16[104,1152]{1,0:T(8,128)(2,1)S(1)}, u32[]{:S(2)}, u32[]{:S(2)}) collective-permute-start(bf16[104,1152]{1,0:T(8,128)(2,1)S(1)} %shard_map.66.refs_0_), channel_id=1, source_target_pairs={{0,32},{16,48},{32,0},{48,16},{64,96},{80,112},{96,64},{112,80},{1... | collective-permute-start | bytes 718856 | tf_op jit(solution)/shard_map/ppermute | solution.py:319
  68.5 8.3 %collective-permute-done.10.refs_9_ = bf16[64,448]{1,0:T(8,128)(2,1)S(1)} collective-permute-done((bf16[64,448]{1,0:T(8,128)(2,1)S(1)}, bf16[64,448]{1,0:T(8,128)(2,1)S(1)}, u32[]{:S(2)}, u32[]{:S(2)}) %collective-permute-start.10) | collective-permute-done | bytes 57376 | tf_op jit(solution)/shard_map/ppermute | solution.py:311
  76.8 2.8 %collective-permute-start.7 = (bf16[104,1152]{1,0:T(8,128)(2,1)S(1)}, bf16[104,1152]{1,0:T(8,128)(2,1)S(1)}, u32[]{:S(2)}, u32[]{:S(2)}) collective-permute-start(bf16[104,1152]{1,0:T(8,128)(2,1)S(1)} %shard_map.66.refs_0_), channel_id=1, source_target_pairs={{0,48},{16,0},{32,16},{48,32},{64,112},{80,64},{96,80},{112,96},{1... | collective-permute-start | bytes 718856 | tf_op jit(solution)/shard_map/ppermute | solution.py:319
  79.6 3.3 %collective-permute-start.8 = (bf16[104,1152]{1,0:T(8,128)(2,1)S(1)}, bf16[104,1152]{1,0:T(8,128)(2,1)S(1)}, u32[]{:S(2)}, u32[]{:S(2)}) collective-permute-start(bf16[104,1152]{1,0:T(8,128)(2,1)S(1)} %collective-permute-done.3.refs_4_), channel_id=1, source_target_pairs={{0,32},{16,48},{32,0},{48,16},{64,96},{80,112},{96,64},{112,80},{1... | collective-permute-start | bytes 718856 | tf_op jit(solution)/shard_map/ppermute | solution.py:319
  82.9 3.8 %collective-permute-start.9 = (bf16[104,1152]{1,0:T(8,128)(2,1)S(1)}, bf16[104,1152]{1,0:T(8,128)(2,1)S(1)}, u32[]{:S(2)}, u32[]{:S(2)}) collective-permute-start(bf16[104,1152]{1,0:T(8,128)(2,1)S(1)} %collective-permute-done.3.refs_4_), channel_id=1, source_target_pairs={{0,48},{16,0},{32,16},{48,32},{64,112},{80,64},{96,80},{112,96},{1... | collective-permute-start | bytes 718856 | tf_op jit(solution)/shard_map/ppermute | solution.py:319
  86.7 4.3 %collective-permute-done.7.refs_3_ = bf16[104,1152]{1,0:T(8,128)(2,1)S(1)} collective-permute-done((bf16[104,1152]{1,0:T(8,128)(2,1)S(1)}, bf16[104,1152]{1,0:T(8,128)(2,1)S(1)}, u32[]{:S(2)}, u32[]{:S(2)}) %collective-permute-start.7) | collective-permute-done | bytes 239648 | tf_op jit(solution)/shard_map/ppermute | solution.py:319
  91.0 2.6 %collective-permute-done.9.refs_7_ = bf16[104,1152]{1,0:T(8,128)(2,1)S(1)} collective-permute-done((bf16[104,1152]{1,0:T(8,128)(2,1)S(1)}, bf16[104,1152]{1,0:T(8,128)(2,1)S(1)}, u32[]{:S(2)}, u32[]{:S(2)}) %collective-permute-start.9) | collective-permute-done | bytes 239648 | tf_op jit(solution)/shard_map/ppermute | solution.py:319
  96.6 4.9 %shard_map.68 = (f32[2,1,448]{2,1,0:T(1,128)S(1)}, f32[2,768,256]{2,1,0:T(8,128)S(1)}, f32[2,384,384]{2,1,0:T(8,128)S(1)}, bf16[768,256]{1,0:T(8,128)(2,1)S(1)}, bf16[400,384]{1,0:T(8,128)(2,1)S(1)}) custom-call(s32[1]{0:T(128)} %bitcast.place_ref, s32[32]{0:T(128)S(1)} %copy-done.11, bf16[8,144,896]{2,1,0:T(8,128)(2,1)} %all-to-all-done.rows_ref, ...), custom_call_target="tpu_custom_call" | custom-call | tf_op jit(solution)/shard_map/pallas_call | solution.py:222
  103.0 5.4 %all-to-all-start.1 = ((bf16[8,144,896]{2,1,0:T(8,128)(2,1)}), bf16[8,144,896]{2,1,0:T(8,128)(2,1)}, u32[]{:S(2)}, u32[]{:S(2)}) async-start(bf16[8,144,896]{2,1,0:T(8,128)(2,1)} %copy-done.3), calls=%async_computation.1 | async-start | bytes 4128768 | tf_op jit(solution)/shard_map/all_to_all | solution.py:333
  112.4 7.1 %collective-permute-done.13.up_got_ref = bf16[768,256]{1,0:T(8,128)(2,1)S(1)} collective-permute-done((bf16[768,256]{1,0:T(8,128)(2,1)}, bf16[768,256]{1,0:T(8,128)(2,1)S(1)}, u32[]{:S(2)}, u32[]{:S(2)}) %collective-permute-start.13) | collective-permute-done | bytes 393248 | tf_op jit(solution)/shard_map/ppermute | solution.py:323
  119.7 5.3 %collective-permute-start.15 = (bf16[768,256]{1,0:T(8,128)(2,1)S(1)}, bf16[768,256]{1,0:T(8,128)(2,1)S(1)}, u32[]{:S(2)}, u32[]{:S(2)}) collective-permute-start(bf16[768,256]{1,0:T(8,128)(2,1)S(1)} %get-tuple-element.49), channel_id=1, source_target_pairs={{0,128},{16,144},{32,160},{48,176},{64,192},{80,208},{96,224},{112... | collective-permute-start | bytes 1179656 | tf_op jit(solution)/shard_map/ppermute | solution.py:323
  125.6 2.0 collective-permute-done.19.up_got_ref
  128.8 24.4 %collective-permute-start.21 = (bf16[400,384]{1,0:T(8,128)(2,1)}, bf16[400,384]{1,0:T(8,128)(2,1)}, u32[]{:S(2)}, u32[]{:S(2)}) collective-permute-start(bf16[400,384]{1,0:T(8,128)(2,1)} %get-tuple-element.61), channel_id=1, source_target_pairs={{0,128},{16,144},{32,160},{48,176},{64,192},{80,208},{96,224},{112... | collective-permute-start | bytes 921608 | tf_op jit(solution)/shard_map/ppermute | solution.py:323
  154.6 12.6 %collective-permute-done.15.up_got_ref = bf16[768,256]{1,0:T(8,128)(2,1)S(1)} collective-permute-done((bf16[768,256]{1,0:T(8,128)(2,1)S(1)}, bf16[768,256]{1,0:T(8,128)(2,1)S(1)}, u32[]{:S(2)}, u32[]{:S(2)}) %collective-permute-start.15) | collective-permute-done | bytes 393248 | tf_op jit(solution)/shard_map/ppermute | solution.py:323
  170.2 5.0 %shard_map.70 = (f32[2,1,448]{2,1,0:T(1,128)S(1)}, f32[2,768,256]{2,1,0:T(8,128)S(1)}, f32[2,384,384]{2,1,0:T(8,128)S(1)}) custom-call(s32[1]{0:T(128)} %bitcast.place_ref, s32[32]{0:T(128)S(1)} %copy-done.11, bf16[8,144,896]{2,1,0:T(8,128)(2,1)} %all-to-all-done.1.rows_ref, bf16[768,1152]{1,0:T(8,128)(2,1)S(1)} %copy-done.2, ...), custom_call_target="tpu_custom_call" | custom-call | tf_op jit(solution)/shard_map/pallas_call | solution.py:222
  175.5 6.4 %collective-permute-start.17 = (bf16[768,256]{1,0:T(8,128)(2,1)S(1)}, bf16[768,256]{1,0:T(8,128)(2,1)S(1)}, u32[]{:S(2)}, u32[]{:S(2)}) collective-permute-start(bf16[768,256]{1,0:T(8,128)(2,1)S(1)} %get-tuple-element.56), channel_id=1, source_target_pairs={{0,128},{16,144},{32,160},{48,176},{64,192},{80,208},{96,224},{112... | collective-permute-start | bytes 1179656 | tf_op jit(solution)/shard_map/ppermute | solution.py:323
  184.7 7.1 %collective-permute-start.23 = (bf16[400,384]{1,0:T(8,128)(2,1)S(1)}, bf16[400,384]{1,0:T(8,128)(2,1)S(1)}, u32[]{:S(2)}, u32[]{:S(2)}) collective-permute-start(bf16[400,384]{1,0:T(8,128)(2,1)S(1)} %get-tuple-element.63), channel_id=1, source_target_pairs={{0,128},{16,144},{32,160},{48,176},{64,192},{80,208},{96,224},{112... | collective-permute-start | bytes 921608 | tf_op jit(solution)/shard_map/ppermute | solution.py:323
  193.1 6.4 %collective-permute-done.23.refs_4_ = bf16[400,384]{1,0:T(8,128)(2,1)S(1)} collective-permute-done((bf16[400,384]{1,0:T(8,128)(2,1)S(1)}, bf16[400,384]{1,0:T(8,128)(2,1)S(1)}, u32[]{:S(2)}, u32[]{:S(2)}) %collective-permute-start.23) | collective-permute-done | bytes 307232 | tf_op jit(solution)/shard_map/ppermute | solution.py:323
  199.5 8.1 %collective-permute-done.24.refs_5_ = bf16[400,384]{1,0:T(8,128)(2,1)S(1)} collective-permute-done((bf16[400,384]{1,0:T(8,128)(2,1)S(1)}, bf16[400,384]{1,0:T(8,128)(2,1)S(1)}, u32[]{:S(2)}, u32[]{:S(2)}) %collective-permute-start.24) | collective-permute-done | bytes 307232 | tf_op jit(solution)/shard_map/ppermute | solution.py:323
  (67 shorter events, 25.6 us)
Async XLA Ops:
  2.6 19.7 %collective-permute-start = (bf16[24,1152]{1,0:T(8,128)(2,1)S(1)}, bf16[24,1152]{1,0:T(8,128)(2,1)S(1)}, u32[]{:S(2)}, u32[]{:S(2)}) collective-permute-start(bf16[24,1152]{1,0:T(8,128)(2,1)S(1)} %get-tuple-element.67), channel_id=1, source_target_pairs={{0,128},{16,144},{32,160},{48,176},{64,192},{80,208},{96,224},{112... | collective-permute-start | bytes 165896 | tf_op jit(solution)/shard_map/ppermute | solution.py:311
  7.8 14.6 %collective-permute-start.1 = (bf16[24,1152]{1,0:T(8,128)(2,1)S(1)}, bf16[24,1152]{1,0:T(8,128)(2,1)S(1)}, u32[]{:S(2)}, u32[]{:S(2)}) collective-permute-start(bf16[24,1152]{1,0:T(8,128)(2,1)S(1)} %get-tuple-element.66), channel_id=1, source_target_pairs={{0,256},{16,272},{32,288},{48,304},{64,320},{80,336},{96,352},{112... | collective-permute-start | bytes 165896 | tf_op jit(solution)/shard_map/ppermute | solution.py:311
  16.9 7.1 %collective-permute-start.2 = (bf16[24,1152]{1,0:T(8,128)(2,1)S(1)}, bf16[24,1152]{1,0:T(8,128)(2,1)S(1)}, u32[]{:S(2)}, u32[]{:S(2)}) collective-permute-start(bf16[24,1152]{1,0:T(8,128)(2,1)S(1)} %get-tuple-element.65), channel_id=1, source_target_pairs={{0,384},{16,400},{32,416},{48,432},{64,448},{80,464},{96,480},{112... | collective-permute-start | bytes 165896 | tf_op jit(solution)/shard_map/ppermute | solution.py:311
  24.1 9.1 %collective-permute-start.3 = (bf16[104,1152]{1,0:T(8,128)(2,1)S(1)}, bf16[104,1152]{1,0:T(8,128)(2,1)S(1)}, u32[]{:S(2)}, u32[]{:S(2)}) collective-permute-start(bf16[104,1152]{1,0:T(8,128)(2,1)S(1)} %shard_map.66.refs_0_), channel_id=1, source_target_pairs={{0,64},{16,80},{32,96},{48,112},{64,0},{80,16},{96,32},{112,48},{1... | collective-permute-start | bytes 718856 | tf_op jit(solution)/shard_map/ppermute | solution.py:344
  33.2 8.4 %collective-permute-start.4 = (bf16[104,1152]{1,0:T(8,128)(2,1)S(1)}, bf16[104,1152]{1,0:T(8,128)(2,1)S(1)}, u32[]{:S(2)}, u32[]{:S(2)}) collective-permute-start(bf16[104,1152]{1,0:T(8,128)(2,1)S(1)} %collective-permute-done.3.refs_4_), channel_id=1, source_target_pairs={{0,16},{16,32},{32,48},{48,0},{64,80},{80,96},{96,112},{112,64},{1... | collective-permute-start | bytes 718856 | tf_op jit(solution)/shard_map/ppermute | solution.py:319
  41.6 6.5 %copy-start.9 = (bf16[64,448]{1,0:T(8,128)(2,1)S(1)}, bf16[64,448]{1,0:T(8,128)(2,1)}, u32[]{:S(2)}) copy-start(bf16[64,448]{1,0:T(8,128)(2,1)} %refs_8_.1) | copy-start | bytes 172036
  41.6 53.5 %all-to-all-start = ((bf16[8,144,896]{2,1,0:T(8,128)(2,1)}), bf16[8,144,896]{2,1,0:T(8,128)(2,1)}, u32[]{:S(2)}, u32[]{:S(2)}) async-start(bf16[8,144,896]{2,1,0:T(8,128)(2,1)} %get-tuple-element.39), calls=%async_computation | async-start | bytes 4128768 | tf_op jit(solution)/shard_map/all_to_all | solution.py:333
  48.1 47.0 %copy-start.11 = (s32[32]{0:T(128)S(1)}, s32[32]{0:T(128)}, u32[]{:S(2)}) copy-start(s32[32]{0:T(128)} %counts_ref.5) | copy-start | bytes 388
  48.1 28.7 %collective-permute-start.10 = (bf16[64,448]{1,0:T(8,128)(2,1)S(1)}, bf16[64,448]{1,0:T(8,128)(2,1)S(1)}, u32[]{:S(2)}, u32[]{:S(2)}) collective-permute-start(bf16[64,448]{1,0:T(8,128)(2,1)S(1)} %copy-done.9), channel_id=1, source_target_pairs={{0,128},{16,144},{32,160},{48,176},{64,192},{80,208},{96,224},{112... | collective-permute-start | bytes 172040 | tf_op jit(solution)/shard_map/ppermute | solution.py:311
  50.7 28.9 %collective-permute-start.11 = (bf16[64,448]{1,0:T(8,128)(2,1)S(1)}, bf16[64,448]{1,0:T(8,128)(2,1)S(1)}, u32[]{:S(2)}, u32[]{:S(2)}) collective-permute-start(bf16[64,448]{1,0:T(8,128)(2,1)S(1)} %copy-done.9), channel_id=1, source_target_pairs={{0,256},{16,272},{32,288},{48,304},{64,320},{80,336},{96,352},{112... | collective-permute-start | bytes 172040 | tf_op jit(solution)/shard_map/ppermute | solution.py:311
  59.1 23.8 %collective-permute-start.12 = (bf16[64,448]{1,0:T(8,128)(2,1)S(1)}, bf16[64,448]{1,0:T(8,128)(2,1)S(1)}, u32[]{:S(2)}, u32[]{:S(2)}) collective-permute-start(bf16[64,448]{1,0:T(8,128)(2,1)S(1)} %copy-done.9), channel_id=1, source_target_pairs={{0,384},{16,400},{32,416},{48,432},{64,448},{80,464},{96,480},{112... | collective-permute-start | bytes 172040 | tf_op jit(solution)/shard_map/ppermute | solution.py:311
  61.7 24.9 %collective-permute-start.5 = (bf16[104,1152]{1,0:T(8,128)(2,1)S(1)}, bf16[104,1152]{1,0:T(8,128)(2,1)S(1)}, u32[]{:S(2)}, u32[]{:S(2)}) collective-permute-start(bf16[104,1152]{1,0:T(8,128)(2,1)S(1)} %shard_map.66.refs_0_), channel_id=1, source_target_pairs={{0,16},{16,32},{32,48},{48,0},{64,80},{80,96},{96,112},{112,64},{1... | collective-permute-start | bytes 718856 | tf_op jit(solution)/shard_map/ppermute | solution.py:319
  64.2 22.5 %collective-permute-start.6 = (bf16[104,1152]{1,0:T(8,128)(2,1)S(1)}, bf16[104,1152]{1,0:T(8,128)(2,1)S(1)}, u32[]{:S(2)}, u32[]{:S(2)}) collective-permute-start(bf16[104,1152]{1,0:T(8,128)(2,1)S(1)} %shard_map.66.refs_0_), channel_id=1, source_target_pairs={{0,32},{16,48},{32,0},{48,16},{64,96},{80,112},{96,64},{112,80},{1... | collective-permute-start | bytes 718856 | tf_op jit(solution)/shard_map/ppermute | solution.py:319
  76.8 14.1 %collective-permute-start.7 = (bf16[104,1152]{1,0:T(8,128)(2,1)S(1)}, bf16[104,1152]{1,0:T(8,128)(2,1)S(1)}, u32[]{:S(2)}, u32[]{:S(2)}) collective-permute-start(bf16[104,1152]{1,0:T(8,128)(2,1)S(1)} %shard_map.66.refs_0_), channel_id=1, source_target_pairs={{0,48},{16,0},{32,16},{48,32},{64,112},{80,64},{96,80},{112,96},{1... | collective-permute-start | bytes 718856 | tf_op jit(solution)/shard_map/ppermute | solution.py:319
  79.6 11.4 %collective-permute-start.8 = (bf16[104,1152]{1,0:T(8,128)(2,1)S(1)}, bf16[104,1152]{1,0:T(8,128)(2,1)S(1)}, u32[]{:S(2)}, u32[]{:S(2)}) collective-permute-start(bf16[104,1152]{1,0:T(8,128)(2,1)S(1)} %collective-permute-done.3.refs_4_), channel_id=1, source_target_pairs={{0,32},{16,48},{32,0},{48,16},{64,96},{80,112},{96,64},{112,80},{1... | collective-permute-start | bytes 718856 | tf_op jit(solution)/shard_map/ppermute | solution.py:319
  82.9 10.7 %collective-permute-start.9 = (bf16[104,1152]{1,0:T(8,128)(2,1)S(1)}, bf16[104,1152]{1,0:T(8,128)(2,1)S(1)}, u32[]{:S(2)}, u32[]{:S(2)}) collective-permute-start(bf16[104,1152]{1,0:T(8,128)(2,1)S(1)} %collective-permute-done.3.refs_4_), channel_id=1, source_target_pairs={{0,48},{16,0},{32,16},{48,32},{64,112},{80,64},{96,80},{112,96},{1... | collective-permute-start | bytes 718856 | tf_op jit(solution)/shard_map/ppermute | solution.py:319
  103.0 65.7 %all-to-all-start.1 = ((bf16[8,144,896]{2,1,0:T(8,128)(2,1)}), bf16[8,144,896]{2,1,0:T(8,128)(2,1)}, u32[]{:S(2)}, u32[]{:S(2)}) async-start(bf16[8,144,896]{2,1,0:T(8,128)(2,1)} %copy-done.3), calls=%async_computation.1 | async-start | bytes 4128768 | tf_op jit(solution)/shard_map/all_to_all | solution.py:333
  108.4 11.2 %collective-permute-start.13 = (bf16[768,256]{1,0:T(8,128)(2,1)}, bf16[768,256]{1,0:T(8,128)(2,1)S(1)}, u32[]{:S(2)}, u32[]{:S(2)}) collective-permute-start(bf16[768,256]{1,0:T(8,128)(2,1)} %copy-done.12), channel_id=1, source_target_pairs={{0,128},{16,144},{32,160},{48,176},{64,192},{80,208},{96,224},{112... | collective-permute-start | bytes 1179656 | tf_op jit(solution)/shard_map/ppermute | solution.py:323
  109.7 9.8 %collective-permute-start.14 = (bf16[768,256]{1,0:T(8,128)(2,1)}, bf16[768,256]{1,0:T(8,128)(2,1)S(1)}, u32[]{:S(2)}, u32[]{:S(2)}) collective-permute-start(bf16[768,256]{1,0:T(8,128)(2,1)} %copy-done.12), channel_id=1, source_target_pairs={{384,256},{400,272},{416,288},{432,304},{448,320},{464,336},{480,3... | collective-permute-start | bytes 1179656 | tf_op jit(solution)/shard_map/ppermute | solution.py:323
  110.4 17.3 %collective-permute-start.19 = (bf16[400,384]{1,0:T(8,128)(2,1)}, bf16[400,384]{1,0:T(8,128)(2,1)S(1)}, u32[]{:S(2)}, u32[]{:S(2)}) collective-permute-start(bf16[400,384]{1,0:T(8,128)(2,1)} %copy-done.13), channel_id=1, source_target_pairs={{0,128},{16,144},{32,160},{48,176},{64,192},{80,208},{96,224},{112... | collective-permute-start | bytes 921608 | tf_op jit(solution)/shard_map/ppermute | solution.py:323
  111.7 15.9 %collective-permute-start.20 = (bf16[400,384]{1,0:T(8,128)(2,1)}, bf16[400,384]{1,0:T(8,128)(2,1)S(1)}, u32[]{:S(2)}, u32[]{:S(2)}) collective-permute-start(bf16[400,384]{1,0:T(8,128)(2,1)} %copy-done.13), channel_id=1, source_target_pairs={{384,256},{400,272},{416,288},{432,304},{448,320},{464,336},{480,3... | collective-permute-start | bytes 921608 | tf_op jit(solution)/shard_map/ppermute | solution.py:323
  119.7 47.5 %collective-permute-start.15 = (bf16[768,256]{1,0:T(8,128)(2,1)S(1)}, bf16[768,256]{1,0:T(8,128)(2,1)S(1)}, u32[]{:S(2)}, u32[]{:S(2)}) collective-permute-start(bf16[768,256]{1,0:T(8,128)(2,1)S(1)} %get-tuple-element.49), channel_id=1, source_target_pairs={{0,128},{16,144},{32,160},{48,176},{64,192},{80,208},{96,224},{112... | collective-permute-start | bytes 1179656 | tf_op jit(solution)/shard_map/ppermute | solution.py:323
  124.9 43.0 %collective-permute-start.16 = (bf16[768,256]{1,0:T(8,128)(2,1)S(1)}, bf16[768,256]{1,0:T(8,128)(2,1)S(1)}, u32[]{:S(2)}, u32[]{:S(2)}) collective-permute-start(bf16[768,256]{1,0:T(8,128)(2,1)S(1)} %get-tuple-element.50), channel_id=1, source_target_pairs={{256,128},{272,144},{288,160},{304,176},{320,192},{336,208},{352,2... | collective-permute-start | bytes 1179656 | tf_op jit(solution)/shard_map/ppermute | solution.py:323
  128.8 54.4 %collective-permute-start.21 = (bf16[400,384]{1,0:T(8,128)(2,1)}, bf16[400,384]{1,0:T(8,128)(2,1)}, u32[]{:S(2)}, u32[]{:S(2)}) collective-permute-start(bf16[400,384]{1,0:T(8,128)(2,1)} %get-tuple-element.61), channel_id=1, source_target_pairs={{0,128},{16,144},{32,160},{48,176},{64,192},{80,208},{96,224},{112... | collective-permute-start | bytes 921608 | tf_op jit(solution)/shard_map/ppermute | solution.py:323
  153.2 30.0 %collective-permute-start.22 = (bf16[400,384]{1,0:T(8,128)(2,1)}, bf16[400,384]{1,0:T(8,128)(2,1)}, u32[]{:S(2)}, u32[]{:S(2)}) collective-permute-start(bf16[400,384]{1,0:T(8,128)(2,1)} %get-tuple-element.62), channel_id=1, source_target_pairs={{256,128},{272,144},{288,160},{304,176},{320,192},{336,208},{352,2... | collective-permute-start | bytes 921608 | tf_op jit(solution)/shard_map/ppermute | solution.py:323
  170.2 5.0 %copy-start.5 = (bf16[768,256]{1,0:T(8,128)(2,1)S(1)}, bf16[768,256]{1,0:T(8,128)(2,1)}, u32[]{:S(2)}) copy-start(bf16[768,256]{1,0:T(8,128)(2,1)} %copy-done.4) | copy-start | bytes 1179652
  170.2 5.1 %copy-start.7 = (bf16[768,256]{1,0:T(8,128)(2,1)S(1)}, bf16[768,256]{1,0:T(8,128)(2,1)}, u32[]{:S(2)}) copy-start(bf16[768,256]{1,0:T(8,128)(2,1)} %copy-done.6) | copy-start | bytes 1179652
  175.5 17.6 %copy-start.14 = (bf16[448]{0:T(512)(128)(2,1)S(1)}, bf16[448]{0:T(512)(128)(2,1)}, u32[]{:S(2)}) copy-start(bf16[448]{0:T(512)(128)(2,1)} %param.10) | copy-start | bytes 2692
  175.5 32.1 %collective-permute-start.17 = (bf16[768,256]{1,0:T(8,128)(2,1)S(1)}, bf16[768,256]{1,0:T(8,128)(2,1)S(1)}, u32[]{:S(2)}, u32[]{:S(2)}) collective-permute-start(bf16[768,256]{1,0:T(8,128)(2,1)S(1)} %get-tuple-element.56), channel_id=1, source_target_pairs={{0,128},{16,144},{32,160},{48,176},{64,192},{80,208},{96,224},{112... | collective-permute-start | bytes 1179656 | tf_op jit(solution)/shard_map/ppermute | solution.py:323
  181.9 25.7 %collective-permute-start.18 = (bf16[768,256]{1,0:T(8,128)(2,1)S(1)}, bf16[768,256]{1,0:T(8,128)(2,1)S(1)}, u32[]{:S(2)}, u32[]{:S(2)}) collective-permute-start(bf16[768,256]{1,0:T(8,128)(2,1)S(1)} %get-tuple-element.57), channel_id=1, source_target_pairs={{128,0},{144,16},{160,32},{176,48},{192,64},{208,80},{224,96},{240... | collective-permute-start | bytes 1179656 | tf_op jit(solution)/shard_map/ppermute | solution.py:323
  184.7 14.8 %collective-permute-start.23 = (bf16[400,384]{1,0:T(8,128)(2,1)S(1)}, bf16[400,384]{1,0:T(8,128)(2,1)S(1)}, u32[]{:S(2)}, u32[]{:S(2)}) collective-permute-start(bf16[400,384]{1,0:T(8,128)(2,1)S(1)} %get-tuple-element.63), channel_id=1, source_target_pairs={{0,128},{16,144},{32,160},{48,176},{64,192},{80,208},{96,224},{112... | collective-permute-start | bytes 921608 | tf_op jit(solution)/shard_map/ppermute | solution.py:323
  191.8 15.8 %collective-permute-start.24 = (bf16[400,384]{1,0:T(8,128)(2,1)S(1)}, bf16[400,384]{1,0:T(8,128)(2,1)S(1)}, u32[]{:S(2)}, u32[]{:S(2)}) collective-permute-start(bf16[400,384]{1,0:T(8,128)(2,1)S(1)} %get-tuple-element.64), channel_id=1, source_target_pairs={{128,0},{144,16},{160,32},{176,48},{192,64},{208,80},{224,96},{240... | collective-permute-start | bytes 921608 | tf_op jit(solution)/shard_map/ppermute | solution.py:323
  (10 other events, 10.1 us)

commit v4 on v3

--- a/solution.py
+++ b/solution.py
@@ -18,6 +18,7 @@
 OWN_TOKENS = 24
 FEATURES = 4096
 WINDOW = 384
+PARTS = ((0, 1), (2, 3))
 FRONT = 256
 HALF = TOKENS // 2
 LANES = 2 * (UNITS - FRONT)
@@ -102,46 +103,47 @@
     return jnp.where(k == 0, jnp.where(last, 1, 3), jnp.where(k == 1, 2, jnp.where(k == 2, jnp.where(last, 3, 1), 0)))
 
 
-def pack_kernel(place_ref, rows_ref, *out_refs):
+def pack_kernel(ks, place_ref, rows_ref, *out_refs):
     step = pl.program_id(0)
-    for k in range(PAIRS):
-
-        @pl.when(step == k)
+    for n, (part, at) in enumerate(ks):
+
+        @pl.when(step == n)
         def _():
-            at = UNITS * (k % 2)
             for i in range(GROUP):
-                out_refs[k // 2][i, :, at : at + UNITS] = rows_ref[:, UNITS * i : UNITS * (i + 1)]
-
-
-def pack(place, rows):
-    def block(k, place_ref):
+                out_refs[part][i, :, UNITS * at : UNITS * (at + 1)] = rows_ref[:, UNITS * i : UNITS * (i + 1)]
+
+
+def pack(place, rows, parts):
+    ks = [(n, at) for n, part in enumerate(parts) for at in range(len(part))]
+    first = parts[0][0]
+
+    def block(n, place_ref):
         pair = place_ref[0] // GROUP
-        return 0, lax.rem(pair + offset_of(k, pair), PAIRS)
-
-    return pl.pallas_call(
-        pack_kernel,
+        return 0, lax.rem(pair + offset_of(n + first, pair), PAIRS)
+
+    return list(pl.pallas_call(
+        functools.partial(pack_kernel, ks),
         grid_spec=pltpu.PrefetchScalarGridSpec(
             num_scalar_prefetch=1,
-            grid=(PAIRS,),
+            grid=(len(ks),),
             in_specs=[pl.BlockSpec((SLOTS, GROUP * UNITS), block)],
-            out_specs=[pl.BlockSpec((GROUP, SLOTS, 2 * UNITS), lambda k, _: (0, 0, 0))] * 2,
+            out_specs=[pl.BlockSpec((GROUP, SLOTS, len(part) * UNITS), lambda n, _: (0, 0, 0)) for part in parts],
         ),
-        out_shape=[jax.ShapeDtypeStruct((GROUP, SLOTS, 2 * UNITS), jnp.bfloat16)] * 2,
-        compiler_params=params(),
-    )(place, rows)
+        out_shape=[jax.ShapeDtypeStruct((GROUP, SLOTS, len(part) * UNITS), jnp.bfloat16) for part in parts],
+        compiler_params=params(),
+    )(place, rows))
 
 
 def assemble_kernel(place_ref, *refs):
-    block_refs, up_refs = refs[:8], refs[8:12]
-    tokens_ref, down_ref, up_ref = refs[12:]
+    block_refs, up_refs = refs[:4], refs[4:8]
+    tokens_ref, down_ref, up_ref = refs[8:]
     place = place_ref[0]
     pair, side, x = place // GROUP, (place // 4) % 2, place % 4
-    for far in range(2):
-        for step in range(4):
-            block_ref = block_refs[4 * far + step]
+    for step, block_ref in enumerate(block_refs):
+        for far in range(2):
             origin = 4 * lax.rem(side + far, 2) + lax.rem(x - step + 4, 4)
-            tokens_ref[pl.ds(pl.multiple_of(origin * 96, 96), 96), :] = block_ref[0:96, :]
-            folded = block_ref[96:104, :].astype(jnp.float32)
+            tokens_ref[pl.ds(pl.multiple_of(origin * 96, 96), 96), :] = block_ref[far, 0:96, :]
+            folded = block_ref[far, 96:104, :].astype(jnp.float32)
             down_ref[origin] = jnp.concatenate(
                 [folded[:, RANK * g : RANK * g + RANK] for g in range(SLOTS // 8)], axis=0
             ).astype(jnp.bfloat16)
@@ -157,7 +159,7 @@
             jax.ShapeDtypeStruct((GROUP, SLOTS, RANK), jnp.bfloat16),
             jax.ShapeDtypeStruct((PAIRS, RANK, UNITS), jnp.bfloat16),
         ],
-        in_specs=[whole(pltpu.SMEM)] + [whole()] * 12,
+        in_specs=[whole(pltpu.SMEM)] + [whole()] * 8,
         out_specs=[whole()] * 3,
         compiler_params=params(),
     )(place, *blocks, *ups)
@@ -338,14 +340,16 @@
     own = own_windows(place, counts, tokens)
     moved = [to_pair(own[step], step) for step in range(1, PAIRS)]
     ups = [adapter_up_factor] + [to_pair(adapter_up_factor, step) for step in range(1, PAIRS)]
-    frozen_slot_rows, moved[0] = lax.optimization_barrier((frozen_slot_rows, moved[0]))
-    sends = list(pack(place, frozen_slot_rows))
     column = collect(place, own, *moved, adapter_down_factor)
     other = lax.ppermute(column, AXIS, [(f, f ^ 4) for f in range(GROUP * PAIRS)])
-    blocks = [column] + [along_x(column, step) for step in range(1, 4)]
-    blocks += [other] + [along_x(other, step) for step in range(1, 4)]
-    sends[0], blocks[5] = lax.optimization_barrier((sends[0], blocks[5]))
+    frozen_slot_rows, column = lax.optimization_barrier((frozen_slot_rows, column))
+    sends = pack(place, frozen_slot_rows, PARTS[:1])
+    sends[0], other = lax.optimization_barrier((sends[0], other))
     rows = exchange(sends[0])
+    frozen_slot_rows, other = lax.optimization_barrier((frozen_slot_rows, other))
+    sends += pack(place, frozen_slot_rows, PARTS[1:])
+    blocks = jnp.stack([column, other])
+    blocks = [blocks] + [along_x(blocks, step) for step in range(1, 4)]
     all_tokens, down, up = assemble(place, blocks, ups)
     early_squares, early_front, early_back, first_front, first_back = partial_products(
         0, place, counts, rows, all_tokens, down, up

time: 210 us -> 201 us (0.957)
  the two profiles are of different devices: /device:TPU:46 before, /device:TPU:30 now
where the time goes in v4:
time: 201 us; the launch traced here: 200 us
  starting transfers between devices  109 us (54%)
  waiting for transfers between devices  56.1 us (28%)
  Pallas kernels  17.5 us (9%)
  local copies, waits for them, and re-layouts  16.4 us (8%)
    ppermute x12, waiting for transfers between devices, hop(): lax.ppermute(array, AXIS, [(GROUP * p + i, GROUP * (p + way) + i) for p i...  45.1 us
    ppermute x12, starting transfers between devices, hop(): lax.ppermute(array, AXIS, [(GROUP * p + i, GROUP * (p + way) + i) for p i...  43.5 us
    ppermute x6, starting transfers between devices, to_pair(): lax.ppermute(array, AXIS, [(GROUP * p + i, GROUP * ((p + step) % PAIRS) +...  39.8 us
    unnamed x35, local copies, waits for them, and re-layouts  15.3 us
    all_to_all x2, starting transfers between devices, exchange(): return lax.all_to_all(send, AXIS, 0, 0, axis_index_groups=NEAR, tiled=True)  13.5 us
    pallas_call x2, Pallas kernels, partial_products(): pl.pallas_call(functools.partial(partial_kernel, stage), out_shape=out_sh...  9.94 us
    ppermute x3, starting transfers between devices, along_x(): lax.ppermute(array, AXIS, [(4 * z + x, 4 * z + (x + step) % 4) for z in r...  8.66 us
    ppermute x6, waiting for transfers between devices, to_pair(): lax.ppermute(array, AXIS, [(GROUP * p + i, GROUP * ((p + step) % PAIRS) +...  4.93 us
  transfers between devices with their start and end apart: 24, of which 8 were waited for; matrix products, arithmetic and copies ran while one was open for 0% of the time, Pallas kernels for 5%

profile of v4, /device:TPU:30, one launch (start us, length us, event | category | flops | bytes accessed | tf_op | source)
XLA Modules:
  0.0 199.8 jit_solution(3216974118103492076)
XLA Ops:
  2.6 5.2 %collective-permute-start = (bf16[24,1152]{1,0:T(8,128)(2,1)S(1)}, bf16[24,1152]{1,0:T(8,128)(2,1)S(1)}, u32[]{:S(2)}, u32[]{:S(2)}) collective-permute-start(bf16[24,1152]{1,0:T(8,128)(2,1)S(1)} %get-tuple-element.67), channel_id=1, source_target_pairs={{0,128},{16,144},{32,160},{48,176},{64,192},{80,208},{96,224},{112... | collective-permute-start | bytes 165896 | tf_op jit(solution)/shard_map/ppermute | solution.py:313
  7.8 9.1 %collective-permute-start.1 = (bf16[24,1152]{1,0:T(8,128)(2,1)S(1)}, bf16[24,1152]{1,0:T(8,128)(2,1)S(1)}, u32[]{:S(2)}, u32[]{:S(2)}) collective-permute-start(bf16[24,1152]{1,0:T(8,128)(2,1)S(1)} %get-tuple-element.66), channel_id=1, source_target_pairs={{0,256},{16,272},{32,288},{48,304},{64,320},{80,336},{96,352},{112... | collective-permute-start | bytes 165896 | tf_op jit(solution)/shard_map/ppermute | solution.py:313
  16.9 4.6 %collective-permute-start.2 = (bf16[24,1152]{1,0:T(8,128)(2,1)S(1)}, bf16[24,1152]{1,0:T(8,128)(2,1)S(1)}, u32[]{:S(2)}, u32[]{:S(2)}) collective-permute-start(bf16[24,1152]{1,0:T(8,128)(2,1)S(1)} %get-tuple-element.65), channel_id=1, source_target_pairs={{0,384},{16,400},{32,416},{48,432},{64,448},{80,464},{96,480},{112... | collective-permute-start | bytes 165896 | tf_op jit(solution)/shard_map/ppermute | solution.py:313
  22.3 1.6 collective-permute-done.2.three_ref
  24.0 3.9 %collective-permute-start.3 = (bf16[104,1152]{1,0:T(8,128)(2,1)S(1)}, bf16[104,1152]{1,0:T(8,128)(2,1)S(1)}, u32[]{:S(2)}, u32[]{:S(2)}) collective-permute-start(bf16[104,1152]{1,0:T(8,128)(2,1)S(1)} %shard_map.65), channel_id=1, source_target_pairs={{0,64},{16,80},{32,96},{48,112},{64,0},{80,16},{96,32},{112,48},{1... | collective-permute-start | bytes 718856 | tf_op jit(solution)/shard_map/ppermute | solution.py:344
  27.9 2.2 %copy-done = bf16[144,14336]{1,0:T(8,128)(2,1)S(1)} copy-done((bf16[144,14336]{1,0:T(8,128)(2,1)S(1)}, bf16[144,14336]{1,0:T(8,128)(2,1)}, u32[]{:S(2)}) %copy-start) | copy-done | bytes 4128792
  30.1 2.0 %shard_map.66 = bf16[8,144,896]{2,1,0:T(8,128)(2,1)} custom-call(s32[1]{0:T(128)} %bitcast.place_ref, bf16[144,14336]{1,0:T(8,128)(2,1)S(1)} %copy-done), custom_call_target="tpu_custom_call" | custom-call | tf_op jit(solution)/shard_map/pallas_call | solution.py:124
  33.4 5.9 %all-to-all-start = ((bf16[8,144,896]{2,1,0:T(8,128)(2,1)}), bf16[8,144,896]{2,1,0:T(8,128)(2,1)}, u32[]{:S(2)}, u32[]{:S(2)}) async-start(bf16[8,144,896]{2,1,0:T(8,128)(2,1)} %shard_map.66), calls=%async_computation | async-start | bytes 4128768 | tf_op jit(solution)/shard_map/all_to_all | solution.py:335
  39.4 1.9 collective-permute-start.4
  41.3 4.8 %collective-permute-start.5 = (bf16[2,104,1152]{2,1,0:T(8,128)(2,1)S(1)}, bf16[2,104,1152]{2,1,0:T(8,128)(2,1)S(1)}, u32[]{:S(2)}, u32[]{:S(2)}) collective-permute-start(bf16[2,104,1152]{2,1,0:T(8,128)(2,1)S(1)} %pad_maximum_fusion.refs_0_), channel_id=1, source_target_pairs={{0,32},{16,48},{32,0},{48,16},{64,96},{80,112},{96,64},{112,80},{1... | collective-permute-start | bytes 1437704 | tf_op jit(solution)/shard_map/ppermute | solution.py:321
  46.2 1.9 collective-permute-start.6
  48.1 2.5 %collective-permute-start.7 = (bf16[64,448]{1,0:T(8,128)(2,1)S(1)}, bf16[64,448]{1,0:T(8,128)(2,1)S(1)}, u32[]{:S(2)}, u32[]{:S(2)}) collective-permute-start(bf16[64,448]{1,0:T(8,128)(2,1)S(1)} %copy-done.11), channel_id=1, source_target_pairs={{0,128},{16,144},{32,160},{48,176},{64,192},{80,208},{96,224},{112... | collective-permute-start | bytes 172040 | tf_op jit(solution)/shard_map/ppermute | solution.py:313
  50.6 8.4 %collective-permute-start.8 = (bf16[64,448]{1,0:T(8,128)(2,1)S(1)}, bf16[64,448]{1,0:T(8,128)(2,1)S(1)}, u32[]{:S(2)}, u32[]{:S(2)}) collective-permute-start(bf16[64,448]{1,0:T(8,128)(2,1)S(1)} %copy-done.11), channel_id=1, source_target_pairs={{0,256},{16,272},{32,288},{48,304},{64,320},{80,336},{96,352},{112... | collective-permute-start | bytes 172040 | tf_op jit(solution)/shard_map/ppermute | solution.py:313
  58.9 3.3 %collective-permute-done.7.refs_5_ = bf16[64,448]{1,0:T(8,128)(2,1)S(1)} collective-permute-done((bf16[64,448]{1,0:T(8,128)(2,1)S(1)}, bf16[64,448]{1,0:T(8,128)(2,1)S(1)}, u32[]{:S(2)}, u32[]{:S(2)}) %collective-permute-start.7) | collective-permute-done | bytes 57376 | tf_op jit(solution)/shard_map/ppermute | solution.py:313
  62.3 10.1 %collective-permute-start.9 = (bf16[64,448]{1,0:T(8,128)(2,1)S(1)}, bf16[64,448]{1,0:T(8,128)(2,1)S(1)}, u32[]{:S(2)}, u32[]{:S(2)}) collective-permute-start(bf16[64,448]{1,0:T(8,128)(2,1)S(1)} %copy-done.11), channel_id=1, source_target_pairs={{0,384},{16,400},{32,416},{48,432},{64,448},{80,464},{96,480},{112... | collective-permute-start | bytes 172040 | tf_op jit(solution)/shard_map/ppermute | solution.py:313
  72.4 2.2 %copy-done.1 = bf16[144,14336]{1,0:T(8,128)(2,1)S(1)} copy-done((bf16[144,14336]{1,0:T(8,128)(2,1)S(1)}, bf16[144,14336]{1,0:T(8,128)(2,1)}, u32[]{:S(2)}) %copy-start.1) | copy-done | bytes 4128792
  76.6 4.8 %collective-permute-done.6.refs_3_ = bf16[2,104,1152]{2,1,0:T(8,128)(2,1)S(1)} collective-permute-done((bf16[2,104,1152]{2,1,0:T(8,128)(2,1)S(1)}, bf16[2,104,1152]{2,1,0:T(8,128)(2,1)S(1)}, u32[]{:S(2)}, u32[]{:S(2)}) %collective-permute-start.6) | collective-permute-done | bytes 479264 | tf_op jit(solution)/shard_map/ppermute | solution.py:321
  82.9 1.5 copy-done.4
  84.4 4.9 %shard_map.69 = (f32[2,1,448]{2,1,0:T(1,128)S(1)}, f32[2,768,256]{2,1,0:T(8,128)S(1)}, f32[2,384,384]{2,1,0:T(8,128)S(1)}, bf16[768,256]{1,0:T(8,128)(2,1)S(1)}, bf16[400,384]{1,0:T(8,128)(2,1)S(1)}) custom-call(s32[1]{0:T(128)} %bitcast.place_ref, s32[32]{0:T(128)S(1)} %copy-done.13, bf16[8,144,896]{2,1,0:T(8,128)(2,1)} %all-to-all-done.rows_ref, ...), custom_call_target="tpu_custom_call" | custom-call | tf_op jit(solution)/shard_map/pallas_call | solution.py:224
  90.8 7.6 %all-to-all-start.1 = ((bf16[8,144,896]{2,1,0:T(8,128)(2,1)}), bf16[8,144,896]{2,1,0:T(8,128)(2,1)}, u32[]{:S(2)}, u32[]{:S(2)}) async-start(bf16[8,144,896]{2,1,0:T(8,128)(2,1)} %copy-done.2), calls=%async_computation.1 | async-start | bytes 4128768 | tf_op jit(solution)/shard_map/all_to_all | solution.py:335
  98.4 2.0 collective-permute-start.10
  103.0 27.7 %collective-permute-done.10.up_got_ref = bf16[768,256]{1,0:T(8,128)(2,1)S(1)} collective-permute-done((bf16[768,256]{1,0:T(8,128)(2,1)}, bf16[768,256]{1,0:T(8,128)(2,1)S(1)}, u32[]{:S(2)}, u32[]{:S(2)}) %collective-permute-start.10) | collective-permute-done | bytes 393248 | tf_op jit(solution)/shard_map/ppermute | solution.py:325
  130.9 5.3 %collective-permute-start.12 = (bf16[768,256]{1,0:T(8,128)(2,1)S(1)}, bf16[768,256]{1,0:T(8,128)(2,1)S(1)}, u32[]{:S(2)}, u32[]{:S(2)}) collective-permute-start(bf16[768,256]{1,0:T(8,128)(2,1)S(1)} %get-tuple-element.49), channel_id=1, source_target_pairs={{0,128},{16,144},{32,160},{48,176},{64,192},{80,208},{96,224},{112... | collective-permute-start | bytes 1179656 | tf_op jit(solution)/shard_map/ppermute | solution.py:325
  138.5 6.0 %collective-permute-start.18 = (bf16[400,384]{1,0:T(8,128)(2,1)}, bf16[400,384]{1,0:T(8,128)(2,1)}, u32[]{:S(2)}, u32[]{:S(2)}) collective-permute-start(bf16[400,384]{1,0:T(8,128)(2,1)} %get-tuple-element.61), channel_id=1, source_target_pairs={{0,128},{16,144},{32,160},{48,176},{64,192},{80,208},{96,224},{112... | collective-permute-start | bytes 921608 | tf_op jit(solution)/shard_map/ppermute | solution.py:325
  144.4 1.4 collective-permute-start.19
  147.3 1.5 copy-done.5
  148.8 5.0 %shard_map.71 = (f32[2,1,448]{2,1,0:T(1,128)S(1)}, f32[2,768,256]{2,1,0:T(8,128)S(1)}, f32[2,384,384]{2,1,0:T(8,128)S(1)}) custom-call(s32[1]{0:T(128)} %bitcast.place_ref, s32[32]{0:T(128)S(1)} %copy-done.13, bf16[8,144,896]{2,1,0:T(8,128)(2,1)} %all-to-all-done.1.rows_ref, bf16[768,1152]{1,0:T(8,128)(2,1)S(1)} %copy-done.5, ...), custom_call_target="tpu_custom_call" | custom-call | tf_op jit(solution)/shard_map/pallas_call | solution.py:224
  154.2 17.5 %collective-permute-start.14 = (bf16[768,256]{1,0:T(8,128)(2,1)S(1)}, bf16[768,256]{1,0:T(8,128)(2,1)S(1)}, u32[]{:S(2)}, u32[]{:S(2)}) collective-permute-start(bf16[768,256]{1,0:T(8,128)(2,1)S(1)} %get-tuple-element.56), channel_id=1, source_target_pairs={{0,128},{16,144},{32,160},{48,176},{64,192},{80,208},{96,224},{112... | collective-permute-start | bytes 1179656 | tf_op jit(solution)/shard_map/ppermute | solution.py:325
  173.0 1.4 shard_map.74
  174.4 5.5 %collective-permute-start.20 = (bf16[400,384]{1,0:T(8,128)(2,1)S(1)}, bf16[400,384]{1,0:T(8,128)(2,1)S(1)}, u32[]{:S(2)}, u32[]{:S(2)}) collective-permute-start(bf16[400,384]{1,0:T(8,128)(2,1)S(1)} %get-tuple-element.63), channel_id=1, source_target_pairs={{0,128},{16,144},{32,160},{48,176},{64,192},{80,208},{96,224},{112... | collective-permute-start | bytes 921608 | tf_op jit(solution)/shard_map/ppermute | solution.py:325
  181.2 3.1 %collective-permute-done.20.refs_4_ = bf16[400,384]{1,0:T(8,128)(2,1)S(1)} collective-permute-done((bf16[400,384]{1,0:T(8,128)(2,1)S(1)}, bf16[400,384]{1,0:T(8,128)(2,1)S(1)}, u32[]{:S(2)}, u32[]{:S(2)}) %collective-permute-start.20) | collective-permute-done | bytes 307232 | tf_op jit(solution)/shard_map/ppermute | solution.py:325
  184.3 13.9 %collective-permute-done.21.refs_5_ = bf16[400,384]{1,0:T(8,128)(2,1)S(1)} collective-permute-done((bf16[400,384]{1,0:T(8,128)(2,1)S(1)}, bf16[400,384]{1,0:T(8,128)(2,1)S(1)}, u32[]{:S(2)}, u32[]{:S(2)}) %collective-permute-start.21) | collective-permute-done | bytes 307232 | tf_op jit(solution)/shard_map/ppermute | solution.py:325
  (67 shorter events, 21.1 us)
Async XLA Ops:
  2.6 19.7 %collective-permute-start = (bf16[24,1152]{1,0:T(8,128)(2,1)S(1)}, bf16[24,1152]{1,0:T(8,128)(2,1)S(1)}, u32[]{:S(2)}, u32[]{:S(2)}) collective-permute-start(bf16[24,1152]{1,0:T(8,128)(2,1)S(1)} %get-tuple-element.67), channel_id=1, source_target_pairs={{0,128},{16,144},{32,160},{48,176},{64,192},{80,208},{96,224},{112... | collective-permute-start | bytes 165896 | tf_op jit(solution)/shard_map/ppermute | solution.py:313
  7.8 14.6 %collective-permute-start.1 = (bf16[24,1152]{1,0:T(8,128)(2,1)S(1)}, bf16[24,1152]{1,0:T(8,128)(2,1)S(1)}, u32[]{:S(2)}, u32[]{:S(2)}) collective-permute-start(bf16[24,1152]{1,0:T(8,128)(2,1)S(1)} %get-tuple-element.66), channel_id=1, source_target_pairs={{0,256},{16,272},{32,288},{48,304},{64,320},{80,336},{96,352},{112... | collective-permute-start | bytes 165896 | tf_op jit(solution)/shard_map/ppermute | solution.py:313
  16.9 7.1 %collective-permute-start.2 = (bf16[24,1152]{1,0:T(8,128)(2,1)S(1)}, bf16[24,1152]{1,0:T(8,128)(2,1)S(1)}, u32[]{:S(2)}, u32[]{:S(2)}) collective-permute-start(bf16[24,1152]{1,0:T(8,128)(2,1)S(1)} %get-tuple-element.65), channel_id=1, source_target_pairs={{0,384},{16,400},{32,416},{48,432},{64,448},{80,464},{96,480},{112... | collective-permute-start | bytes 165896 | tf_op jit(solution)/shard_map/ppermute | solution.py:313
  24.0 9.4 %collective-permute-start.3 = (bf16[104,1152]{1,0:T(8,128)(2,1)S(1)}, bf16[104,1152]{1,0:T(8,128)(2,1)S(1)}, u32[]{:S(2)}, u32[]{:S(2)}) collective-permute-start(bf16[104,1152]{1,0:T(8,128)(2,1)S(1)} %shard_map.65), channel_id=1, source_target_pairs={{0,64},{16,80},{32,96},{48,112},{64,0},{80,16},{96,32},{112,48},{1... | collective-permute-start | bytes 718856 | tf_op jit(solution)/shard_map/ppermute | solution.py:344
  27.9 2.2 %copy-start = (bf16[144,14336]{1,0:T(8,128)(2,1)S(1)}, bf16[144,14336]{1,0:T(8,128)(2,1)}, u32[]{:S(2)}) copy-start(bf16[144,14336]{1,0:T(8,128)(2,1)} %rows_ref.1) | copy-start | bytes 12386308
  32.1 16.0 %copy-start.11 = (bf16[64,448]{1,0:T(8,128)(2,1)S(1)}, bf16[64,448]{1,0:T(8,128)(2,1)}, u32[]{:S(2)}) copy-start(bf16[64,448]{1,0:T(8,128)(2,1)} %refs_4_.1) | copy-start | bytes 172036
  33.4 49.5 %all-to-all-start = ((bf16[8,144,896]{2,1,0:T(8,128)(2,1)}), bf16[8,144,896]{2,1,0:T(8,128)(2,1)}, u32[]{:S(2)}, u32[]{:S(2)}) async-start(bf16[8,144,896]{2,1,0:T(8,128)(2,1)} %shard_map.66), calls=%async_computation | async-start | bytes 4128768 | tf_op jit(solution)/shard_map/all_to_all | solution.py:335
  39.4 37.2 %collective-permute-start.4 = (bf16[2,104,1152]{2,1,0:T(8,128)(2,1)S(1)}, bf16[2,104,1152]{2,1,0:T(8,128)(2,1)S(1)}, u32[]{:S(2)}, u32[]{:S(2)}) collective-permute-start(bf16[2,104,1152]{2,1,0:T(8,128)(2,1)S(1)} %pad_maximum_fusion.refs_0_), channel_id=1, source_target_pairs={{0,16},{16,32},{32,48},{48,0},{64,80},{80,96},{96,112},{112,64},{1... | collective-permute-start | bytes 1437704 | tf_op jit(solution)/shard_map/ppermute | solution.py:321
  41.3 35.3 %collective-permute-start.5 = (bf16[2,104,1152]{2,1,0:T(8,128)(2,1)S(1)}, bf16[2,104,1152]{2,1,0:T(8,128)(2,1)S(1)}, u32[]{:S(2)}, u32[]{:S(2)}) collective-permute-start(bf16[2,104,1152]{2,1,0:T(8,128)(2,1)S(1)} %pad_maximum_fusion.refs_0_), channel_id=1, source_target_pairs={{0,32},{16,48},{32,0},{48,16},{64,96},{80,112},{96,64},{112,80},{1... | collective-permute-start | bytes 1437704 | tf_op jit(solution)/shard_map/ppermute | solution.py:321
  46.2 35.2 %collective-permute-start.6 = (bf16[2,104,1152]{2,1,0:T(8,128)(2,1)S(1)}, bf16[2,104,1152]{2,1,0:T(8,128)(2,1)S(1)}, u32[]{:S(2)}, u32[]{:S(2)}) collective-permute-start(bf16[2,104,1152]{2,1,0:T(8,128)(2,1)S(1)} %pad_maximum_fusion.refs_0_), channel_id=1, source_target_pairs={{0,48},{16,0},{32,16},{48,32},{64,112},{80,64},{96,80},{112,96},{1... | collective-permute-start | bytes 1437704 | tf_op jit(solution)/shard_map/ppermute | solution.py:321
  48.1 14.2 %collective-permute-start.7 = (bf16[64,448]{1,0:T(8,128)(2,1)S(1)}, bf16[64,448]{1,0:T(8,128)(2,1)S(1)}, u32[]{:S(2)}, u32[]{:S(2)}) collective-permute-start(bf16[64,448]{1,0:T(8,128)(2,1)S(1)} %copy-done.11), channel_id=1, source_target_pairs={{0,128},{16,144},{32,160},{48,176},{64,192},{80,208},{96,224},{112... | collective-permute-start | bytes 172040 | tf_op jit(solution)/shard_map/ppermute | solution.py:313
  50.6 26.0 %collective-permute-start.8 = (bf16[64,448]{1,0:T(8,128)(2,1)S(1)}, bf16[64,448]{1,0:T(8,128)(2,1)S(1)}, u32[]{:S(2)}, u32[]{:S(2)}) collective-permute-start(bf16[64,448]{1,0:T(8,128)(2,1)S(1)} %copy-done.11), channel_id=1, source_target_pairs={{0,256},{16,272},{32,288},{48,304},{64,320},{80,336},{96,352},{112... | collective-permute-start | bytes 172040 | tf_op jit(solution)/shard_map/ppermute | solution.py:313
  62.3 14.3 %collective-permute-start.9 = (bf16[64,448]{1,0:T(8,128)(2,1)S(1)}, bf16[64,448]{1,0:T(8,128)(2,1)S(1)}, u32[]{:S(2)}, u32[]{:S(2)}) collective-permute-start(bf16[64,448]{1,0:T(8,128)(2,1)S(1)} %copy-done.11), channel_id=1, source_target_pairs={{0,384},{16,400},{32,416},{48,432},{64,448},{80,464},{96,480},{112... | collective-permute-start | bytes 172040 | tf_op jit(solution)/shard_map/ppermute | solution.py:313
  72.4 2.2 %copy-start.1 = (bf16[144,14336]{1,0:T(8,128)(2,1)S(1)}, bf16[144,14336]{1,0:T(8,128)(2,1)}, u32[]{:S(2)}) copy-start(bf16[144,14336]{1,0:T(8,128)(2,1)} %rows_ref.1) | copy-start | bytes 12386308
  76.6 6.4 %copy-start.13 = (s32[32]{0:T(128)S(1)}, s32[32]{0:T(128)}, u32[]{:S(2)}) copy-start(s32[32]{0:T(128)} %counts_ref.5) | copy-start | bytes 388
  82.9 1.5 copy-start.4
  90.8 56.5 %all-to-all-start.1 = ((bf16[8,144,896]{2,1,0:T(8,128)(2,1)}), bf16[8,144,896]{2,1,0:T(8,128)(2,1)}, u32[]{:S(2)}, u32[]{:S(2)}) async-start(bf16[8,144,896]{2,1,0:T(8,128)(2,1)} %copy-done.2), calls=%async_computation.1 | async-start | bytes 4128768 | tf_op jit(solution)/shard_map/all_to_all | solution.py:335
  98.4 32.4 %collective-permute-start.10 = (bf16[768,256]{1,0:T(8,128)(2,1)}, bf16[768,256]{1,0:T(8,128)(2,1)S(1)}, u32[]{:S(2)}, u32[]{:S(2)}) collective-permute-start(bf16[768,256]{1,0:T(8,128)(2,1)} %copy-done.14), channel_id=1, source_target_pairs={{0,128},{16,144},{32,160},{48,176},{64,192},{80,208},{96,224},{112... | collective-permute-start | bytes 1179656 | tf_op jit(solution)/shard_map/ppermute | solution.py:325
  100.3 30.4 %collective-permute-start.11 = (bf16[768,256]{1,0:T(8,128)(2,1)}, bf16[768,256]{1,0:T(8,128)(2,1)S(1)}, u32[]{:S(2)}, u32[]{:S(2)}) collective-permute-start(bf16[768,256]{1,0:T(8,128)(2,1)} %copy-done.14), channel_id=1, source_target_pairs={{384,256},{400,272},{416,288},{432,304},{448,320},{464,336},{480,3... | collective-permute-start | bytes 1179656 | tf_op jit(solution)/shard_map/ppermute | solution.py:325
  101.0 36.3 %collective-permute-start.16 = (bf16[400,384]{1,0:T(8,128)(2,1)}, bf16[400,384]{1,0:T(8,128)(2,1)S(1)}, u32[]{:S(2)}, u32[]{:S(2)}) collective-permute-start(bf16[400,384]{1,0:T(8,128)(2,1)} %copy-done.15), channel_id=1, source_target_pairs={{0,128},{16,144},{32,160},{48,176},{64,192},{80,208},{96,224},{112... | collective-permute-start | bytes 921608 | tf_op jit(solution)/shard_map/ppermute | solution.py:325
  102.4 35.0 %collective-permute-start.17 = (bf16[400,384]{1,0:T(8,128)(2,1)}, bf16[400,384]{1,0:T(8,128)(2,1)S(1)}, u32[]{:S(2)}, u32[]{:S(2)}) collective-permute-start(bf16[400,384]{1,0:T(8,128)(2,1)} %copy-done.15), channel_id=1, source_target_pairs={{384,256},{400,272},{416,288},{432,304},{448,320},{464,336},{480,3... | collective-permute-start | bytes 921608 | tf_op jit(solution)/shard_map/ppermute | solution.py:325
  130.9 14.9 %collective-permute-start.12 = (bf16[768,256]{1,0:T(8,128)(2,1)S(1)}, bf16[768,256]{1,0:T(8,128)(2,1)S(1)}, u32[]{:S(2)}, u32[]{:S(2)}) collective-permute-start(bf16[768,256]{1,0:T(8,128)(2,1)S(1)} %get-tuple-element.49), channel_id=1, source_target_pairs={{0,128},{16,144},{32,160},{48,176},{64,192},{80,208},{96,224},{112... | collective-permute-start | bytes 1179656 | tf_op jit(solution)/shard_map/ppermute | solution.py:325
  136.2 10.4 %collective-permute-start.13 = (bf16[768,256]{1,0:T(8,128)(2,1)S(1)}, bf16[768,256]{1,0:T(8,128)(2,1)S(1)}, u32[]{:S(2)}, u32[]{:S(2)}) collective-permute-start(bf16[768,256]{1,0:T(8,128)(2,1)S(1)} %get-tuple-element.50), channel_id=1, source_target_pairs={{256,128},{272,144},{288,160},{304,176},{320,192},{336,208},{352,2... | collective-permute-start | bytes 1179656 | tf_op jit(solution)/shard_map/ppermute | solution.py:325
  138.5 34.5 %collective-permute-start.18 = (bf16[400,384]{1,0:T(8,128)(2,1)}, bf16[400,384]{1,0:T(8,128)(2,1)}, u32[]{:S(2)}, u32[]{:S(2)}) collective-permute-start(bf16[400,384]{1,0:T(8,128)(2,1)} %get-tuple-element.61), channel_id=1, source_target_pairs={{0,128},{16,144},{32,160},{48,176},{64,192},{80,208},{96,224},{112... | collective-permute-start | bytes 921608 | tf_op jit(solution)/shard_map/ppermute | solution.py:325
  144.4 28.6 %collective-permute-start.19 = (bf16[400,384]{1,0:T(8,128)(2,1)}, bf16[400,384]{1,0:T(8,128)(2,1)}, u32[]{:S(2)}, u32[]{:S(2)}) collective-permute-start(bf16[400,384]{1,0:T(8,128)(2,1)} %get-tuple-element.62), channel_id=1, source_target_pairs={{256,128},{272,144},{288,160},{304,176},{320,192},{336,208},{352,2... | collective-permute-start | bytes 921608 | tf_op jit(solution)/shard_map/ppermute | solution.py:325
  148.8 5.0 %copy-start.7 = (bf16[768,256]{1,0:T(8,128)(2,1)S(1)}, bf16[768,256]{1,0:T(8,128)(2,1)}, u32[]{:S(2)}) copy-start(bf16[768,256]{1,0:T(8,128)(2,1)} %copy-done.6) | copy-start | bytes 1179652
  148.8 5.1 %copy-start.9 = (bf16[768,256]{1,0:T(8,128)(2,1)S(1)}, bf16[768,256]{1,0:T(8,128)(2,1)}, u32[]{:S(2)}) copy-start(bf16[768,256]{1,0:T(8,128)(2,1)} %copy-done.8) | copy-start | bytes 1179652
  154.1 27.1 %copy-start.16 = (bf16[448]{0:T(512)(128)(2,1)S(1)}, bf16[448]{0:T(512)(128)(2,1)}, u32[]{:S(2)}) copy-start(bf16[448]{0:T(512)(128)(2,1)} %param.10) | copy-start | bytes 2692
  154.2 44.0 %collective-permute-start.14 = (bf16[768,256]{1,0:T(8,128)(2,1)S(1)}, bf16[768,256]{1,0:T(8,128)(2,1)S(1)}, u32[]{:S(2)}, u32[]{:S(2)}) collective-permute-start(bf16[768,256]{1,0:T(8,128)(2,1)S(1)} %get-tuple-element.56), channel_id=1, source_target_pairs={{0,128},{16,144},{32,160},{48,176},{64,192},{80,208},{96,224},{112... | collective-permute-start | bytes 1179656 | tf_op jit(solution)/shard_map/ppermute | solution.py:325
  171.7 26.5 %collective-permute-start.15 = (bf16[768,256]{1,0:T(8,128)(2,1)S(1)}, bf16[768,256]{1,0:T(8,128)(2,1)S(1)}, u32[]{:S(2)}, u32[]{:S(2)}) collective-permute-start(bf16[768,256]{1,0:T(8,128)(2,1)S(1)} %get-tuple-element.57), channel_id=1, source_target_pairs={{128,0},{144,16},{160,32},{176,48},{192,64},{208,80},{224,96},{240... | collective-permute-start | bytes 1179656 | tf_op jit(solution)/shard_map/ppermute | solution.py:325
  174.4 9.9 %collective-permute-start.20 = (bf16[400,384]{1,0:T(8,128)(2,1)S(1)}, bf16[400,384]{1,0:T(8,128)(2,1)S(1)}, u32[]{:S(2)}, u32[]{:S(2)}) collective-permute-start(bf16[400,384]{1,0:T(8,128)(2,1)S(1)} %get-tuple-element.63), channel_id=1, source_target_pairs={{0,128},{16,144},{32,160},{48,176},{64,192},{80,208},{96,224},{112... | collective-permute-start | bytes 921608 | tf_op jit(solution)/shard_map/ppermute | solution.py:325
  179.9 18.2 %collective-permute-start.21 = (bf16[400,384]{1,0:T(8,128)(2,1)S(1)}, bf16[400,384]{1,0:T(8,128)(2,1)S(1)}, u32[]{:S(2)}, u32[]{:S(2)}) collective-permute-start(bf16[400,384]{1,0:T(8,128)(2,1)S(1)} %get-tuple-element.64), channel_id=1, source_target_pairs={{128,0},{144,16},{160,32},{176,48},{192,64},{208,80},{224,96},{240... | collective-permute-start | bytes 921608 | tf_op jit(solution)/shard_map/ppermute | solution.py:325
  (9 other events, 8.6 us)

commit v5 on v4

--- a/solution.py
+++ b/solution.py
@@ -350,13 +350,14 @@
     sends += pack(place, frozen_slot_rows, PARTS[1:])
     blocks = jnp.stack([column, other])
     blocks = [blocks] + [along_x(blocks, step) for step in range(1, 4)]
-    all_tokens, down, up = assemble(place, blocks, ups)
+    sends[1], rows, up1, up2, up3, *blocks = lax.optimization_barrier((sends[1], rows, *ups[1:], *blocks))
+    all_tokens, down, up = assemble(place, blocks, [ups[0], up1, up2, up3])
+    last_rows = exchange(sends[1])
     early_squares, early_front, early_back, first_front, first_back = partial_products(
         0, place, counts, rows, all_tokens, down, up
     )
-    sends[1], early_front = lax.optimization_barrier((sends[1], early_front))
     a, b = hops((first_front, first_front), 1), hops((first_back, first_back), 1)
-    rows = exchange(sends[1])
+    rows = last_rows
     a = hops(forward(2, place, a, early_front, early_front, early_squares, early_squares), 2)
     b = hops(forward(2, place, b, early_back, early_back, early_squares, early_squares), 2)
     rows, *a = lax.optimization_barrier((rows, *a))

time: 201 us -> 199 us (0.990)
  the two profiles are of different devices: /device:TPU:30 before, /device:TPU:1 now
where the time goes in v5:
time: 199 us; the launch traced here: 196 us
  starting transfers between devices  106 us (53%)
  waiting for transfers between devices  58.7 us (29%)
  Pallas kernels  19.1 us (10%)
  local copies, waits for them, and re-layouts  11.3 us (6%)
    ppermute x12, starting transfers between devices, hop(): lax.ppermute(array, AXIS, [(GROUP * p + i, GROUP * (p + way) + i) for p i...  45.1 us
    ppermute x12, waiting for transfers between devices, hop(): lax.ppermute(array, AXIS, [(GROUP * p + i, GROUP * (p + way) + i) for p i...  43.6 us
    ppermute x6, starting transfers between devices, to_pair(): lax.ppermute(array, AXIS, [(GROUP * p + i, GROUP * ((p + step) % PAIRS) +...  34.6 us
    all_to_all x2, starting transfers between devices, exchange(): return lax.all_to_all(send, AXIS, 0, 0, axis_index_groups=NEAR, tiled=True)  12.1 us
    ppermute x3, waiting for transfers between devices, along_x(): lax.ppermute(array, AXIS, [(4 * z + x, 4 * z + (x + step) % 4) for z in r...  11.2 us
    ppermute x3, starting transfers between devices, along_x(): lax.ppermute(array, AXIS, [(4 * z + x, 4 * z + (x + step) % 4) for z in r...  10.8 us
    pallas_call x2, Pallas kernels, partial_products(): pl.pallas_call(functools.partial(partial_kernel, stage), out_shape=out_sh...  10.2 us
    unnamed x27, local copies, waits for them, and re-layouts  10.1 us
  transfers between devices with their start and end apart: 24, of which 10 were waited for; matrix products, arithmetic and copies ran while one was open for 0% of the time, Pallas kernels for 9%

profile of v5, /device:TPU:1, one launch (start us, length us, event | category | flops | bytes accessed | tf_op | source)
XLA Modules:
  0.0 195.7 jit_solution(3647711245196560242)
XLA Ops:
  2.6 5.7 %collective-permute-start = (bf16[24,1152]{1,0:T(8,128)(2,1)S(1)}, bf16[24,1152]{1,0:T(8,128)(2,1)S(1)}, u32[]{:S(2)}, u32[]{:S(2)}) collective-permute-start(bf16[24,1152]{1,0:T(8,128)(2,1)S(1)} %get-tuple-element.81), channel_id=1, source_target_pairs={{0,128},{16,144},{32,160},{48,176},{64,192},{80,208},{96,224},{112... | collective-permute-start | bytes 165896 | tf_op jit(solution)/shard_map/ppermute | solution.py:313
  8.3 8.8 %collective-permute-start.1 = (bf16[24,1152]{1,0:T(8,128)(2,1)S(1)}, bf16[24,1152]{1,0:T(8,128)(2,1)S(1)}, u32[]{:S(2)}, u32[]{:S(2)}) collective-permute-start(bf16[24,1152]{1,0:T(8,128)(2,1)S(1)} %get-tuple-element.80), channel_id=1, source_target_pairs={{0,256},{16,272},{32,288},{48,304},{64,320},{80,336},{96,352},{112... | collective-permute-start | bytes 165896 | tf_op jit(solution)/shard_map/ppermute | solution.py:313
  17.1 4.3 %collective-permute-start.2 = (bf16[24,1152]{1,0:T(8,128)(2,1)S(1)}, bf16[24,1152]{1,0:T(8,128)(2,1)S(1)}, u32[]{:S(2)}, u32[]{:S(2)}) collective-permute-start(bf16[24,1152]{1,0:T(8,128)(2,1)S(1)} %get-tuple-element.79), channel_id=1, source_target_pairs={{0,384},{16,400},{32,416},{48,432},{64,448},{80,464},{96,480},{112... | collective-permute-start | bytes 165896 | tf_op jit(solution)/shard_map/ppermute | solution.py:313
  23.8 3.8 %collective-permute-start.3 = (bf16[104,1152]{1,0:T(8,128)(2,1)S(1)}, bf16[104,1152]{1,0:T(8,128)(2,1)S(1)}, u32[]{:S(2)}, u32[]{:S(2)}) collective-permute-start(bf16[104,1152]{1,0:T(8,128)(2,1)S(1)} %shard_map.65), channel_id=1, source_target_pairs={{0,64},{16,80},{32,96},{48,112},{64,0},{80,16},{96,32},{112,48},{1... | collective-permute-start | bytes 718856 | tf_op jit(solution)/shard_map/ppermute | solution.py:344
  27.5 2.2 %copy-done = bf16[144,14336]{1,0:T(8,128)(2,1)S(1)} copy-done((bf16[144,14336]{1,0:T(8,128)(2,1)S(1)}, bf16[144,14336]{1,0:T(8,128)(2,1)}, u32[]{:S(2)}) %copy-start) | copy-done | bytes 4128792
  29.7 2.0 %shard_map.66 = bf16[8,144,896]{2,1,0:T(8,128)(2,1)} custom-call(s32[1]{0:T(128)} %bitcast.place_ref, bf16[144,14336]{1,0:T(8,128)(2,1)S(1)} %copy-done), custom_call_target="tpu_custom_call" | custom-call | tf_op jit(solution)/shard_map/pallas_call | solution.py:124
  31.7 6.5 %all-to-all-start = ((bf16[8,144,896]{2,1,0:T(8,128)(2,1)}), bf16[8,144,896]{2,1,0:T(8,128)(2,1)}, u32[]{:S(2)}, u32[]{:S(2)}) async-start(bf16[8,144,896]{2,1,0:T(8,128)(2,1)} %shard_map.66), calls=%async_computation | async-start | bytes 4128768 | tf_op jit(solution)/shard_map/all_to_all | solution.py:335
  38.2 3.4 %collective-permute-start.7 = (bf16[2,104,1152]{2,1,0:T(8,128)(2,1)S(1)}, bf16[2,104,1152]{2,1,0:T(8,128)(2,1)S(1)}, u32[]{:S(2)}, u32[]{:S(2)}) collective-permute-start(bf16[2,104,1152]{2,1,0:T(8,128)(2,1)S(1)} %pad_maximum_fusion.refs_0_), channel_id=1, source_target_pairs={{0,16},{16,32},{32,48},{48,0},{64,80},{80,96},{96,112},{112,64},{1... | collective-permute-start | bytes 1437704 | tf_op jit(solution)/shard_map/ppermute | solution.py:321
  41.6 4.3 %collective-permute-start.8 = (bf16[2,104,1152]{2,1,0:T(8,128)(2,1)S(1)}, bf16[2,104,1152]{2,1,0:T(8,128)(2,1)S(1)}, u32[]{:S(2)}, u32[]{:S(2)}) collective-permute-start(bf16[2,104,1152]{2,1,0:T(8,128)(2,1)S(1)} %pad_maximum_fusion.refs_0_), channel_id=1, source_target_pairs={{0,32},{16,48},{32,0},{48,16},{64,96},{80,112},{96,64},{112,80},{1... | collective-permute-start | bytes 1437704 | tf_op jit(solution)/shard_map/ppermute | solution.py:321
  45.9 3.1 %collective-permute-start.9 = (bf16[2,104,1152]{2,1,0:T(8,128)(2,1)S(1)}, bf16[2,104,1152]{2,1,0:T(8,128)(2,1)S(1)}, u32[]{:S(2)}, u32[]{:S(2)}) collective-permute-start(bf16[2,104,1152]{2,1,0:T(8,128)(2,1)S(1)} %pad_maximum_fusion.refs_0_), channel_id=1, source_target_pairs={{0,48},{16,0},{32,16},{48,32},{64,112},{80,64},{96,80},{112,96},{1... | collective-permute-start | bytes 1437704 | tf_op jit(solution)/shard_map/ppermute | solution.py:321
  49.0 1.9 collective-permute-start.4
  51.0 6.6 %collective-permute-start.5 = (bf16[64,448]{1,0:T(8,128)(2,1)S(1)}, bf16[64,448]{1,0:T(8,128)(2,1)S(1)}, u32[]{:S(2)}, u32[]{:S(2)}) collective-permute-start(bf16[64,448]{1,0:T(8,128)(2,1)S(1)} %copy-done.9), channel_id=1, source_target_pairs={{0,256},{16,272},{32,288},{48,304},{64,320},{80,336},{96,352},{112... | collective-permute-start | bytes 172040 | tf_op jit(solution)/shard_map/ppermute | solution.py:313
  57.6 2.5 %collective-permute-done.4.refs_5_ = bf16[64,448]{1,0:T(8,128)(2,1)S(1)} collective-permute-done((bf16[64,448]{1,0:T(8,128)(2,1)S(1)}, bf16[64,448]{1,0:T(8,128)(2,1)S(1)}, u32[]{:S(2)}, u32[]{:S(2)}) %collective-permute-start.4) | collective-permute-done | bytes 57376 | tf_op jit(solution)/shard_map/ppermute | solution.py:313
  60.1 7.2 %collective-permute-start.6 = (bf16[64,448]{1,0:T(8,128)(2,1)S(1)}, bf16[64,448]{1,0:T(8,128)(2,1)S(1)}, u32[]{:S(2)}, u32[]{:S(2)}) collective-permute-start(bf16[64,448]{1,0:T(8,128)(2,1)S(1)} %copy-done.9), channel_id=1, source_target_pairs={{0,384},{16,400},{32,416},{48,432},{64,448},{80,464},{96,480},{112... | collective-permute-start | bytes 172040 | tf_op jit(solution)/shard_map/ppermute | solution.py:313
  67.4 2.2 %copy-done.1 = bf16[144,14336]{1,0:T(8,128)(2,1)S(1)} copy-done((bf16[144,14336]{1,0:T(8,128)(2,1)S(1)}, bf16[144,14336]{1,0:T(8,128)(2,1)}, u32[]{:S(2)}) %copy-start.1) | copy-done | bytes 4128792
  69.5 2.0 %shard_map.67 = bf16[8,144,896]{2,1,0:T(8,128)(2,1)} custom-call(s32[1]{0:T(128)} %bitcast.place_ref, bf16[144,14336]{1,0:T(8,128)(2,1)S(1)} %copy-done.1), custom_call_target="tpu_custom_call" | custom-call | tf_op jit(solution)/shard_map/pallas_call | solution.py:124
  71.5 4.6 %collective-permute-done.7.refs_1_ = bf16[2,104,1152]{2,1,0:T(8,128)(2,1)S(1)} collective-permute-done((bf16[2,104,1152]{2,1,0:T(8,128)(2,1)S(1)}, bf16[2,104,1152]{2,1,0:T(8,128)(2,1)S(1)}, u32[]{:S(2)}, u32[]{:S(2)}) %collective-permute-start.7) | collective-permute-done | bytes 479264 | tf_op jit(solution)/shard_map/ppermute | solution.py:321
  76.1 6.5 %collective-permute-done.8.refs_2_ = bf16[2,104,1152]{2,1,0:T(8,128)(2,1)S(1)} collective-permute-done((bf16[2,104,1152]{2,1,0:T(8,128)(2,1)S(1)}, bf16[2,104,1152]{2,1,0:T(8,128)(2,1)S(1)}, u32[]{:S(2)}, u32[]{:S(2)}) %collective-permute-start.8) | collective-permute-done | bytes 479264 | tf_op jit(solution)/shard_map/ppermute | solution.py:321
  82.7 5.6 %all-to-all-start.1 = ((bf16[8,144,896]{2,1,0:T(8,128)(2,1)}), bf16[8,144,896]{2,1,0:T(8,128)(2,1)}, u32[]{:S(2)}, u32[]{:S(2)}) async-start(bf16[8,144,896]{2,1,0:T(8,128)(2,1)} %shard_map.67), calls=%async_computation.1 | async-start | bytes 4128768 | tf_op jit(solution)/shard_map/all_to_all | solution.py:335
  88.9 5.2 %shard_map.69 = (f32[2,1,448]{2,1,0:T(1,128)S(1)}, f32[2,768,256]{2,1,0:T(8,128)S(1)}, f32[2,384,384]{2,1,0:T(8,128)S(1)}, bf16[768,256]{1,0:T(8,128)(2,1)S(1)}, bf16[400,384]{1,0:T(8,128)(2,1)S(1)}) custom-call(s32[1]{0:T(128)} %bitcast.place_ref, s32[32]{0:T(128)S(1)} %copy-done.11, bf16[8,144,896]{2,1,0:T(8,128)(2,1)} %all-to-all-done.rows_ref, ...), custom_call_target="tpu_custom_call" | custom-call | tf_op jit(solution)/shard_map/pallas_call | solution.py:224
  94.2 1.7 collective-permute-start.10
  98.5 19.2 %collective-permute-done.10.up_got_ref = bf16[768,256]{1,0:T(8,128)(2,1)S(1)} collective-permute-done((bf16[768,256]{1,0:T(8,128)(2,1)S(1)}, bf16[768,256]{1,0:T(8,128)(2,1)S(1)}, u32[]{:S(2)}, u32[]{:S(2)}) %collective-permute-start.10) | collective-permute-done | bytes 393248 | tf_op jit(solution)/shard_map/ppermute | solution.py:325
  117.9 5.0 %collective-permute-start.12 = (bf16[768,256]{1,0:T(8,128)(2,1)S(1)}, bf16[768,256]{1,0:T(8,128)(2,1)S(1)}, u32[]{:S(2)}, u32[]{:S(2)}) collective-permute-start(bf16[768,256]{1,0:T(8,128)(2,1)S(1)} %get-tuple-element.63), channel_id=1, source_target_pairs={{0,128},{16,144},{32,160},{48,176},{64,192},{80,208},{96,224},{112... | collective-permute-start | bytes 1179656 | tf_op jit(solution)/shard_map/ppermute | solution.py:325
  125.4 5.7 %collective-permute-start.18 = (bf16[400,384]{1,0:T(8,128)(2,1)}, bf16[400,384]{1,0:T(8,128)(2,1)}, u32[]{:S(2)}, u32[]{:S(2)}) collective-permute-start(bf16[400,384]{1,0:T(8,128)(2,1)} %get-tuple-element.75), channel_id=1, source_target_pairs={{0,128},{16,144},{32,160},{48,176},{64,192},{80,208},{96,224},{112... | collective-permute-start | bytes 921608 | tf_op jit(solution)/shard_map/ppermute | solution.py:325
  131.1 1.4 collective-permute-start.19
  134.3 1.5 copy-done.3
  135.7 5.0 %shard_map.71 = (f32[2,1,448]{2,1,0:T(1,128)S(1)}, f32[2,768,256]{2,1,0:T(8,128)S(1)}, f32[2,384,384]{2,1,0:T(8,128)S(1)}) custom-call(s32[1]{0:T(128)} %bitcast.place_ref, s32[32]{0:T(128)S(1)} %copy-done.11, bf16[8,144,896]{2,1,0:T(8,128)(2,1)} %all-to-all-done.1.rows_ref, bf16[768,1152]{1,0:T(8,128)(2,1)S(1)} %copy-done.3, ...), custom_call_target="tpu_custom_call" | custom-call | tf_op jit(solution)/shard_map/pallas_call | solution.py:224
  141.0 7.1 %collective-permute-start.14 = (bf16[768,256]{1,0:T(8,128)(2,1)S(1)}, bf16[768,256]{1,0:T(8,128)(2,1)S(1)}, u32[]{:S(2)}, u32[]{:S(2)}) collective-permute-start(bf16[768,256]{1,0:T(8,128)(2,1)S(1)} %get-tuple-element.70), channel_id=1, source_target_pairs={{0,128},{16,144},{32,160},{48,176},{64,192},{80,208},{96,224},{112... | collective-permute-start | bytes 1179656 | tf_op jit(solution)/shard_map/ppermute | solution.py:325
  149.4 1.5 shard_map.74
  150.9 18.3 %collective-permute-start.20 = (bf16[400,384]{1,0:T(8,128)(2,1)S(1)}, bf16[400,384]{1,0:T(8,128)(2,1)S(1)}, u32[]{:S(2)}, u32[]{:S(2)}) collective-permute-start(bf16[400,384]{1,0:T(8,128)(2,1)S(1)} %get-tuple-element.77), channel_id=1, source_target_pairs={{0,128},{16,144},{32,160},{48,176},{64,192},{80,208},{96,224},{112... | collective-permute-start | bytes 921608 | tf_op jit(solution)/shard_map/ppermute | solution.py:325
  170.5 2.5 %collective-permute-done.20.refs_4_ = bf16[400,384]{1,0:T(8,128)(2,1)S(1)} collective-permute-done((bf16[400,384]{1,0:T(8,128)(2,1)S(1)}, bf16[400,384]{1,0:T(8,128)(2,1)S(1)}, u32[]{:S(2)}, u32[]{:S(2)}) %collective-permute-start.20) | collective-permute-done | bytes 307232 | tf_op jit(solution)/shard_map/ppermute | solution.py:325
  173.0 21.0 %collective-permute-done.21.refs_5_ = bf16[400,384]{1,0:T(8,128)(2,1)S(1)} collective-permute-done((bf16[400,384]{1,0:T(8,128)(2,1)S(1)}, bf16[400,384]{1,0:T(8,128)(2,1)S(1)}, u32[]{:S(2)}, u32[]{:S(2)}) %collective-permute-start.21) | collective-permute-done | bytes 307232 | tf_op jit(solution)/shard_map/ppermute | solution.py:325
  (59 shorter events, 17.2 us)
Async XLA Ops:
  2.6 19.7 %collective-permute-start = (bf16[24,1152]{1,0:T(8,128)(2,1)S(1)}, bf16[24,1152]{1,0:T(8,128)(2,1)S(1)}, u32[]{:S(2)}, u32[]{:S(2)}) collective-permute-start(bf16[24,1152]{1,0:T(8,128)(2,1)S(1)} %get-tuple-element.81), channel_id=1, source_target_pairs={{0,128},{16,144},{32,160},{48,176},{64,192},{80,208},{96,224},{112... | collective-permute-start | bytes 165896 | tf_op jit(solution)/shard_map/ppermute | solution.py:313
  8.3 14.0 %collective-permute-start.1 = (bf16[24,1152]{1,0:T(8,128)(2,1)S(1)}, bf16[24,1152]{1,0:T(8,128)(2,1)S(1)}, u32[]{:S(2)}, u32[]{:S(2)}) collective-permute-start(bf16[24,1152]{1,0:T(8,128)(2,1)S(1)} %get-tuple-element.80), channel_id=1, source_target_pairs={{0,256},{16,272},{32,288},{48,304},{64,320},{80,336},{96,352},{112... | collective-permute-start | bytes 165896 | tf_op jit(solution)/shard_map/ppermute | solution.py:313
  17.1 6.5 %collective-permute-start.2 = (bf16[24,1152]{1,0:T(8,128)(2,1)S(1)}, bf16[24,1152]{1,0:T(8,128)(2,1)S(1)}, u32[]{:S(2)}, u32[]{:S(2)}) collective-permute-start(bf16[24,1152]{1,0:T(8,128)(2,1)S(1)} %get-tuple-element.79), channel_id=1, source_target_pairs={{0,384},{16,400},{32,416},{48,432},{64,448},{80,464},{96,480},{112... | collective-permute-start | bytes 165896 | tf_op jit(solution)/shard_map/ppermute | solution.py:313
  23.8 8.0 %collective-permute-start.3 = (bf16[104,1152]{1,0:T(8,128)(2,1)S(1)}, bf16[104,1152]{1,0:T(8,128)(2,1)S(1)}, u32[]{:S(2)}, u32[]{:S(2)}) collective-permute-start(bf16[104,1152]{1,0:T(8,128)(2,1)S(1)} %shard_map.65), channel_id=1, source_target_pairs={{0,64},{16,80},{32,96},{48,112},{64,0},{80,16},{96,32},{112,48},{1... | collective-permute-start | bytes 718856 | tf_op jit(solution)/shard_map/ppermute | solution.py:344
  27.5 2.2 %copy-start = (bf16[144,14336]{1,0:T(8,128)(2,1)S(1)}, bf16[144,14336]{1,0:T(8,128)(2,1)}, u32[]{:S(2)}) copy-start(bf16[144,14336]{1,0:T(8,128)(2,1)} %rows_ref.1) | copy-start | bytes 12386308
  31.7 17.3 %copy-start.9 = (bf16[64,448]{1,0:T(8,128)(2,1)S(1)}, bf16[64,448]{1,0:T(8,128)(2,1)}, u32[]{:S(2)}) copy-start(bf16[64,448]{1,0:T(8,128)(2,1)} %refs_4_.1) | copy-start | bytes 172036
  31.7 51.0 %all-to-all-start = ((bf16[8,144,896]{2,1,0:T(8,128)(2,1)}), bf16[8,144,896]{2,1,0:T(8,128)(2,1)}, u32[]{:S(2)}, u32[]{:S(2)}) async-start(bf16[8,144,896]{2,1,0:T(8,128)(2,1)} %shard_map.66), calls=%async_computation | async-start | bytes 4128768 | tf_op jit(solution)/shard_map/all_to_all | solution.py:335
  38.2 37.9 %collective-permute-start.7 = (bf16[2,104,1152]{2,1,0:T(8,128)(2,1)S(1)}, bf16[2,104,1152]{2,1,0:T(8,128)(2,1)S(1)}, u32[]{:S(2)}, u32[]{:S(2)}) collective-permute-start(bf16[2,104,1152]{2,1,0:T(8,128)(2,1)S(1)} %pad_maximum_fusion.refs_0_), channel_id=1, source_target_pairs={{0,16},{16,32},{32,48},{48,0},{64,80},{80,96},{96,112},{112,64},{1... | collective-permute-start | bytes 1437704 | tf_op jit(solution)/shard_map/ppermute | solution.py:321
  41.6 41.0 %collective-permute-start.8 = (bf16[2,104,1152]{2,1,0:T(8,128)(2,1)S(1)}, bf16[2,104,1152]{2,1,0:T(8,128)(2,1)S(1)}, u32[]{:S(2)}, u32[]{:S(2)}) collective-permute-start(bf16[2,104,1152]{2,1,0:T(8,128)(2,1)S(1)} %pad_maximum_fusion.refs_0_), channel_id=1, source_target_pairs={{0,32},{16,48},{32,0},{48,16},{64,96},{80,112},{96,64},{112,80},{1... | collective-permute-start | bytes 1437704 | tf_op jit(solution)/shard_map/ppermute | solution.py:321
  45.9 36.8 %collective-permute-start.9 = (bf16[2,104,1152]{2,1,0:T(8,128)(2,1)S(1)}, bf16[2,104,1152]{2,1,0:T(8,128)(2,1)S(1)}, u32[]{:S(2)}, u32[]{:S(2)}) collective-permute-start(bf16[2,104,1152]{2,1,0:T(8,128)(2,1)S(1)} %pad_maximum_fusion.refs_0_), channel_id=1, source_target_pairs={{0,48},{16,0},{32,16},{48,32},{64,112},{80,64},{96,80},{112,96},{1... | collective-permute-start | bytes 1437704 | tf_op jit(solution)/shard_map/ppermute | solution.py:321
  49.0 11.1 %collective-permute-start.4 = (bf16[64,448]{1,0:T(8,128)(2,1)S(1)}, bf16[64,448]{1,0:T(8,128)(2,1)S(1)}, u32[]{:S(2)}, u32[]{:S(2)}) collective-permute-start(bf16[64,448]{1,0:T(8,128)(2,1)S(1)} %copy-done.9), channel_id=1, source_target_pairs={{0,128},{16,144},{32,160},{48,176},{64,192},{80,208},{96,224},{112... | collective-permute-start | bytes 172040 | tf_op jit(solution)/shard_map/ppermute | solution.py:313
  51.0 20.5 %collective-permute-start.5 = (bf16[64,448]{1,0:T(8,128)(2,1)S(1)}, bf16[64,448]{1,0:T(8,128)(2,1)S(1)}, u32[]{:S(2)}, u32[]{:S(2)}) collective-permute-start(bf16[64,448]{1,0:T(8,128)(2,1)S(1)} %copy-done.9), channel_id=1, source_target_pairs={{0,256},{16,272},{32,288},{48,304},{64,320},{80,336},{96,352},{112... | collective-permute-start | bytes 172040 | tf_op jit(solution)/shard_map/ppermute | solution.py:313
  60.1 11.4 %collective-permute-start.6 = (bf16[64,448]{1,0:T(8,128)(2,1)S(1)}, bf16[64,448]{1,0:T(8,128)(2,1)S(1)}, u32[]{:S(2)}, u32[]{:S(2)}) collective-permute-start(bf16[64,448]{1,0:T(8,128)(2,1)S(1)} %copy-done.9), channel_id=1, source_target_pairs={{0,384},{16,400},{32,416},{48,432},{64,448},{80,464},{96,480},{112... | collective-permute-start | bytes 172040 | tf_op jit(solution)/shard_map/ppermute | solution.py:313
  67.3 2.2 %copy-start.1 = (bf16[144,14336]{1,0:T(8,128)(2,1)S(1)}, bf16[144,14336]{1,0:T(8,128)(2,1)}, u32[]{:S(2)}) copy-start(bf16[144,14336]{1,0:T(8,128)(2,1)} %rows_ref.1) | copy-start | bytes 12386308
  82.7 51.6 %all-to-all-start.1 = ((bf16[8,144,896]{2,1,0:T(8,128)(2,1)}), bf16[8,144,896]{2,1,0:T(8,128)(2,1)}, u32[]{:S(2)}, u32[]{:S(2)}) async-start(bf16[8,144,896]{2,1,0:T(8,128)(2,1)} %shard_map.67), calls=%async_computation.1 | async-start | bytes 4128768 | tf_op jit(solution)/shard_map/all_to_all | solution.py:335
  88.6 5.6 %copy-start.2 = (bf16[768,1152]{1,0:T(8,128)(2,1)}, bf16[768,1152]{1,0:T(8,128)(2,1)S(1)}, u32[]{:S(2)}) copy-start(bf16[768,1152]{1,0:T(8,128)(2,1)S(1)} %get-tuple-element.57.tokens_ref) | copy-start | bytes 5308420
  94.2 23.6 %collective-permute-start.10 = (bf16[768,256]{1,0:T(8,128)(2,1)S(1)}, bf16[768,256]{1,0:T(8,128)(2,1)S(1)}, u32[]{:S(2)}, u32[]{:S(2)}) collective-permute-start(bf16[768,256]{1,0:T(8,128)(2,1)S(1)} %get-tuple-element.60), channel_id=1, source_target_pairs={{0,128},{16,144},{32,160},{48,176},{64,192},{80,208},{96,224},{112... | collective-permute-start | bytes 1179656 | tf_op jit(solution)/shard_map/ppermute | solution.py:325
  95.8 21.9 %collective-permute-start.11 = (bf16[768,256]{1,0:T(8,128)(2,1)S(1)}, bf16[768,256]{1,0:T(8,128)(2,1)S(1)}, u32[]{:S(2)}, u32[]{:S(2)}) collective-permute-start(bf16[768,256]{1,0:T(8,128)(2,1)S(1)} %get-tuple-element.60), channel_id=1, source_target_pairs={{384,256},{400,272},{416,288},{432,304},{448,320},{464,336},{480,3... | collective-permute-start | bytes 1179656 | tf_op jit(solution)/shard_map/ppermute | solution.py:325
  96.5 27.8 %collective-permute-start.16 = (bf16[400,384]{1,0:T(8,128)(2,1)S(1)}, bf16[400,384]{1,0:T(8,128)(2,1)S(1)}, u32[]{:S(2)}, u32[]{:S(2)}) collective-permute-start(bf16[400,384]{1,0:T(8,128)(2,1)S(1)} %get-tuple-element.73), channel_id=1, source_target_pairs={{0,128},{16,144},{32,160},{48,176},{64,192},{80,208},{96,224},{112... | collective-permute-start | bytes 921608 | tf_op jit(solution)/shard_map/ppermute | solution.py:325
  97.8 26.5 %collective-permute-start.17 = (bf16[400,384]{1,0:T(8,128)(2,1)S(1)}, bf16[400,384]{1,0:T(8,128)(2,1)S(1)}, u32[]{:S(2)}, u32[]{:S(2)}) collective-permute-start(bf16[400,384]{1,0:T(8,128)(2,1)S(1)} %get-tuple-element.73), channel_id=1, source_target_pairs={{384,256},{400,272},{416,288},{432,304},{448,320},{464,336},{480,3... | collective-permute-start | bytes 921608 | tf_op jit(solution)/shard_map/ppermute | solution.py:325
  117.9 14.8 %collective-permute-start.12 = (bf16[768,256]{1,0:T(8,128)(2,1)S(1)}, bf16[768,256]{1,0:T(8,128)(2,1)S(1)}, u32[]{:S(2)}, u32[]{:S(2)}) collective-permute-start(bf16[768,256]{1,0:T(8,128)(2,1)S(1)} %get-tuple-element.63), channel_id=1, source_target_pairs={{0,128},{16,144},{32,160},{48,176},{64,192},{80,208},{96,224},{112... | collective-permute-start | bytes 1179656 | tf_op jit(solution)/shard_map/ppermute | solution.py:325
  122.9 10.6 %collective-permute-start.13 = (bf16[768,256]{1,0:T(8,128)(2,1)S(1)}, bf16[768,256]{1,0:T(8,128)(2,1)S(1)}, u32[]{:S(2)}, u32[]{:S(2)}) collective-permute-start(bf16[768,256]{1,0:T(8,128)(2,1)S(1)} %get-tuple-element.64), channel_id=1, source_target_pairs={{256,128},{272,144},{288,160},{304,176},{320,192},{336,208},{352,2... | collective-permute-start | bytes 1179656 | tf_op jit(solution)/shard_map/ppermute | solution.py:325
  125.4 24.0 %collective-permute-start.18 = (bf16[400,384]{1,0:T(8,128)(2,1)}, bf16[400,384]{1,0:T(8,128)(2,1)}, u32[]{:S(2)}, u32[]{:S(2)}) collective-permute-start(bf16[400,384]{1,0:T(8,128)(2,1)} %get-tuple-element.75), channel_id=1, source_target_pairs={{0,128},{16,144},{32,160},{48,176},{64,192},{80,208},{96,224},{112... | collective-permute-start | bytes 921608 | tf_op jit(solution)/shard_map/ppermute | solution.py:325
  131.1 18.3 %collective-permute-start.19 = (bf16[400,384]{1,0:T(8,128)(2,1)}, bf16[400,384]{1,0:T(8,128)(2,1)}, u32[]{:S(2)}, u32[]{:S(2)}) collective-permute-start(bf16[400,384]{1,0:T(8,128)(2,1)} %get-tuple-element.76), channel_id=1, source_target_pairs={{256,128},{272,144},{288,160},{304,176},{320,192},{336,208},{352,2... | collective-permute-start | bytes 921608 | tf_op jit(solution)/shard_map/ppermute | solution.py:325
  134.3 1.5 copy-start.3
  135.7 5.0 %copy-start.5 = (bf16[768,256]{1,0:T(8,128)(2,1)S(1)}, bf16[768,256]{1,0:T(8,128)(2,1)}, u32[]{:S(2)}) copy-start(bf16[768,256]{1,0:T(8,128)(2,1)} %copy-done.4) | copy-start | bytes 1179652
  135.7 5.1 %copy-start.7 = (bf16[768,256]{1,0:T(8,128)(2,1)S(1)}, bf16[768,256]{1,0:T(8,128)(2,1)}, u32[]{:S(2)}) copy-start(bf16[768,256]{1,0:T(8,128)(2,1)} %copy-done.6) | copy-start | bytes 1179652
  141.0 29.5 %copy-start.12 = (bf16[448]{0:T(512)(128)(2,1)S(1)}, bf16[448]{0:T(512)(128)(2,1)}, u32[]{:S(2)}) copy-start(bf16[448]{0:T(512)(128)(2,1)} %param.10) | copy-start | bytes 2692
  141.0 53.0 %collective-permute-start.14 = (bf16[768,256]{1,0:T(8,128)(2,1)S(1)}, bf16[768,256]{1,0:T(8,128)(2,1)S(1)}, u32[]{:S(2)}, u32[]{:S(2)}) collective-permute-start(bf16[768,256]{1,0:T(8,128)(2,1)S(1)} %get-tuple-element.70), channel_id=1, source_target_pairs={{0,128},{16,144},{32,160},{48,176},{64,192},{80,208},{96,224},{112... | collective-permute-start | bytes 1179656 | tf_op jit(solution)/shard_map/ppermute | solution.py:325
  148.1 45.9 %collective-permute-start.15 = (bf16[768,256]{1,0:T(8,128)(2,1)S(1)}, bf16[768,256]{1,0:T(8,128)(2,1)S(1)}, u32[]{:S(2)}, u32[]{:S(2)}) collective-permute-start(bf16[768,256]{1,0:T(8,128)(2,1)S(1)} %get-tuple-element.71), channel_id=1, source_target_pairs={{128,0},{144,16},{160,32},{176,48},{192,64},{208,80},{224,96},{240... | collective-permute-start | bytes 1179656 | tf_op jit(solution)/shard_map/ppermute | solution.py:325
  150.9 22.1 %collective-permute-start.20 = (bf16[400,384]{1,0:T(8,128)(2,1)S(1)}, bf16[400,384]{1,0:T(8,128)(2,1)S(1)}, u32[]{:S(2)}, u32[]{:S(2)}) collective-permute-start(bf16[400,384]{1,0:T(8,128)(2,1)S(1)} %get-tuple-element.77), channel_id=1, source_target_pairs={{0,128},{16,144},{32,160},{48,176},{64,192},{80,208},{96,224},{112... | collective-permute-start | bytes 921608 | tf_op jit(solution)/shard_map/ppermute | solution.py:325
  169.2 24.8 %collective-permute-start.21 = (bf16[400,384]{1,0:T(8,128)(2,1)S(1)}, bf16[400,384]{1,0:T(8,128)(2,1)S(1)}, u32[]{:S(2)}, u32[]{:S(2)}) collective-permute-start(bf16[400,384]{1,0:T(8,128)(2,1)S(1)} %get-tuple-element.78), channel_id=1, source_target_pairs={{128,0},{144,16},{160,32},{176,48},{192,64},{208,80},{224,96},{240... | collective-permute-start | bytes 921608 | tf_op jit(solution)/shard_map/ppermute | solution.py:325
  (5 other events, 3.8 us)
